TPU v7x, 128 devices: a whole 4x4x4 slice. The times are simulated.
128 devices in a mesh: dp: 64 (over y_lo, x, z, core), tensor: 2 (over y_hi).
Axes of the slice: x: 4, y: 4 (y_hi: 2, y_lo: 2; y = y_hi * 2 + y_lo), z: 4, core: 2. Of those that a mesh axis runs over, the one named last changes fastest.
Arguments:
- tokens: bfloat16 [16384, 1024], P(('dp', 'tensor')), may hold values from -6 to 6
- routes: int32 [16384, 8], P('dp'), may hold values from 0 to 31, all different within a row; in each aligned block of 256 rows (0 to 255, 256 to 511, ...) at most 80 rows name the same one
- cotangent: bfloat16 [16384, 1024], P(('dp', 'tensor')), may hold values from -6 to 6
- attn_gain: bfloat16 [1024], P('dp'), may hold values from 0.5 to 1.5
- query_weight: bfloat16 [1024, 1024], P('dp', 'tensor'), may hold values from -0.1875 to 0.1875
- key_weight: bfloat16 [1024, 512], P('dp', 'tensor'), may hold values from -0.1875 to 0.1875
- value_weight: bfloat16 [1024, 512], P('dp', 'tensor'), may hold values from -0.1875 to 0.1875
- out_weight: bfloat16 [1024, 1024], P('dp', 'tensor'), may hold values from -0.75 to 0.75
- moe_gain: bfloat16 [1024], P('dp'), may hold values from 0.5 to 1.5
- router_weight: bfloat16 [1024, 32], P('dp'), may hold values from -0.09375 to 0.09375
- expert_gate: bfloat16 [1024, 32, 512], P('dp', None, 'tensor'), may hold values from -0.1875 to 0.1875
- expert_up: bfloat16 [1024, 32, 512], P('dp', None, 'tensor'), may hold values from -0.1875 to 0.1875
- expert_down: bfloat16 [1024, 32, 512], P('dp', None, 'tensor'), may hold values from -1 to 1
Outputs:
- output: bfloat16 [16384, 1024], P(('dp', 'tensor'))
- input_grad: bfloat16 [16384, 1024], P(('dp', 'tensor'))
- attn_gain_grad: float32 [1024], P('dp')
- query_weight_grad: float32 [1024, 1024], P('dp', 'tensor')
- key_weight_grad: float32 [1024, 512], P('dp', 'tensor')
- value_weight_grad: float32 [1024, 512], P('dp', 'tensor')
- out_weight_grad: float32 [1024, 1024], P('dp', 'tensor')
- moe_gain_grad: float32 [1024], P('dp')
- router_weight_grad: float32 [1024, 32], P('dp')
- expert_gate_grad: float32 [1024, 32, 512], P('dp', None, 'tensor')
- expert_up_grad: float32 [1024, 32, 512], P('dp', None, 'tensor')
- expert_down_grad: float32 [1024, 32, 512], P('dp', None, 'tensor')
Inputs may be any that keep to these rules, and one draw needn't show every extreme that they name: `routes`: each row names 8 different experts. Within each sequence (each aligned block of 256 rows) no expert is named by more than 80 rows, and in some sequence one expert is named by exactly 80 rows.
All inputs are finite; a program needn't handle non-finite values.
Results may differ from a plain program's by a relative error of at most 0.018.
Values may be sent and summed in bfloat16 or wider, within the bound.
No kernel may reach another device: no remote copies, remote signals or barrier semaphores. Data moves between devices by JAX's collectives and lax.ppermute only.
A program may use at most 320 MiB of HBM per device.

v0:
```python
import math

import jax
import jax.numpy as jnp
from jax import lax
from jax.sharding import PartitionSpec as P

HDIM = 64


exact_mode = lax.Precision.HIGHEST
norm_eps = 1e-06
rope_base = 10000.0
block_limit = 512
rows_contract = (((1,), (1,)), ((), ()))
tokens_contract = (((0,), (0,)), ((), ()))


def rms_forward(values, gain_vec):
    factor = lax.rsqrt(jnp.mean(values * values, axis=1, keepdims=True) + norm_eps)
    normed = values * factor
    return (normed, factor, (normed * gain_vec.astype(jnp.float32)).astype(jnp.bfloat16))


def rms_backward(grad_in, normed, factor, gain_vec):
    gain_grad = jnp.sum(grad_in * normed, axis=0)
    inner_grad = grad_in * gain_vec.astype(jnp.float32)
    return (
        factor * (inner_grad - normed * jnp.mean(inner_grad * normed, axis=1, keepdims=True)),
        gain_grad,
    )


def rotary_tables(length, head_size):
    half_dim = head_size // 2
    frequency = rope_base ** (-(jnp.arange(half_dim, dtype=jnp.float32) * 2.0 / head_size))
    angles = jnp.arange(length, dtype=jnp.float32)[:, None] * frequency[None, :]
    angles = jnp.concatenate([angles, angles], axis=1)
    return (jnp.cos(angles), jnp.sin(angles))


def rotate(values, cos_tab, sin_tab):
    half_dim = values.shape[-1] // 2
    turned = jnp.concatenate([-values[..., half_dim:], values[..., :half_dim]], axis=-1)
    return values * cos_tab[:, None, :] + turned * sin_tab[:, None, :]


def rotate_back(grad_in, cos_tab, sin_tab):
    half_dim = grad_in.shape[-1] // 2
    scaled = grad_in * sin_tab[:, None, :]
    turned = jnp.concatenate([scaled[..., half_dim:], -scaled[..., :half_dim]], axis=-1)
    return grad_in * cos_tab[:, None, :] + turned


def slot_tables(route_rows, experts, capacity):
    count = route_rows.shape[0] * route_rows.shape[1]
    flat_routes = route_rows.reshape(count)
    onehot = (flat_routes[:, None] == jnp.arange(experts, dtype=jnp.int32)[None, :]).astype(
        jnp.int32
    )
    before = jnp.cumsum(onehot, axis=0) - onehot
    places = jnp.sum(before * onehot, axis=1)
    slot_of = flat_routes * capacity + places
    order = jnp.arange(count, dtype=jnp.int32)
    route_of = jnp.zeros((experts * capacity,), jnp.int32).at[slot_of].set(order)
    filled = jnp.zeros((experts * capacity,), jnp.float32).at[slot_of].set(1.0)
    return (slot_of, route_of, filled)


def block_scores(query_block, keys_all, row_start, scale_value):
    block_rows = query_block.shape[0]
    scores = (
        jnp.einsum("qngd,knd->ngqk", query_block, keys_all, preferred_element_type=jnp.float32)
        * scale_value
    )
    allowed = (row_start + jnp.arange(block_rows, dtype=jnp.int32))[:, None] >= jnp.arange(
        keys_all.shape[0], dtype=jnp.int32
    )[None, :]
    return jnp.where(allowed[None, None], scores, -1e30)


def attend_forward(queries, keys_all, values_all, scale_value):
    seq_len = queries.shape[0]
    block_rows = min(seq_len, block_limit)

    def one_block(block_id):
        row_start = block_id * block_rows
        scores = block_scores(queries, keys_all, row_start, scale_value)
        row_peak = jnp.max(scores, axis=3, keepdims=True)
        log_total = row_peak + jnp.log(jnp.sum(jnp.exp(scores - row_peak), axis=3, keepdims=True))
        attn_probs = jnp.exp(scores - log_total).astype(jnp.bfloat16)
        context = jnp.einsum(
            "ngqk,knd->qngd", attn_probs, values_all, preferred_element_type=jnp.float32
        )
        return (context, log_total[..., 0])

    context, log_total = lax.map(one_block, jnp.arange(seq_len // block_rows, dtype=jnp.int32))
    return (context.reshape(seq_len, -1), log_total)


def attend_backward(queries, keys_all, values_all, log_total, context_grad, scale_value):
    seq_len = queries.shape[0]
    block_rows = min(seq_len, block_limit)

    def one_block(totals, block_id):
        row_start = block_id * block_rows
        scores = block_scores(queries, keys_all, row_start, scale_value)
        probs_full = jnp.exp(scores - log_total[block_id][..., None])
        prob_back = jnp.einsum(
            "qngd,knd->ngqk", context_grad, values_all, preferred_element_type=jnp.float32
        )
        value_grad = jnp.einsum(
            "ngqk,qngd->knd",
            probs_full.astype(jnp.bfloat16),
            context_grad,
            preferred_element_type=jnp.float32,
        )
        spread = jnp.sum(probs_full * prob_back, axis=3, keepdims=True)
        score_grad = (probs_full * (prob_back - spread)).astype(jnp.bfloat16)
        query_grad = (
            jnp.einsum("ngqk,knd->qngd", score_grad, keys_all, preferred_element_type=jnp.float32)
            * scale_value
        )
        key_grad = (
            jnp.einsum("ngqk,qngd->knd", score_grad, queries, preferred_element_type=jnp.float32)
            * scale_value
        )
        return ((totals[0] + key_grad, totals[1] + value_grad), query_grad)

    zeros_keys = jnp.zeros(keys_all.shape, jnp.float32)
    totals, query_grad = lax.scan(
        one_block, (zeros_keys, zeros_keys), jnp.arange(seq_len // block_rows, dtype=jnp.int32)
    )
    return (query_grad.reshape(queries.shape), totals[0], totals[1])


def swiglu_back(hidden_grad, gate_pre, up_pre):
    sigmoid_vals = jax.nn.sigmoid(gate_pre)
    gate_grad = (
        hidden_grad * up_pre * sigmoid_vals * (1.0 + gate_pre * (1.0 - sigmoid_vals))
    ).astype(jnp.bfloat16)
    up_grad = (hidden_grad * gate_pre * sigmoid_vals).astype(jnp.bfloat16)
    return (gate_grad, up_grad)


def body(
    tokens,
    routes,
    cotangent,
    attn_gain,
    query_weight,
    key_weight,
    value_weight,
    out_weight,
    moe_gain,
    router_weight,
    expert_gate,
    expert_up,
    expert_down,
):
    local_rows = tokens.shape[0]
    width_model = tokens.shape[1]
    seq_len = local_rows * lax.axis_size("tensor")
    own_start = lax.axis_index("tensor") * local_rows
    experts = router_weight.shape[1]
    route_count = routes.shape[1]
    capacity = (5 * route_count * seq_len // (4 * experts) + 7) // 8 * 8
    heads_here = query_weight.shape[1] // HDIM
    kv_here = key_weight.shape[1] // HDIM
    group = heads_here // kv_here
    scale_value = 1.0 / math.sqrt(HDIM)
    cos_tab, sin_tab = rotary_tables(seq_len, HDIM)
    gain_one, gain_two, full_query, full_key, full_value, full_out = (
        lax.all_gather(attn_gain, "dp", axis=0, tiled=True),
        lax.all_gather(moe_gain, "dp", axis=0, tiled=True),
        lax.all_gather(query_weight, "dp", axis=0, tiled=True),
        lax.all_gather(key_weight, "dp", axis=0, tiled=True),
        lax.all_gather(value_weight, "dp", axis=0, tiled=True),
        lax.all_gather(out_weight, "dp", axis=0, tiled=True),
    )
    all_rows = lax.all_gather(tokens, "tensor", axis=0, tiled=True).astype(jnp.float32)
    normed_one, factor_one, attn_in = rms_forward(all_rows, gain_one)
    query_lin = jnp.dot(attn_in, full_query, preferred_element_type=jnp.float32)
    key_lin = jnp.dot(attn_in, full_key, preferred_element_type=jnp.float32)
    value_rows = (
        jnp.dot(attn_in, full_value, preferred_element_type=jnp.float32)
        .astype(jnp.bfloat16)
        .reshape(seq_len, kv_here, HDIM)
    )
    queries = (
        rotate(query_lin.reshape(seq_len, heads_here, HDIM), cos_tab, sin_tab)
        .astype(jnp.bfloat16)
        .reshape(seq_len, kv_here, group, HDIM)
    )
    keys_rot = rotate(key_lin.reshape(seq_len, kv_here, HDIM), cos_tab, sin_tab).astype(
        jnp.bfloat16
    )
    context, log_total = attend_forward(queries, keys_rot, value_rows, scale_value)
    context_low = context.astype(jnp.bfloat16)
    attn_part = lax.dot_general(
        context_low, full_out, rows_contract, preferred_element_type=jnp.float32
    )
    middle = all_rows + lax.psum(attn_part, "tensor")
    normed_two, factor_two, moe_in = rms_forward(middle, gain_two)
    slot_of, route_of, filled = slot_tables(routes, experts, capacity)
    token_of = route_of // route_count
    dispatched = (moe_in[token_of] * filled[:, None].astype(jnp.bfloat16)).reshape(
        experts, capacity, width_model
    )
    pieces = (
        lax.all_gather(expert_gate, "dp", axis=0, tiled=True),
        lax.all_gather(expert_up, "dp", axis=0, tiled=True),
        lax.all_gather(router_weight, "dp", axis=0, tiled=True),
    )
    gate_sums = (
        jnp.einsum("ecr,ref->ecf", dispatched, pieces[0], preferred_element_type=jnp.float32),
        jnp.einsum("ecr,ref->ecf", dispatched, pieces[1], preferred_element_type=jnp.float32),
        jnp.dot(moe_in, pieces[2], preferred_element_type=jnp.float32),
    )
    gate_e, up_e, logits = gate_sums
    hidden_e = (jax.nn.silu(gate_e) * up_e).astype(jnp.bfloat16)
    picked = (routes[:, :, None] == jnp.arange(experts, dtype=jnp.int32)[None, None, :]).astype(
        jnp.float32
    )
    chosen = jnp.sum(picked * logits[:, None, :], axis=2)
    route_gates = jax.nn.softmax(chosen, axis=1)
    pieces = (lax.all_gather(expert_down, "dp", axis=0, tiled=True),)
    span_rows = pieces[0].shape[0]
    routed_cols = jnp.einsum(
        "ecf,ref->ecr", hidden_e, pieces[0], preferred_element_type=jnp.float32
    ).reshape(experts * capacity, span_rows)
    slot_out = routed_cols
    routed_rows = slot_out[slot_of].reshape(seq_len, route_count, width_model)
    moe_part = jnp.sum(route_gates[:, :, None] * routed_rows, axis=1)
    final_rows = middle + lax.psum(moe_part.astype(jnp.bfloat16), "tensor").astype(jnp.float32)
    output = lax.dynamic_slice_in_dim(final_rows, own_start, local_rows, 0).astype(jnp.bfloat16)
    grad_full = lax.all_gather(cotangent, "tensor", axis=0, tiled=True).astype(jnp.float32)
    route_dots = jnp.sum(routed_rows * grad_full[:, None, :], axis=2)
    chosen_grad = route_gates * (
        route_dots - jnp.sum(route_gates * route_dots, axis=1, keepdims=True)
    )
    logit_grad = jnp.sum(picked * chosen_grad[:, :, None], axis=1)
    moe_in_wide = moe_in.astype(jnp.float32)
    router_part = lax.dot_general(moe_in_wide, logit_grad, tokens_contract, precision=exact_mode)
    gate_of = route_gates.reshape(-1)[route_of] * filled
    slot_grad = (
        (grad_full[token_of] * gate_of[:, None])
        .astype(jnp.bfloat16)
        .reshape(experts, capacity, width_model)
    )
    grad_expert_down = jnp.einsum(
        "ecr,ecf->ref", slot_grad, hidden_e, preferred_element_type=jnp.float32
    )
    pieces = (lax.all_gather(expert_down, "dp", axis=0, tiled=True),)
    hidden_grad_e = jnp.einsum(
        "ecr,ref->ecf", slot_grad, pieces[0], preferred_element_type=jnp.float32
    )
    gate_grad_e, up_grad_e = swiglu_back(hidden_grad_e, gate_e, up_e)
    pieces = (
        lax.all_gather(expert_gate, "dp", axis=0, tiled=True),
        lax.all_gather(expert_up, "dp", axis=0, tiled=True),
        lax.all_gather(router_weight, "dp", axis=0, tiled=True),
    )
    span_rows = pieces[0].shape[0]
    routed_cols = jnp.einsum(
        "ecf,ref->ecr", gate_grad_e, pieces[0], preferred_element_type=jnp.float32
    )
    routed_cols = (
        routed_cols
        + jnp.einsum("ecf,ref->ecr", up_grad_e, pieces[1], preferred_element_type=jnp.float32)
    ).reshape(experts * capacity, span_rows)
    router_cols = lax.dot_general(
        logit_grad, pieces[2].astype(jnp.float32), rows_contract, precision=exact_mode
    )
    moe_in_part = router_cols + jnp.sum(
        routed_cols[slot_of].reshape(seq_len, route_count, width_model), axis=1
    )
    moe_in_grad, router_total = (
        lax.psum(moe_in_part.astype(jnp.bfloat16), "tensor").astype(jnp.float32),
        lax.psum(router_part.astype(jnp.bfloat16), "tensor").astype(jnp.float32),
    )
    middle_norm_grad, gain_two_grad = rms_backward(moe_in_grad, normed_two, factor_two, gain_two)
    middle_grad = grad_full + middle_norm_grad
    grad_expert_gate = jnp.einsum(
        "ecr,ecf->ref", dispatched, gate_grad_e, preferred_element_type=jnp.float32
    )
    grad_expert_up = jnp.einsum(
        "ecr,ecf->ref", dispatched, up_grad_e, preferred_element_type=jnp.float32
    )
    result_gate, result_up, result_down, result_router, result_gain = (
        lax.psum_scatter(grad_expert_gate, "dp", scatter_dimension=0, tiled=True),
        lax.psum_scatter(grad_expert_up, "dp", scatter_dimension=0, tiled=True),
        lax.psum_scatter(grad_expert_down, "dp", scatter_dimension=0, tiled=True),
        lax.psum_scatter(router_total, "dp", scatter_dimension=0, tiled=True),
        lax.psum_scatter(gain_two_grad, "dp", scatter_dimension=0, tiled=True),
    )
    attn_out_grad = middle_grad.astype(jnp.bfloat16)
    grad_out_weight = lax.dot_general(
        attn_out_grad, context_low, tokens_contract, preferred_element_type=jnp.float32
    )
    context_grad = (
        jnp.dot(attn_out_grad, full_out, preferred_element_type=jnp.float32)
        .astype(jnp.bfloat16)
        .reshape(seq_len, kv_here, group, HDIM)
    )
    query_grad, key_grad, value_grad = attend_backward(
        queries, keys_rot, value_rows, log_total, context_grad, scale_value
    )
    query_lin_grad = (
        rotate_back(query_grad.reshape(seq_len, heads_here, HDIM), cos_tab, sin_tab)
        .reshape(seq_len, -1)
        .astype(jnp.bfloat16)
    )
    key_lin_grad = rotate_back(key_grad, cos_tab, sin_tab).reshape(seq_len, -1).astype(jnp.bfloat16)
    value_lin_grad = value_grad.reshape(seq_len, -1).astype(jnp.bfloat16)
    attn_in_part = lax.dot_general(
        query_lin_grad, full_query, rows_contract, preferred_element_type=jnp.float32
    )
    attn_in_part = attn_in_part + lax.dot_general(
        key_lin_grad, full_key, rows_contract, preferred_element_type=jnp.float32
    )
    attn_in_part = attn_in_part + lax.dot_general(
        value_lin_grad, full_value, rows_contract, preferred_element_type=jnp.float32
    )
    grad_query_weight = lax.dot_general(
        attn_in, query_lin_grad, tokens_contract, preferred_element_type=jnp.float32
    )
    grad_key_weight = lax.dot_general(
        attn_in, key_lin_grad, tokens_contract, preferred_element_type=jnp.float32
    )
    grad_value_weight = lax.dot_general(
        attn_in, value_lin_grad, tokens_contract, preferred_element_type=jnp.float32
    )
    attn_in_grad = lax.psum(attn_in_part.astype(jnp.bfloat16), "tensor").astype(jnp.float32)
    rows_norm_grad, gain_one_grad = rms_backward(attn_in_grad, normed_one, factor_one, gain_one)
    input_grad = lax.dynamic_slice_in_dim(
        middle_grad + rows_norm_grad, own_start, local_rows, 0
    ).astype(jnp.bfloat16)
    attn_results = (
        lax.psum_scatter(gain_one_grad, "dp", scatter_dimension=0, tiled=True),
        lax.psum_scatter(grad_query_weight, "dp", scatter_dimension=0, tiled=True),
        lax.psum_scatter(grad_key_weight, "dp", scatter_dimension=0, tiled=True),
        lax.psum_scatter(grad_value_weight, "dp", scatter_dimension=0, tiled=True),
        lax.psum_scatter(grad_out_weight, "dp", scatter_dimension=0, tiled=True),
    )
    return (
        output,
        input_grad,
        attn_results[0],
        attn_results[1],
        attn_results[2],
        attn_results[3],
        attn_results[4],
        result_gain,
        result_router,
        result_gate,
        result_up,
        result_down,
    )


def solution(mesh):
    in_specs = (
        P(("dp", "tensor"), None),
        P("dp", None),
        P(("dp", "tensor"), None),
        P("dp"),
        P("dp", "tensor"),
        P("dp", "tensor"),
        P("dp", "tensor"),
        P("dp", "tensor"),
        P("dp"),
        P("dp", None),
        P("dp", None, "tensor"),
        P("dp", None, "tensor"),
        P("dp", None, "tensor"),
    )
    out_specs = (
        P(("dp", "tensor"), None),
        P(("dp", "tensor"), None),
        P("dp"),
        P("dp", "tensor"),
        P("dp", "tensor"),
        P("dp", "tensor"),
        P("dp", "tensor"),
        P("dp"),
        P("dp", None),
        P("dp", None, "tensor"),
        P("dp", None, "tensor"),
        P("dp", None, "tensor"),
    )
    return jax.shard_map(body, mesh=mesh, in_specs=in_specs, out_specs=out_specs, check_vma=False)
```

profile of v0, /device:TPU:0, one launch (start us, length us, event | category | flops | bytes accessed | tf_op | source)
XLA Modules:
  0.0 3422.4 jit_solution(12245949478620615722)
XLA Ops:
  8.7 85.2 %all_gather.42 = bf16[1024,256]{1,0:T(8,128)(2,1)S(1)} all-gather(bf16[16,256]{1,0:T(8,128)(2,1)} %param.19), channel_id=1, replica_groups=mesh['dp'=64,'tensor'=2] {'dp'}, dimensions={0}, use_global_device_ids=true | all-gather | bytes 532480 | tf_op jit(solution)/shard_map/all_gather | solution.py:178
  93.9 10.9 all_gather.40
  108.5 138.6 %all-reduce.5 = (bf16[1024]{0:T(1024)(128)(2,1)S(1)}, bf16[1024]{0:T(1024)(128)(2,1)S(1)}) all-reduce(bf16[1024]{0:T(1024)(128)(2,1)S(1)} %dynamic-update-slice, bf16[1024]{0:T(1024)(128)(2,1)S(1)} %dynamic-update-slice.1), channel_id=1, replica_groups=mesh['dp'=64,'tensor'=2] {'dp'}, use_global_device_ids=true, to_apply=%add | all-reduce | flops 2048 | bytes 8192
  247.3 77.9 %all_gather.43 = bf16[1024,256]{1,0:T(8,128)(2,1)S(1)} all-gather(bf16[16,256]{1,0:T(8,128)(2,1)} %param.18), channel_id=1, replica_groups=mesh['dp'=64,'tensor'=2] {'dp'}, dimensions={0}, use_global_device_ids=true | all-gather | bytes 532480 | tf_op jit(solution)/shard_map/all_gather | solution.py:177
  332.2 2.8 fusion.68
  338.6 9.1 reduce-window.6
  348.3 13.4 all_gather.51
  362.9 8.1 scatter_custom_fusion
  370.9 8.1 scatter_custom_fusion.1
  379.1 9.0 gather_fusion.2
  388.0 82.8 %all_gather.47 = bf16[1024,32]{1,0:T(8,128)(2,1)S(1)} all-gather(bf16[16,32]{1,0:T(8,128)(2,1)S(1)} %copy-done.50), channel_id=1, replica_groups=mesh['dp'=64,'tensor'=2] {'dp'}, dimensions={0}, use_global_device_ids=true | all-gather | bytes 66560 | tf_op jit(solution)/shard_map/all_gather | solution.py:213
  473.5 8.9 gather_fusion
  483.0 13.6 gather_fusion.3
  496.8 14.7 all-gather.10.cloned.1.call-done
  511.5 12.0 fusion.6
  523.6 112.2 %all-gather.12.cloned.1.call-done = bf16[1024,32,256]{2,0,1:T(8,128)(2,1)} async-done(((bf16[16,32,256]{2,0,1:T(8,128)(2,1)}), bf16[1024,32,256]{2,0,1:T(8,128)(2,1)}) %all-gather.12.cloned.1.call-update) | async-done | bytes 16777232 | tf_op jit(solution)/shard_map/all_gather | solution.py:212
  635.8 12.0 fusion.4
  647.8 113.1 %all-gather.14.cloned.1.call-done = bf16[1024,32,256]{2,0,1:T(8,128)(2,1)} async-done(((bf16[16,32,256]{2,0,1:T(8,128)(2,1)}), bf16[1024,32,256]{2,0,1:T(8,128)(2,1)}) %all-gather.14.cloned.1.call-update) | async-done | bytes 16777232 | tf_op jit(solution)/shard_map/all_gather | solution.py:227
  760.9 15.5 multiply_convert_fusion.1
  776.4 11.0 fusion.71
  787.4 14.9 convolution_add_fusion
  802.3 15.7 gather_fusion.4
  818.0 6.5 bitcast_reduce_fusion
  824.6 11.0 fusion.70
  835.6 15.7 gather_fusion.1
  851.3 6.3 fusion.1
  857.8 2.7 fusion.17
  862.2 34.3 %all-reduce.13.cloned.1.call-done = bf16[256,1024]{1,0:T(8,128)(2,1)} async-done(((bf16[256,1024]{1,0:T(8,128)(2,1)}), bf16[256,1024]{1,0:T(8,128)(2,1)}) %all-reduce.13.cloned.1.call-update) | async-done | bytes 524304 | tf_op jit(solution)/shard_map/psum | solution.py:279
  896.5 2.4 fusion.25
  901.9 2.4 convolution_convert_fusion.1
  906.1 2.3 fusion.12
  913.7 53.7 %all-reduce.15.cloned.1.call-done = (bf16[256,1024]{1,0:T(8,128)(2,1)}, bf16[256,1024]{1,0:T(8,128)(2,1)}, bf16[1024,32]{1,0:T(8,128)(2,1)}) async-done(((bf16[256,1024]{1,0:T(8,128)(2,1)}, bf16[256,1024]{1,0:T(8,128)(2,1)}, bf16[1024,32]{1,0:T(8,128)(2,1)}), (bf16[256,1024]{1,0:T(8,128)(2,1)}, bf16[256,1024]{1,0:T(8,128)(2,1)}, bf16[1024,32]{1,0:T(8,128)(2,1)})) %all-reduce.15.cloned.1.call-update) | async-done | bytes 1114128 | tf_op jit(solution)/shard_map/psum | solution.py:235
  969.3 2.4 fusion.59
  977.3 15.7 convolution_bitcast_fusion.2
  993.1 34.2 copy.121
  1028.6 15.7 convolution_bitcast_fusion.1
  1044.3 34.1 copy.122
  1079.8 17.3 convolution_bitcast_fusion
  1097.0 34.3 %copy.123 = f32[1024,32,256]{2,1,0:T(8,128)} copy(f32[1024,32,256]{0,2,1:T(8,128)} %convolution_bitcast_fusion) | data formatting | bytes 67108864 | tf_op jit(solution)/shard_map/ecr,ecf->ref/transpose | solution.py:251
  1134.1 145.0 %all-reduce.4 = (f32[1024]{0:T(1024)S(1)}, f32[1024]{0:T(1024)S(1)}) all-reduce(f32[1024]{0:T(1024)S(1)} %get-tuple-element.85, f32[1024]{0:T(1024)S(1)} %copy-done.48), channel_id=2, replica_groups=mesh['dp'=64,'tensor'=2] {'dp'}, use_global_device_ids=true, to_apply=%region_25.26.clone | all-reduce | flops 2048 | bytes 16384
  1280.3 2.2 fusion.28
  1282.6 256.2 %reduce-scatter.11.cloned.1.call-done = f32[16,256]{1,0:T(8,128)} async-done(((f32[1024,256]{1,0:T(8,128)}), f32[16,256]{1,0:T(8,128)}) %reduce-scatter.11.cloned.1.call-update) | async-done | bytes 16400 | tf_op jit(solution)/shard_map/reduce_scatter | solution.py:342
  1538.7 284.5 %reduce-scatter.13.cloned.1.call-done = f32[16,256]{1,0:T(8,128)} async-done(((f32[1024,256]{1,0:T(8,128)}), f32[16,256]{1,0:T(8,128)}) %reduce-scatter.13.cloned.1.call-update) | async-done | bytes 16400 | tf_op jit(solution)/shard_map/reduce_scatter | solution.py:343
  1823.2 285.8 %reduce-scatter.9.cloned.1.call-done = f32[16,512]{1,0:T(8,128)} async-done(((f32[1024,512]{1,0:T(8,128)}), f32[16,512]{1,0:T(8,128)}) %reduce-scatter.9.cloned.1.call-update) | async-done | bytes 32784 | tf_op jit(solution)/shard_map/reduce_scatter | solution.py:341
  2109.0 286.7 %reduce-scatter.15.cloned.1.call-done = f32[16,512]{1,0:T(8,128)} async-done(((f32[1024,512]{1,0:T(8,128)}), f32[16,512]{1,0:T(8,128)}) %reduce-scatter.15.cloned.1.call-update) | async-done | bytes 32784 | tf_op jit(solution)/shard_map/reduce_scatter | solution.py:344
  2395.7 340.2 %reduce-scatter.19.cloned.1.call-done = f32[16,32,256]{2,1,0:T(8,128)} async-done(((f32[1024,32,256]{2,1,0:T(8,128)}), f32[16,32,256]{2,1,0:T(8,128)}) %reduce-scatter.19.cloned.1.call-update) | async-done | bytes 524304 | tf_op jit(solution)/shard_map/reduce_scatter | solution.py:291
  2735.9 339.9 %reduce-scatter.21.cloned.1.call-done = f32[16,32,256]{2,1,0:T(8,128)} async-done(((f32[1024,32,256]{2,1,0:T(8,128)}), f32[16,32,256]{2,1,0:T(8,128)}) %reduce-scatter.21.cloned.1.call-update) | async-done | bytes 524304 | tf_op jit(solution)/shard_map/reduce_scatter | solution.py:292
  3075.8 339.8 %reduce-scatter.23.cloned.1.call-done = f32[16,32,256]{2,1,0:T(8,128)} async-done(((f32[1024,32,256]{2,1,0:T(8,128)}), f32[16,32,256]{2,1,0:T(8,128)}) %reduce-scatter.23.cloned.1.call-update) | async-done | bytes 524304 | tf_op jit(solution)/shard_map/reduce_scatter | solution.py:293
  (229 shorter events, 45.0 us)
Async XLA Ops:
  7.2 319.9 %all-gather.6.cloned.1.call-start = ((), (), s32[]{:S(2)}) async-start(), calls=%async_computation.8 | async-start | bytes 1064960 | tf_op jit(solution)/shard_map/all_gather | solution.py:176
  7.9 324.3 %all-gather.8.cloned.1.call-start = ((), (), s32[]{:S(2)}) async-start(), calls=%async_computation.9 | async-start | bytes 1064960 | tf_op jit(solution)/shard_map/all_gather | solution.py:179
  8.7 462.2 %all-reduce.11.cloned.1.call-start = ((), (), s32[]{:S(2)}) async-start(), calls=%async_computation.10 | async-start | bytes 2097152 | tf_op jit(solution)/shard_map/psum | solution.py:203
  93.9 235.2 %copy-start.17 = (bf16[1024,256]{1,0:T(8,128)(2,1)}, bf16[1024,256]{1,0:T(8,128)(2,1)S(1)}, u32[]{:S(2)}) copy-start(bf16[1024,256]{1,0:T(8,128)(2,1)S(1)} %all_gather.42) | copy-start | bytes 1572868
  104.9 366.0 %copy-start.2 = (bf16[256,1024]{1,0:T(8,128)(2,1)}, bf16[256,1024]{1,0:T(8,128)(2,1)S(1)}, u32[]{:S(2)}) copy-start(bf16[256,1024]{1,0:T(8,128)(2,1)S(1)} %all_gather.40) | copy-start | bytes 1572868
  247.1 81.9 %copy-start.43 = (f32[1024]{0:T(1024)}, f32[1024]{0:T(1024)S(1)}, u32[]{:S(2)}) copy-start(f32[1024]{0:T(1024)S(1)} %convert_element_type.131) | copy-start | bytes 12292
  247.3 81.7 %copy-start.46 = (f32[256]{0:T(256)}, f32[256]{0:T(256)S(1)}, u32[]{:S(2)}) copy-start(f32[256]{0:T(256)S(1)} %add_rsqrt_fusion.1) | copy-start | bytes 3076
  325.2 5.2 copy-start.19
  326.5 4.2 copy-start.24
  326.5 4.2 copy-start.27
  327.1 5.1 copy-start.29
  329.9 5.3 copy-start.33
  329.9 6.2 copy-start.34
  330.4 6.6 copy-start.35
  330.4 7.5 copy-start.42
  330.8 17.3 copy-start.38
  331.7 16.6 copy-start.32
  332.2 16.1 copy-start.13
  335.1 176.4 %all-gather.10.cloned.1.call-start = ((), (), s32[]{:S(2)}) async-start(), calls=%async_computation.11 | async-start | bytes 17039360 | tf_op jit(solution)/shard_map/all_gather | solution.py:211
  336.0 299.8 %all-gather.12.cloned.1.call-start = ((), (), s32[]{:S(2)}) async-start(), calls=%async_computation.12 | async-start | bytes 17039360 | tf_op jit(solution)/shard_map/all_gather | solution.py:212
  337.0 423.9 %all-gather.14.cloned.1.call-start = ((), (), s32[]{:S(2)}) async-start(), calls=%async_computation.13 | async-start | bytes 17039360 | tf_op jit(solution)/shard_map/all_gather | solution.py:227
  337.9 558.6 %all-reduce.13.cloned.1.call-start = ((), (), s32[]{:S(2)}) async-start(), calls=%async_computation.14 | async-start | bytes 1048576 | tf_op jit(solution)/shard_map/psum | solution.py:279
  338.3 558.2 %copy-start.45 = (f32[1024]{0:T(1024)}, f32[1024]{0:T(1024)S(1)}, u32[]{:S(2)}) copy-start(f32[1024]{0:T(1024)S(1)} %convert_element_type.140) | copy-start | bytes 12292
  379.0 9.0 copy-start.50
  472.3 424.1 %copy-start.49 = (f32[256]{0:T(256)}, f32[256]{0:T(256)S(1)}, u32[]{:S(2)}) copy-start(f32[256]{0:T(256)S(1)} %add_rsqrt_fusion) | copy-start | bytes 3076
  496.8 264.1 %copy-start.40 = (f32[32,80]{1,0:T(8,128)}, f32[32,80]{1,0:T(8,128)S(1)}, u32[]{:S(2)}) copy-start(f32[32,80]{1,0:T(8,128)S(1)} %mul.384) | copy-start | bytes 30724
  818.0 6.5 copy-start.7
  857.8 48.3 %copy-start.30 = (bf16[256,256]{0,1:T(8,128)(2,1)S(1)}, bf16[256,256]{0,1:T(8,128)(2,1)}, u32[]{:S(2)}) copy-start(bf16[256,256]{0,1:T(8,128)(2,1)} %copy-done.29) | copy-start | bytes 393220
  857.8 48.3 %copy-start.39 = (f32[1,8,256]{2,1,0:T(8,128)S(1)}, f32[1,8,256]{2,1,0:T(8,128)}, u32[]{:S(2)}) copy-start(f32[1,8,256]{2,1,0:T(8,128)} %copy-done.38) | copy-start | bytes 24580
  860.5 106.9 %all-reduce.15.cloned.1.call-start = ((), (), s32[]{:S(2)}) async-start(), calls=%async_computation.23 | async-start | bytes 2621440 | tf_op jit(solution)/shard_map/psum | solution.py:235
  898.9 9.5 copy-start.1
  906.1 4.2 copy-start.22
  911.4 57.9 %copy-start.3 = (bf16[256,1024]{1,0:T(8,128)(2,1)S(1)}, bf16[256,1024]{1,0:T(8,128)(2,1)}, u32[]{:S(2)}) copy-start(bf16[256,1024]{1,0:T(8,128)(2,1)} %copy-done.2) | copy-start | bytes 1572868
  911.4 57.9 %copy-start.44 = (f32[1024]{0:T(1024)S(1)}, f32[1024]{0:T(1024)}, u32[]{:S(2)}) copy-start(f32[1024]{0:T(1024)} %copy-done.43) | copy-start | bytes 12292
  911.4 57.9 %copy-start.47 = (f32[256]{0:T(256)S(1)}, f32[256]{0:T(256)}, u32[]{:S(2)}) copy-start(f32[256]{0:T(256)} %copy-done.46) | copy-start | bytes 3076
  911.6 57.6 %copy-start.23 = (bf16[256,4,64]{0,2,1:T(8,128)(2,1)}, bf16[256,4,64]{0,2,1:T(8,128)(2,1)S(1)}, u32[]{:S(2)}) copy-start(bf16[256,4,64]{0,2,1:T(8,128)(2,1)S(1)} %fusion.42) | copy-start | bytes 393220
  913.7 368.9 %reduce-scatter.17.cloned.1.call-start = ((), (), s32[]{:S(2)}) async-start(), calls=%async_computation.19 | async-start | bytes 532480 | tf_op jit(solution)/shard_map/reduce_scatter | solution.py:294
  969.2 6.1 copy-start.10
  969.3 6.1 copy-start.14
  969.3 569.5 %reduce-scatter.11.cloned.1.call-start = ((), (), s32[]{:S(2)}) async-start(), calls=%async_computation.16 | async-start | bytes 1064960 | tf_op jit(solution)/shard_map/reduce_scatter | solution.py:342
  971.8 851.4 %reduce-scatter.13.cloned.1.call-start = ((), (), s32[]{:S(2)}) async-start(), calls=%async_computation.17 | async-start | bytes 1064960 | tf_op jit(solution)/shard_map/reduce_scatter | solution.py:343
  973.3 1135.7 %reduce-scatter.9.cloned.1.call-start = ((), (), s32[]{:S(2)}) async-start(), calls=%async_computation.15 | async-start | bytes 2129920 | tf_op jit(solution)/shard_map/reduce_scatter | solution.py:341
  975.3 1420.4 %reduce-scatter.15.cloned.1.call-start = ((), (), s32[]{:S(2)}) async-start(), calls=%async_computation.18 | async-start | bytes 2129920 | tf_op jit(solution)/shard_map/reduce_scatter | solution.py:344
  977.3 1758.6 %reduce-scatter.19.cloned.1.call-start = ((), (), s32[]{:S(2)}) async-start(), calls=%async_computation.20 | async-start | bytes 34078720 | tf_op jit(solution)/shard_map/reduce_scatter | solution.py:291
  1027.3 2048.5 %reduce-scatter.21.cloned.1.call-start = ((), (), s32[]{:S(2)}) async-start(), calls=%async_computation.21 | async-start | bytes 34078720 | tf_op jit(solution)/shard_map/reduce_scatter | solution.py:292
  1078.5 2337.1 %reduce-scatter.23.cloned.1.call-start = ((), (), s32[]{:S(2)}) async-start(), calls=%async_computation.22 | async-start | bytes 34078720 | tf_op jit(solution)/shard_map/reduce_scatter | solution.py:293
  1131.3 149.0 %copy-start.5 = (f32[256,1024]{1,0:T(8,128)S(1)}, f32[256,1024]{1,0:T(8,128)}, u32[]{:S(2)}) copy-start(f32[256,1024]{1,0:T(8,128)} %copy-done.4) | copy-start | bytes 3145732
  1131.3 149.0 %copy-start.11 = (f32[256,1024]{1,0:T(8,128)S(1)}, f32[256,1024]{1,0:T(8,128)}, u32[]{:S(2)}) copy-start(f32[256,1024]{1,0:T(8,128)} %copy-done.9) | copy-start | bytes 3145732
  (19 other events, 27.8 us)
Sparse Core Ops, SparseCore 0:
  9.7 104.0 all-gather.5
  115.6 100.5 all-gather.7
  335.2 50.9 all-reduce.10
  388.5 122.9 all-gather.9
  513.8 121.9 all-gather.11
  638.1 122.7 all-gather.13
  860.7 35.7 all-reduce.12
  913.8 53.5 all-reduce.14
  970.5 283.5 reduce-scatter.16
  1256.8 281.8 reduce-scatter.10
  1541.8 281.3 reduce-scatter.12
  1826.0 282.9 reduce-scatter.8
  2112.0 283.6 reduce-scatter.14
  2398.5 337.3 reduce-scatter.18
  2738.7 337.0 reduce-scatter.20
  3078.6 336.9 reduce-scatter.22
where the time goes:
time: 3430 us; the launch traced here: 3420 us
  waiting for transfers between devices  2460 us (72%)
  blocking collectives  554 us (16%)
  local copies, waits for them, and re-layouts  199 us (6%)
  matrix products  153 us (4%)
  other arithmetic  36.8 us (1%)
    reduce_scatter x1, waiting for transfers between devices, body(): lax.psum_scatter(grad_expert_gate, 'dp', scatter_dimension=0, tiled=True)  340 us
    reduce_scatter x1, waiting for transfers between devices, body(): lax.psum_scatter(grad_expert_up, 'dp', scatter_dimension=0, tiled=True)  340 us
    reduce_scatter x1, waiting for transfers between devices, body(): lax.psum_scatter(grad_expert_down, 'dp', scatter_dimension=0, tiled=True)  340 us
    reduce_scatter x1, waiting for transfers between devices, body(): lax.psum_scatter(grad_out_weight, 'dp', scatter_dimension=0, tiled=True)  287 us
    reduce_scatter x1, waiting for transfers between devices, body(): lax.psum_scatter(grad_query_weight, 'dp', scatter_dimension=0, tiled=True)  286 us
    reduce_scatter x1, waiting for transfers between devices, body(): lax.psum_scatter(grad_value_weight, 'dp', scatter_dimension=0, tiled=True)  284 us
    unnamed x2, blocking collectives  284 us
    reduce_scatter x1, waiting for transfers between devices, body(): lax.psum_scatter(grad_key_weight, 'dp', scatter_dimension=0, tiled=True)  256 us
  transfers between devices with their start and end apart: 16, of which 12 were waited for; matrix products, arithmetic and copies ran while one was open for 8% of the time, Pallas kernels for 0%

commit v1 on v0

v1 whole, which is shorter than its diff:
```python
import functools

import jax
import jax.numpy as jnp
from jax import lax
from jax.experimental import pallas as pl
from jax.experimental.pallas import tpu as pltpu
from jax.sharding import Mesh, PartitionSpec as P

bf16 = jnp.bfloat16
f32 = jnp.float32

D = 1024
HDIM = 64
SEQ = 256
HALF = 128
EXPERTS = 32
CAP = 80
SLOTS = 16 * CAP
EXT = D + 128
PACK = 1664
NORM_EPS = 1e-06
ROPE_BASE = 10000.0
SCALE = 0.125
PLANE = ("x", "z")
CHIPS = ("yl", "x", "z")
NT = (((1,), (1,)), ((), ()))
TN = (((0,), (0,)), ((), ()))
VMEM_BYTES = 56 * 1024 * 1024


def mo(value, by):
    return pl.multiple_of(value, by)


def dot(a, b, dims=(((1,), (0,)), ((), ()))):
    return lax.dot_general(a, b, dims, preferred_element_type=f32)


def split(value):
    high = value.astype(bf16)
    return high, (value - high.astype(f32)).astype(bf16)


def iota(shape, dim):
    return lax.broadcasted_iota(jnp.int32, shape, dim)


def call(kernel, outs, args, scratch=(), grid=None, in_specs=None, out_specs=None, flops=0):
    smem = pl.BlockSpec(memory_space=pltpu.SMEM)
    params = pltpu.CompilerParams(vmem_limit_bytes=VMEM_BYTES)
    out_shape = [jax.ShapeDtypeStruct(shape, kind) for shape, kind in outs]
    nbytes = sum(a.size * a.dtype.itemsize for a in args) + sum(
        o.size * jnp.dtype(o.dtype).itemsize for o in out_shape
    )
    cost = pl.CostEstimate(flops=flops, bytes_accessed=nbytes, transcendentals=0)
    if grid is None:
        vmem = pl.BlockSpec(memory_space=pltpu.VMEM)
        in_specs = [smem] + [vmem] * (len(args) - 1)
        out_specs = [vmem] * len(outs)
        return pl.pallas_call(
            kernel,
            out_shape=out_shape,
            in_specs=in_specs,
            out_specs=out_specs,
            scratch_shapes=scratch,
            compiler_params=params,
            cost_estimate=cost,
        )(*args)
    return pl.pallas_call(
        kernel,
        grid=grid,
        out_shape=out_shape,
        in_specs=[smem] + in_specs,
        out_specs=out_specs,
        scratch_shapes=scratch,
        compiler_params=params,
        cost_estimate=cost,
    )(*args)


def route_kernel(pos, routes, cot_own, cot_oth, tab, mask_out, grad, sent, turned):
    half = pos[0]
    named = routes[...]
    lane = iota((SEQ, 128), 1)
    mask = jnp.zeros((SEQ, 128), f32)
    for k in range(named.shape[1]):
        mask = mask + jnp.where(named[:, k : k + 1] == lane, 1.0, 0.0)
    mask_out[...] = mask
    below = jnp.where(iota((SEQ, SEQ), 0) > iota((SEQ, SEQ), 1), 1.0, 0.0).astype(bf16)
    place = dot(below, mask.astype(bf16))
    turned[...] = jnp.where(mask > 0.0, place, -1.0).T
    slot = iota((CAP, SEQ), 0).astype(f32)
    for i in range(16):
        row = turned[pl.ds(half * 16 + i, 1), :]
        tab[i * CAP : (i + 1) * CAP, :] = jnp.where(slot == row, 1.0, 0.0).astype(bf16)
    grad[pl.ds(mo(half * HALF, HALF), HALF), :] = cot_own[...]
    grad[pl.ds(mo((1 - half) * HALF, HALF), HALF), :] = cot_oth[...]
    for n in range(4):
        cols = slice(n * 256, (n + 1) * 256)
        sent[:, cols] = dot(tab[...], grad[:, cols]).astype(bf16)


def swap_halves(u, low):
    return jnp.where(low, pltpu.roll(u, 224, 1), pltpu.roll(u, 32, 1))


def doubled(tile, low, which):
    other = pltpu.roll(tile, 64, 1)
    return jnp.where(low, tile, other) if which == 0 else jnp.where(low, other, tile)


def stacked(tile, low):
    zero = jnp.zeros_like(tile)
    return jnp.concatenate([jnp.where(low, tile, zero), jnp.where(low, zero, tile)], axis=0)


def attn_kernel(
    pos, tok_own, tok_oth, w_mine, w_oth, cos, sin,
    rows, w, aux, attn_in, q_out, k_out, v_out, ctx, lse_out, part,
):
    half, core = pos[0], pos[1]
    rows[pl.ds(mo(half * HALF, HALF), HALF), :] = tok_own[...]
    rows[pl.ds(mo((1 - half) * HALF, HALF), HALF), :] = tok_oth[...]
    for i in range(32):
        w[pl.ds(mo(i * 32 + core * 16, 16), 16), :] = w_mine[i]
        w[pl.ds(mo(i * 32 + (1 - core) * 16, 16), 16), :] = w_oth[i]
    aux[...] = w[:, 1536:PACK].astype(f32).T
    x = rows[...].astype(f32)
    factor = lax.rsqrt(jnp.mean(x * x, axis=1, keepdims=True) + NORM_EPS)
    attn_in[...] = (x * factor * aux[32:33, :]).astype(bf16)
    low32 = iota((SEQ, 256), 1) % 64 < 32
    low = iota((SEQ, 128), 1) < 64
    for n in range(4):
        lin = dot(attn_in[...], w[:, n * 256 : (n + 1) * 256])
        if n < 3:
            lin = lin * cos[...] + swap_halves(lin, low32) * sin[...]
        if n < 2:
            q_out[:, n * 256 : (n + 1) * 256] = lin.astype(bf16)
        else:
            dst = k_out if n == 2 else v_out
            for m in range(4):
                tile = lin[:, (m // 2) * 128 : (m // 2) * 128 + 128]
                dst[:, m * 128 : (m + 1) * 128] = doubled(tile, low, m % 2).astype(bf16)
    allowed = iota((2 * SEQ, SEQ), 0) % SEQ >= iota((2 * SEQ, SEQ), 1)
    for m in range(4):
        cols = slice(m * 128, (m + 1) * 128)
        scores = dot(stacked(q_out[:, cols], low), k_out[:, cols], NT) * SCALE
        scores = jnp.where(allowed, scores, -1e30)
        peak = jnp.max(scores, axis=1, keepdims=True)
        raised = jnp.exp(scores - peak)
        total = jnp.sum(raised, axis=1, keepdims=True)
        lse_out[m] = jnp.broadcast_to(peak + jnp.log(total), (2 * SEQ, 128))
        probs = (raised * (1.0 / total)).astype(bf16)
        both = dot(probs, v_out[:, cols])
        ctx[:, cols] = jnp.where(low, both[:SEQ], both[SEQ:]).astype(bf16)
    for n in range(4):
        outs = slice(n * 256, (n + 1) * 256)
        part[:, outs] = dot(ctx[...], w[outs, 1024:1536], NT).astype(bf16)


def mid_kernel(pos, rows, part_own, part_oth, aux, tab, mask, middle, moe_in, gates_out, sent):
    value = rows[...].astype(f32) + (part_own[...].astype(f32) + part_oth[...].astype(f32))
    middle[...] = value
    factor = lax.rsqrt(jnp.mean(value * value, axis=1, keepdims=True) + NORM_EPS)
    moe_in[...] = (value * factor * aux[33:34, :]).astype(bf16)
    logits = dot(moe_in[...], aux[...].astype(bf16), NT)
    chosen = jnp.where(mask[...] > 0.0, logits, -1e30)
    raised = jnp.exp(chosen - jnp.max(chosen, axis=1, keepdims=True)) * mask[...]
    gates = raised / jnp.sum(raised, axis=1, keepdims=True)
    gates_out[...] = gates
    high = gates.astype(bf16).astype(f32)
    extra = (high + pltpu.roll(gates - high, 32, 1)).astype(bf16)
    for n in range(4):
        cols = slice(n * 256, (n + 1) * 256)
        sent[:, cols] = dot(tab[...], moe_in[:, cols]).astype(bf16)
    sent[:, D:EXT] = dot(tab[...], extra).astype(bf16)


def expert_kernel(pos, x, c, w_a, w_b, w_c, w_d, dx, gate_g, up_g, scaled, w_down, w_gate, w_up):
    core, late, expert = pos[1], pos[2], pos[3]

    @pl.when(pl.program_id(0) == 0)
    def _():
        for src, at_late, at_core in (
            (w_a, late, core),
            (w_b, 1 - late, core),
            (w_c, late, 1 - core),
            (w_d, 1 - late, 1 - core),
        ):
            for i in range(16):
                rows = pl.ds(mo((at_late * 16 + i) * 32 + at_core * 16, 16), 16)
                for f in range(2):
                    for j, dst in enumerate((w_gate, w_up, w_down)):
                        dst[rows, f * 256 : (f + 1) * 256] = src[f, i, :, j * 256 : (j + 1) * 256]

    ext = x[:, D:EXT].astype(f32)
    lane = iota(ext.shape, 1)
    here, here_low = lane == expert, lane == expert + EXPERTS
    gate = jnp.sum(jnp.where(here | here_low, ext, 0.0), axis=1, keepdims=True)
    g = dot(x[:, :D], w_gate[...])
    u = dot(x[:, :D], w_up[...])
    sig = jax.nn.sigmoid(g)
    silu = g * sig
    hidden = (silu * u).astype(bf16).astype(f32)
    raw = dot(c[...], w_down[...])
    gate_grad = jnp.sum(hidden * raw, axis=1, keepdims=True)
    back = gate * raw
    gate_g[...] = (back * u * sig * (1.0 + g * (1.0 - sig))).astype(bf16)
    up_g[...] = (back * silu).astype(bf16)
    scaled[...] = (gate * hidden).astype(bf16)
    for n in range(4):
        cols = slice(n * 256, (n + 1) * 256)
        dx[:, cols] = (dot(gate_g[...], w_gate[cols, :], NT) + dot(up_g[...], w_up[cols, :], NT)).astype(bf16)
    high = gate_grad.astype(bf16).astype(f32)
    dx[:, D:EXT] = jnp.where(here, high, jnp.where(here_low, gate_grad - high, 0.0)).astype(bf16)


def expert_grad_kernel(pos, x, c, gate_g, up_g, scaled, w_down, y, mine, sent, held):
    core = pos[1]
    y[...] = dot(scaled[...], w_down[...], NT).astype(bf16)
    for j, (lhs, rhs) in enumerate(((x, gate_g), (x, up_g), (c, scaled))):
        held[...] = dot(lhs[...], rhs[...], TN).astype(bf16)
        for i in range(8):
            cols = slice(j * 512, (j + 1) * 512)
            mine[i, :, cols] = held[pl.ds(mo(i * 32 + core * 16, 16), 16), :]
            sent[i, :, cols] = held[pl.ds(mo(i * 32 + (1 - core) * 16, 16), 16), :]


def combine_kernel(pos, tab, got, out):
    for start in range(0, EXT, 256):
        cols = slice(start, min(start + 256, EXT))
        out[:, cols] = dot(tab[...], got[:, cols], TN).astype(bf16)


def finish_kernel(pos, tab, got, middle, own, sent, held):
    half = pos[0]
    for n in range(4):
        cols = slice(n * 256, (n + 1) * 256)
        held[:, cols] = dot(tab[...], got[:, cols], TN)
    mine = pl.ds(mo(half * HALF, HALF), HALF)
    own[...] = middle[mine, :] + held[mine, :]
    sent[...] = held[pl.ds(mo((1 - half) * HALF, HALF), HALF), :].astype(bf16)


def back_kernel(
    pos, comb_own, comb_oth, middle, moe_in, gates, aux, grad, rows, attn_in, w, q, k, v, ctx, lse, cos, sin,
    mg_own, part_own, part_sent, mine, sent, mg, dlin, cgrad, aog, apart, pack,
):
    half, core = pos[0], pos[1]
    low32 = iota((SEQ, 256), 1) % 64 < 32
    low = iota((SEQ, 128), 1) < 64
    gg = comb_own[:, D:EXT].astype(f32) + comb_oth[:, D:EXT].astype(f32)
    gg = gg + pltpu.roll(gg, 96, 1)
    gate = gates[...]
    logit_grad = gate * (gg - jnp.sum(gate * gg, axis=1, keepdims=True))
    lg_high, lg_low = split(logit_grad)
    router_t = aux[...].astype(bf16)
    moe_grad = comb_own[:, :D].astype(f32) + comb_oth[:, :D].astype(f32)
    moe_grad = moe_grad + dot(lg_high, router_t) + dot(lg_low, router_t)
    router_grad = dot(lg_high, moe_in[...], TN) + dot(lg_low, moe_in[...], TN)
    value = middle[...]
    factor = lax.rsqrt(jnp.mean(value * value, axis=1, keepdims=True) + NORM_EPS)
    normed = value * factor
    gain_two = jnp.sum(moe_grad * normed, axis=0, keepdims=True)
    inner = moe_grad * aux[33:34, :]
    mg[...] = grad[...].astype(f32) + factor * (
        inner - normed * jnp.mean(inner * normed, axis=1, keepdims=True)
    )
    mg_own[...] = mg[pl.ds(mo(half * HALF, HALF), HALF), :]
    aog[...] = mg[...].astype(bf16)
    for n in range(2):
        cols = slice(n * 256, (n + 1) * 256)
        cgrad[:, cols] = dot(aog[...], w[:, 1024 + n * 256 : 1280 + n * 256]).astype(bf16)
        pack[:, 1024 + n * 256 : 1280 + n * 256] = dot(aog[...], ctx[:, cols], TN).astype(bf16)
    allowed = iota((2 * SEQ, SEQ), 0) % SEQ >= iota((2 * SEQ, SEQ), 1)
    for m in range(4):
        cols = slice(m * 128, (m + 1) * 128)
        qs = stacked(q[:, cols], low)
        cs = stacked(cgrad[:, cols], low)
        scores = dot(qs, k[:, cols], NT) * SCALE
        probs = jnp.where(allowed, jnp.exp(scores - lse[m][:, :1]), 0.0)
        back = dot(cs, v[:, cols], NT)
        spread = jnp.sum(probs * back, axis=1, keepdims=True)
        sg = (probs * (back - spread)).astype(bf16)
        dq = dot(sg, k[:, cols])
        dlin[:, cols] = jnp.where(low, dq[:SEQ], dq[SEQ:]) * SCALE
        dk = dot(sg, qs, TN) * SCALE
        dv = dot(probs.astype(bf16), cs, TN)
        dk = dk + pltpu.roll(dk, 64, 1)
        dv = dv + pltpu.roll(dv, 64, 1)
        for base, val in ((512, dk), (768, dv)):
            at = slice(base + (m // 2) * 128, base + (m // 2) * 128 + 128)
            if m % 2 == 0:
                dlin[:, at] = val
            else:
                dlin[:, at] = jnp.where(low, dlin[:, at], val)
    lows = []
    for n in range(4):
        cols = slice(n * 256, (n + 1) * 256)
        lin = dlin[:, cols]
        if n < 3:
            lin = lin * cos[...] - swap_halves(lin, low32) * sin[...]
        lin = lin.astype(bf16)
        lows.append(lin)
        pack[:, cols] = dot(attn_in[...], lin, TN).astype(bf16)
    lows = jnp.concatenate(lows, axis=1)
    for n in range(4):
        cols = slice(n * 256, (n + 1) * 256)
        apart[:, cols] = dot(lows, w[cols, :1024], NT)
    part_own[...] = apart[pl.ds(mo(half * HALF, HALF), HALF), :]
    part_sent[...] = apart[pl.ds(mo((1 - half) * HALF, HALF), HALF), :].astype(bf16)
    x = rows[...].astype(f32)
    normed_one = x * lax.rsqrt(jnp.mean(x * x, axis=1, keepdims=True) + NORM_EPS)
    gain_one = jnp.sum(apart[...] * normed_one, axis=0, keepdims=True)
    at_row = iota((128, D), 0)
    small = jnp.where(at_row == 32, gain_one, jnp.where(at_row == 33, gain_two, router_grad))
    pack[:, 1536:PACK] = small.T.astype(bf16)
    for i in range(32):
        mine[i] = pack[pl.ds(mo(i * 32 + core * 16, 16), 16), :]
        sent[i] = pack[pl.ds(mo(i * 32 + (1 - core) * 16, 16), 16), :]


def input_kernel(pos, tok, aux, mg, part_own, part_oth, out):
    x = tok[...].astype(f32)
    factor = lax.rsqrt(jnp.mean(x * x, axis=1, keepdims=True) + NORM_EPS)
    normed = x * factor
    inner = (part_own[...] + part_oth[...].astype(f32)) * aux[32:33, :]
    inner = factor * (inner - normed * jnp.mean(inner * normed, axis=1, keepdims=True))
    out[...] = (mg[...] + inner).astype(bf16)


def rotary_tables():
    half_dim = HDIM // 2
    frequency = ROPE_BASE ** (-(jnp.arange(half_dim, dtype=f32) * 2.0 / HDIM))
    angles = jnp.arange(SEQ, dtype=f32)[:, None] * frequency[None, :]
    cos, sin = jnp.cos(angles), jnp.sin(angles)
    cos = jnp.concatenate([cos, cos], axis=1)
    sin = jnp.concatenate([-sin, sin], axis=1)
    return jnp.tile(cos, (1, 4)), jnp.tile(sin, (1, 4))


def swap(value, axis):
    return lax.ppermute(value, axis, [(0, 1), (1, 0)])


def body(
    tokens,
    routes,
    cotangent,
    attn_gain,
    query_weight,
    key_weight,
    value_weight,
    out_weight,
    moe_gain,
    router_weight,
    expert_gate,
    expert_up,
    expert_down,
):
    half, core, late = lax.axis_index("yh"), lax.axis_index("c"), lax.axis_index("yl")
    place = lax.axis_index("x") * 4 + lax.axis_index("z")
    pos = jnp.stack([half, core, late, half * 16 + place]).astype(jnp.int32)
    cos, sin = rotary_tables()

    packed = jnp.concatenate(
        [
            query_weight, key_weight, value_weight, out_weight, router_weight,
            attn_gain[:, None], moe_gain[:, None], jnp.zeros((16, 94), bf16),
        ],
        axis=1,
    )
    packed = jnp.broadcast_to(packed[None], (32, 16, PACK))
    w_mine = lax.all_to_all(packed, CHIPS, 0, 0, tiled=True)
    w_oth = swap(w_mine, "c")
    tok_oth = swap(tokens, "yh")
    cot_oth = swap(cotangent, "yh")

    tab, mask, grad, cot_sent = call(
        route_kernel,
        [((SLOTS, SEQ), bf16), ((SEQ, 128), f32), ((SEQ, D), bf16), ((SLOTS, D), bf16)],
        [pos, routes, cotangent, cot_oth],
        scratch=[pltpu.VMEM((128, SEQ), f32)],
        flops=700_000_000,
    )
    cot_slots = lax.all_to_all(cot_sent, PLANE, 0, 0, tiled=True)

    experts = jnp.stack([expert_gate, expert_up, expert_down])
    experts = experts.reshape(3, 16, 2, 16, 256).transpose(3, 2, 1, 0, 4).reshape(16, 2, 16, 768)
    experts = lax.all_to_all(experts, PLANE, 0, 0, tiled=True)
    e_own = lax.dynamic_index_in_dim(experts, half, 1, keepdims=False)
    e_oth = swap(lax.dynamic_index_in_dim(experts, 1 - half, 1, keepdims=False), "yh")
    e_a = jnp.stack([e_own, e_oth])
    e_b = swap(e_a, "yl")
    e_c = swap(e_a, "c")
    e_d = swap(e_b, "c")

    rows, w, aux, attn_in, q, k, v, ctx, lse, part = call(
        attn_kernel,
        [
            ((SEQ, D), bf16), ((D, PACK), bf16), ((128, D), f32), ((SEQ, D), bf16), ((SEQ, 512), bf16),
            ((SEQ, 512), bf16), ((SEQ, 512), bf16), ((SEQ, 512), bf16), ((4, 512, 128), f32), ((SEQ, D), bf16),
        ],
        [pos, tokens, tok_oth, w_mine, w_oth, cos, sin],
        flops=2_000_000_000,
    )
    part_oth = swap(part, "yh")
    middle, moe_in, gates, x_sent = call(
        mid_kernel,
        [((SEQ, D), f32), ((SEQ, D), bf16), ((SEQ, 128), f32), ((SLOTS, EXT), bf16)],
        [pos, rows, part, part_oth, aux, tab, mask],
        flops=800_000_000,
    )
    x_slots = lax.all_to_all(x_sent, PLANE, 0, 0, tiled=True)

    whole = pl.BlockSpec((2, 16, 16, 768), lambda i: (0, 0, 0, 0))
    by_row = lambda cols: pl.BlockSpec((256, cols), lambda i: (i, 0))
    dx, gate_g, up_g, scaled, w_down = call(
        expert_kernel,
        [
            ((SLOTS, EXT), bf16), ((SLOTS, 512), bf16), ((SLOTS, 512), bf16), ((SLOTS, 512), bf16),
            ((D, 512), bf16),
        ],
        [pos, x_slots, cot_slots, e_a, e_b, e_c, e_d],
        scratch=[pltpu.VMEM((D, 512), bf16), pltpu.VMEM((D, 512), bf16)],
        grid=(5,),
        in_specs=[by_row(EXT), by_row(D), whole, whole, whole, whole],
        out_specs=[by_row(EXT), by_row(512), by_row(512), by_row(512), pl.BlockSpec((D, 512), lambda i: (0, 0))],
        flops=8_000_000_000,
    )
    dx_back = lax.all_to_all(dx, PLANE, 0, 0, tiled=True)

    full = pl.BlockSpec((SLOTS, 512), lambda i: (0, 0))
    by_col = pl.BlockSpec((SLOTS, 256), lambda i: (0, i))
    pieces = pl.BlockSpec((8, 16, 1536), lambda i: (i, 0, 0))
    y, e_mine, e_sent = call(
        expert_grad_kernel,
        [((SLOTS, D), bf16), ((32, 16, 1536), bf16), ((32, 16, 1536), bf16)],
        [pos, x_slots, cot_slots, gate_g, up_g, scaled, w_down],
        scratch=[pltpu.VMEM((256, 512), bf16)],
        grid=(4,),
        in_specs=[by_col, by_col, full, full, full, pl.BlockSpec((256, 512), lambda i: (i, 0))],
        out_specs=[by_col, pieces, pieces],
        flops=5_400_000_000,
    )
    y_back = lax.all_to_all(y, PLANE, 0, 0, tiled=True)

    (comb,) = call(combine_kernel, [((SEQ, EXT), bf16)], [pos, tab, dx_back], flops=700_000_000)
    comb_oth = swap(comb, "yh")
    mg_own, part_own, part_sent, a_mine, a_sent = call(
        back_kernel,
        [
            ((HALF, D), f32), ((HALF, D), f32), ((HALF, D), bf16), ((32, 16, PACK), bf16), ((32, 16, PACK), bf16),
        ],
        [pos, comb, comb_oth, middle, moe_in, gates, aux, grad, rows, attn_in, w, q, k, v, ctx, lse, cos, sin],
        scratch=[
            pltpu.VMEM((SEQ, D), f32), pltpu.VMEM((SEQ, D), f32), pltpu.VMEM((SEQ, 512), bf16),
            pltpu.VMEM((SEQ, D), bf16), pltpu.VMEM((SEQ, D), f32), pltpu.VMEM((D, PACK), bf16),
        ],
        flops=4_000_000_000,
    )

    e_sum = (e_mine.astype(f32) + swap(e_sent, "c").astype(f32)).astype(bf16).reshape(2, 16, 16, 1536)
    e_keep = lax.dynamic_index_in_dim(e_sum, late, 0, keepdims=False)
    e_got = swap(lax.dynamic_index_in_dim(e_sum, 1 - late, 0, keepdims=False), "yl")
    e_sum = (e_keep.astype(f32) + e_got.astype(f32)).astype(bf16).reshape(16, 16, 3, 2, 256)
    e_sum = jnp.stack([e_sum[:, :, :, 0], swap(e_sum[:, :, :, 1], "yh")], axis=1)
    e_sum = lax.all_to_all(e_sum, PLANE, 0, 0, tiled=True)
    e_sum = e_sum.transpose(3, 2, 1, 0, 4).astype(f32)
    e_sum = jnp.where(half == 0, e_sum, e_sum[:, :, ::-1]).reshape(3, 16, EXPERTS, 256)

    out_own, out_sent = call(
        finish_kernel,
        [((HALF, D), f32), ((HALF, D), bf16)],
        [pos, tab, y_back, middle],
        scratch=[pltpu.VMEM((SEQ, D), f32)],
        flops=700_000_000,
    )
    output = (out_own + swap(out_sent, "yh").astype(f32)).astype(bf16)

    part_oth = swap(part_sent, "yh")
    a_sum = (a_mine.astype(f32) + swap(a_sent, "c").astype(f32)).astype(bf16)
    a_sum = lax.all_to_all(a_sum, CHIPS, 0, 0, tiled=True)
    a_sum = jnp.sum(a_sum.astype(f32), axis=0)
    gain_one = a_sum[:, 1568]
    gain_one = gain_one + swap(gain_one, "yh")
    (input_grad,) = call(
        input_kernel, [((HALF, D), bf16)], [pos, tokens, aux, mg_own, part_own, part_oth]
    )
    return (
        output,
        input_grad,
        gain_one,
        a_sum[:, :512],
        a_sum[:, 512:768],
        a_sum[:, 768:1024],
        a_sum[:, 1024:1536],
        a_sum[:, 1569],
        a_sum[:, 1536:1568],
        e_sum[0],
        e_sum[1],
        e_sum[2],
    )


def solution(mesh):
    fine = Mesh(mesh.devices.reshape(2, 4, 4, 2, 2), ("yl", "x", "z", "c", "yh"))
    dp, every = ("yl", "x", "z", "c"), ("yl", "x", "z", "c", "yh")
    in_specs = (
        P(every, None),
        P(dp, None),
        P(every, None),
        P(dp),
        P(dp, "yh"),
        P(dp, "yh"),
        P(dp, "yh"),
        P(dp, "yh"),
        P(dp),
        P(dp, None),
        P(dp, None, "yh"),
        P(dp, None, "yh"),
        P(dp, None, "yh"),
    )
    out_specs = (
        P(every, None),
        P(every, None),
        P(dp),
        P(dp, "yh"),
        P(dp, "yh"),
        P(dp, "yh"),
        P(dp, "yh"),
        P(dp),
        P(dp, None),
        P(dp, None, "yh"),
        P(dp, None, "yh"),
        P(dp, None, "yh"),
    )
    return jax.shard_map(body, mesh=fine, in_specs=in_specs, out_specs=out_specs, check_vma=False)
```

time: 3430 us -> 332 us (0.10)
  waiting for transfers between devices: 2460 us -> 158 us
  blocking collectives: 554 us -> 0 us
  local copies, waits for them, and re-layouts: 199 us -> 26.7 us
  matrix products: 153 us -> 0 us
  starting transfers between devices: 1.12 us -> 70.8 us
  Pallas kernels: 0 us -> 61.3 us
    reduce_scatter x8 -> x0, waiting for transfers between devices: 2130 us -> none  [the longest x1 340 us: body(): lax.psum_scatter(grad_expert_gate, 'dp', scatter_dimension=0, tiled=True)]
    unnamed x2 -> x0, blocking collectives: 284 us -> none
    all_gather x5 -> x0, blocking collectives: 270 us -> none  [the longest x1 85.2 us: body(): lax.all_gather(value_weight, 'dp', axis=0, tiled=True)]
    all_gather x5 -> x0, waiting for transfers between devices: 240 us -> none  [the longest x1 113 us: body(): pieces = (lax.all_gather(expert_down, 'dp', axis=0, tiled=True),)]
    dot_general x30 -> x0, matrix products: 153 us -> none  [the longest x1 17.3 us: body(): jnp.einsum('ecr,ecf->ref', slot_grad, hidden_e, preferred_element_type=jn...]
    transpose x3 -> x0, local copies, waits for them, and re-layouts: 103 us -> none  [the longest x1 34.3 us: body(): jnp.einsum('ecr,ecf->ref', slot_grad, hidden_e, preferred_element_type=jn...]
    ppermute x0 -> x16, waiting for transfers between devices: none -> 90.1 us  [swap(): return lax.ppermute(value, axis, [(0, 1), (1, 0)])]
    psum x3 -> x0, waiting for transfers between devices: 88 us -> none  [the longest x1 53.7 us: body(): lax.psum(moe_part.astype(jnp.bfloat16), 'tensor').astype(jnp.float32)]
  transfers between devices with their start and end apart: 16 -> 24, of which waited for: 12 -> 17; matrix products, arithmetic and copies ran while one was open for 8% -> 8% of each run, Pallas kernels for 0% -> 15%
where the time goes in v1:
time: 332 us; the launch traced here: 330 us
  waiting for transfers between devices  158 us (48%)
  starting transfers between devices  70.8 us (21%)
  Pallas kernels  61.3 us (18%)
  local copies, waits for them, and re-layouts  26.7 us (8%)
  other arithmetic  11.7 us (4%)
    ppermute x16, waiting for transfers between devices, swap(): return lax.ppermute(value, axis, [(0, 1), (1, 0)])  90.1 us
    pallas_call x7, Pallas kernels, call(): pl.pallas_call(kernel, out_shape=out_shape, in_specs=in_specs, out_specs=...  38.7 us
    all_to_all x1, waiting for transfers between devices, body(): dx_back = lax.all_to_all(dx, PLANE, 0, 0, tiled=True)  28.7 us
    pallas_call x2, Pallas kernels, call(): pl.pallas_call(kernel, grid=grid, out_shape=out_shape, in_specs=[smem] +...  22.7 us
    ppermute x16, starting transfers between devices, swap(): return lax.ppermute(value, axis, [(0, 1), (1, 0)])  22.6 us
    all_to_all x1, waiting for transfers between devices, body(): w_mine = lax.all_to_all(packed, CHIPS, 0, 0, tiled=True)  18.9 us
    all_to_all x1, waiting for transfers between devices, body(): e_sum = lax.all_to_all(e_sum, PLANE, 0, 0, tiled=True)  11.1 us
    all_to_all x1, starting transfers between devices, body(): w_mine = lax.all_to_all(packed, CHIPS, 0, 0, tiled=True)  9.51 us
  transfers between devices with their start and end apart: 24, of which 17 were waited for; matrix products, arithmetic and copies ran while one was open for 8% of the time, Pallas kernels for 15%

profile of v1, /device:TPU:0, one launch (start us, length us, event | category | flops | bytes accessed | tf_op | source)
XLA Modules:
  0.0 329.6 jit_solution(9253124764948473594)
XLA Ops:
  4.4 9.5 %all-to-all-start = ((bf16[32,16,1664]{2,1,0:T(8,128)(2,1)}), bf16[32,16,1664]{2,1,0:T(8,128)(2,1)}, u32[]{:S(2)}, u32[]{:S(2)}) async-start(bf16[32,16,1664]{2,1,0:T(8,128)(2,1)} %broadcast_in_dim.20), calls=%async_computation | async-start | bytes 3407872 | tf_op jit(solution)/shard_map/all_to_all | solution.py:375
  15.6 1.8 maximum_bitcast_fusion
  17.4 1.7 reshape.73
  19.1 18.9 %all-to-all-done.w_mine = bf16[32,16,1664]{2,1,0:T(8,128)(2,1)} async-done(((bf16[32,16,1664]{2,1,0:T(8,128)(2,1)}), bf16[32,16,1664]{2,1,0:T(8,128)(2,1)}, u32[]{:S(2)}, u32[]{:S(2)}) %all-to-all-start) | async-done | bytes 1703968 | tf_op jit(solution)/shard_map/all_to_all | solution.py:375
  38.0 4.4 %all-to-all-start.3 = ((bf16[16,2,16,768]{3,2,1,0:T(8,128)(2,1)}), bf16[16,2,16,768]{3,2,1,0:T(8,128)(2,1)S(1)}, u32[]{:S(2)}, u32[]{:S(2)}) async-start(bf16[16,2,16,768]{3,2,1,0:T(8,128)(2,1)} %reshape.73), calls=%async_computation.3 | async-start | bytes 1572864 | tf_op jit(solution)/shard_map/all_to_all | solution.py:391
  42.4 3.0 collective-permute-start
  46.7 5.2 %collective-permute-done.cot_oth = bf16[128,1024]{1,0:T(8,128)(2,1)S(1)} collective-permute-done((bf16[128,1024]{1,0:T(8,128)(2,1)S(1)}, bf16[128,1024]{1,0:T(8,128)(2,1)S(1)}, u32[]{:S(2)}, u32[]{:S(2)}) %collective-permute-start) | collective-permute-done | bytes 262176 | tf_op jit(solution)/shard_map/ppermute | solution.py:344
  52.6 4.2 %shard_map.220 = (bf16[1280,256]{1,0:T(8,128)(2,1)}, f32[256,128]{1,0:T(8,128)}, bf16[256,1024]{1,0:T(8,128)(2,1)}, bf16[1280,1024]{1,0:T(8,128)(2,1)}) custom-call(s32[4]{0:T(128)} %pad_add_fusion.pos, s32[256,8]{1,0:T(8,128)} %copy.68.routes, bf16[128,1024]{1,0:T(8,128)(2,1)} %cot_own.1, bf16[128,1024]{1,0:T(8,128)(2,1)} %copy-done.17), custom_call_target="tpu_custom_call" | custom-call | flops 700000000 | bytes 4464656 | tf_op jit(solution)/shard_map/pallas_call | solution.py:61
  57.0 6.7 %all-to-all-start.2 = ((bf16[16,80,1024]{2,1,0:T(8,128)(2,1)}), bf16[16,80,1024]{2,1,0:T(8,128)(2,1)S(1)}, u32[]{:S(2)}, u32[]{:S(2)}) async-start(bf16[16,80,1024]{2,1,0:T(8,128)(2,1)} %bitcast.52), calls=%async_computation.2 | async-start | bytes 5242880 | tf_op jit(solution)/shard_map/all_to_all | solution.py:387
  63.8 3.0 collective-permute-start.1
  67.7 1.8 copy.71.cos
  70.2 1.8 copy.72.sin
  72.1 6.8 %shard_map.221 = (bf16[256,1024]{1,0:T(8,128)(2,1)}, bf16[1024,1664]{1,0:T(8,128)(2,1)}, f32[128,1024]{1,0:T(8,128)}, bf16[256,1024]{1,0:T(8,128)(2,1)}, bf16[25...) custom-call(s32[4]{0:T(128)} %pad_add_fusion.pos, ...), custom_call_target="tpu_custom_call" | custom-call | flops 2000000000 | bytes 12058640 | tf_op jit(solution)/shard_map/pallas_call | solution.py:61
  79.0 2.9 collective-permute-start.3
  81.9 10.5 %collective-permute-done.3.part_oth = bf16[256,1024]{1,0:T(8,128)(2,1)S(1)} collective-permute-done((bf16[256,1024]{1,0:T(8,128)(2,1)}, bf16[256,1024]{1,0:T(8,128)(2,1)S(1)}, u32[]{:S(2)}, u32[]{:S(2)}) %collective-permute-start.3) | collective-permute-done | bytes 524320 | tf_op jit(solution)/shard_map/ppermute | solution.py:344
  93.2 4.8 %shard_map.222 = (f32[256,1024]{1,0:T(8,128)}, bf16[256,1024]{1,0:T(8,128)(2,1)}, f32[256,128]{1,0:T(8,128)}, bf16[1280,1152]{1,0:T(8,128)(2,1)}) custom-call(s32[4]{0:T(128)} %pad_add_fusion.pos, bf16[256,1024]{1,0:T(8,128)(2,1)} %get-tuple-element.46.rows, bf16[256,1024]{1,0:T(8,128)(2,1)} %get-tuple-element.47.part_own, bf16[256,1024]{1,0:T(8,128)(2,1)} %copy-done.14, ...), custom_call_target="tpu_custom_call" | custom-call | flops 800000000 | bytes 7536656 | tf_op jit(solution)/shard_map/pallas_call | solution.py:61
  99.7 6.7 %all-to-all-start.1 = ((bf16[16,80,1152]{2,1,0:T(8,128)(2,1)}), bf16[16,80,1152]{2,1,0:T(8,128)(2,1)}, u32[]{:S(2)}, u32[]{:S(2)}) async-start(bf16[16,80,1152]{2,1,0:T(8,128)(2,1)} %bitcast.47), calls=%async_computation.1 | async-start | bytes 5898240 | tf_op jit(solution)/shard_map/all_to_all | solution.py:415
  106.5 2.1 collective-permute-start.4
  108.6 9.0 %collective-permute-done.4 = bf16[16,16,768]{2,1,0:T(8,128)(2,1)S(1)} collective-permute-done((bf16[16,16,768]{2,1,0:T(8,128)(2,1)S(1)}, bf16[16,16,768]{2,1,0:T(8,128)(2,1)S(1)}, u32[]{:S(2)}, u32[]{:S(2)}) %collective-permute-start.4) | collective-permute-done | bytes 393248 | tf_op jit(solution)/shard_map/ppermute | solution.py:344
  117.9 13.6 %collective-permute-done.5.w_b = bf16[2,16,16,768]{3,2,1,0:T(8,128)(2,1)S(1)} collective-permute-done((bf16[2,16,16,768]{3,2,1,0:T(8,128)(2,1)S(1)}, bf16[2,16,16,768]{3,2,1,0:T(8,128)(2,1)S(1)}, u32[]{:S(2)}, u32[]{:S(2)}) %collective-permute-start.5) | collective-permute-done | bytes 786464 | tf_op jit(solution)/shard_map/ppermute | solution.py:344
  131.5 2.3 collective-permute-done.7.w_d
  133.8 8.8 %all-to-all-done.1 = bf16[16,80,1152]{2,1,0:T(8,128)(2,1)} async-done(((bf16[16,80,1152]{2,1,0:T(8,128)(2,1)}), bf16[16,80,1152]{2,1,0:T(8,128)(2,1)}, u32[]{:S(2)}, u32[]{:S(2)}) %all-to-all-start.1) | async-done | bytes 2949152 | tf_op jit(solution)/shard_map/all_to_all | solution.py:415
  142.6 12.6 %shard_map.223 = (bf16[1280,1152]{1,0:T(8,128)(2,1)}, bf16[1280,512]{1,0:T(8,128)(2,1)}, bf16[1280,512]{1,0:T(8,128)(2,1)}, bf16[1280,512]{1,0:T(8,128)(2,1)}, bf16[1024,512]{1,0:T(8,128)(2,1)}) custom-call(s32[4]{0:T(128)} %pad_add_fusion.pos, bf16[1280,1152]{1,0:T(8,128)(2,1)} %bitcast.9.x, bf16[1280,1024]{1,0:T(8,128)(2,1)} %bitcast.49, ...), custom_call_target="tpu_custom_call" | custom-call | flops 8000000000 | bytes 16646160 | tf_op jit(solution)/shard_map/pallas_call | solution.py:70
  155.2 5.1 %all-to-all-start.5 = ((bf16[16,80,1152]{2,1,0:T(8,128)(2,1)}), bf16[16,80,1152]{2,1,0:T(8,128)(2,1)S(1)}, u32[]{:S(2)}, u32[]{:S(2)}) async-start(bf16[16,80,1152]{2,1,0:T(8,128)(2,1)} %bitcast.48), calls=%async_computation.5 | async-start | bytes 5898240 | tf_op jit(solution)/shard_map/all_to_all | solution.py:432
  160.3 10.1 %shard_map.224 = (bf16[1280,1024]{1,0:T(8,128)(2,1)}, bf16[32,16,1536]{2,1,0:T(8,128)(2,1)}, bf16[32,16,1536]{2,1,0:T(8,128)(2,1)}) custom-call(s32[4]{0:T(128)} %pad_add_fusion.pos, bf16[1280,1152]{1,0:T(8,128)(2,1)} %bitcast.9.x, bf16[1280,1024]{1,0:T(8,128)(2,1)} %bitcast.50, bf16[1280,512]{1,0:T(8,128)(2,1)} %get-tuple-element.52.gate_g, ...), custom_call_target="tpu_custom_call" | custom-call | flops 5400000000 | bytes 16318480 | tf_op jit(solution)/shard_map/pallas_call | solution.py:70
  170.4 28.7 %all-to-all-done.5 = bf16[16,80,1152]{2,1,0:T(8,128)(2,1)S(1)} async-done(((bf16[16,80,1152]{2,1,0:T(8,128)(2,1)}), bf16[16,80,1152]{2,1,0:T(8,128)(2,1)S(1)}, u32[]{:S(2)}, u32[]{:S(2)}) %all-to-all-start.5) | async-done | bytes 2949152 | tf_op jit(solution)/shard_map/all_to_all | solution.py:432
  199.1 1.6 copy-done
  200.7 4.6 %all-to-all-start.4 = ((bf16[16,80,1024]{2,1,0:T(8,128)(2,1)}), bf16[16,80,1024]{2,1,0:T(8,128)(2,1)}, u32[]{:S(2)}, u32[]{:S(2)}) async-start(bf16[16,80,1024]{2,1,0:T(8,128)(2,1)} %bitcast.51), calls=%async_computation.4 | async-start | bytes 5242880 | tf_op jit(solution)/shard_map/all_to_all | solution.py:447
  205.3 4.1 %shard_map.226.comb_own = bf16[256,1152]{1,0:T(8,128)(2,1)} custom-call(s32[4]{0:T(128)} %pad_add_fusion.pos, bf16[1280,256]{1,0:T(8,128)(2,1)} %get-tuple-element.45.tab, bf16[1280,1152]{1,0:T(8,128)(2,1)} %bitcast.44), custom_call_target="tpu_custom_call" | custom-call | flops 700000000 | bytes 4194320 | tf_op jit(solution)/shard_map/pallas_call | solution.py:61
  209.4 3.2 collective-permute-start.9
  212.6 2.0 add_convert_fusion.1
  214.9 12.4 %collective-permute-done.9.comb_oth = bf16[256,1152]{1,0:T(8,128)(2,1)S(1)} collective-permute-done((bf16[256,1152]{1,0:T(8,128)(2,1)}, bf16[256,1152]{1,0:T(8,128)(2,1)S(1)}, u32[]{:S(2)}, u32[]{:S(2)}) %collective-permute-start.9) | collective-permute-done | bytes 589856 | tf_op jit(solution)/shard_map/ppermute | solution.py:344
  228.2 12.3 %shard_map.227 = (f32[128,1024]{1,0:T(8,128)}, f32[128,1024]{1,0:T(8,128)}, bf16[128,1024]{1,0:T(8,128)(2,1)}, bf16[32,16,1664]{2,1,0:T(8,128)(2,1)}, bf16[32,16,1664]{2,1,0:T(8,128)(2,1)}) custom-call(s32[4]{0:T(128)} %pad_add_fusion.pos, bf16[256,1152]{1,0:T(8,128)(2,1)} %shard_map.226.comb_own, bf16[256,1152]{1,0:T(8,128)(2,1)} %copy-done.13, ...), custom_call_target="tpu_custom_call" | custom-call | flops 4000000000 | bytes 15728656 | tf_op jit(solution)/shard_map/pallas_call | solution.py:61
  240.9 1.7 fusion.5
  242.7 3.3 collective-permute-start.15
  246.1 9.7 %collective-permute-done.15 = bf16[16,16,3,256]{3,1,2,0:T(8,128)(2,1)S(1)} collective-permute-done((bf16[16,16,3,256]{3,1,2,0:T(8,128)(2,1)S(1)}, bf16[16,16,3,256]{3,1,2,0:T(8,128)(2,1)S(1)}, u32[]{:S(2)}, u32[]{:S(2)}) %collective-permute-start.15) | collective-permute-done | bytes 393248 | tf_op jit(solution)/shard_map/ppermute | solution.py:344
  255.9 1.7 copy.80
  257.6 7.2 %all-to-all-start.7 = ((bf16[16,2,16,3,256]{4,1,2,3,0:T(2,128)(2,1)}), bf16[16,2,16,3,256]{4,1,2,3,0:T(2,128)(2,1)S(1)}, u32[]{:S(2)}, u32[]{:S(2)}) async-start(bf16[16,2,16,3,256]{4,1,2,3,0:T(2,128)(2,1)} %copy.80), calls=%async_computation.7 | async-start | bytes 1572864 | tf_op jit(solution)/shard_map/all_to_all | solution.py:469
  264.8 3.1 add_convert_fusion
  267.9 11.1 %all-to-all-done.7 = bf16[16,2,16,3,256]{4,1,2,3,0:T(2,128)(2,1)S(1)} async-done(((bf16[16,2,16,3,256]{4,1,2,3,0:T(2,128)(2,1)}), bf16[16,2,16,3,256]{4,1,2,3,0:T(2,128)(2,1)S(1)}, u32[]{:S(2)}, u32[]{:S(2)}) %all-to-all-start.7) | async-done | bytes 786464 | tf_op jit(solution)/shard_map/all_to_all | solution.py:469
  278.9 4.0 %all-to-all-start.6 = ((bf16[32,16,1664]{2,1,0:T(8,128)(2,1)}), bf16[32,16,1664]{2,1,0:T(8,128)(2,1)S(1)}, u32[]{:S(2)}, u32[]{:S(2)}) async-start(bf16[32,16,1664]{2,1,0:T(8,128)(2,1)} %add_convert_fusion), calls=%async_computation.6 | async-start | bytes 3407872 | tf_op jit(solution)/shard_map/all_to_all | solution.py:484
  282.9 4.1 %shard_map.225 = (f32[128,1024]{1,0:T(8,128)}, bf16[128,1024]{1,0:T(8,128)(2,1)}) custom-call(s32[4]{0:T(128)} %pad_add_fusion.pos, bf16[1280,256]{1,0:T(8,128)(2,1)} %get-tuple-element.45.tab, bf16[1280,1024]{1,0:T(8,128)(2,1)} %bitcast.20.got, f32[256,1024]{1,0:T(8,128)} %get-tuple-element.57.middle), custom_call_target="tpu_custom_call" | custom-call | flops 700000000 | bytes 5111824 | tf_op jit(solution)/shard_map/pallas_call | solution.py:61
  287.0 3.2 collective-permute-start.8
  290.2 18.8 %collective-permute-done.8 = bf16[128,1024]{1,0:T(8,128)(2,1)S(1)} collective-permute-done((bf16[128,1024]{1,0:T(8,128)(2,1)}, bf16[128,1024]{1,0:T(8,128)(2,1)S(1)}, u32[]{:S(2)}, u32[]{:S(2)}) %collective-permute-start.8) | collective-permute-done | bytes 262176 | tf_op jit(solution)/shard_map/ppermute | solution.py:344
  309.0 1.8 add_convert_fusion.2
  313.4 5.2 %collective-permute-done.10.part_oth = bf16[128,1024]{1,0:T(8,128)(2,1)S(1)} collective-permute-done((bf16[128,1024]{1,0:T(8,128)(2,1)S(1)}, bf16[128,1024]{1,0:T(8,128)(2,1)S(1)}, u32[]{:S(2)}, u32[]{:S(2)}) %collective-permute-start.10) | collective-permute-done | bytes 262176 | tf_op jit(solution)/shard_map/ppermute | solution.py:344
  319.4 2.5 shard_map.228
  325.8 3.3 collective-permute-done.12
  (86 shorter events, 22.0 us)
Async XLA Ops:
  4.4 9.5 %copy-start.5 = (bf16[16,32,256]{2,1,0:T(8,128)(2,1)S(1)}, bf16[16,32,256]{2,1,0:T(8,128)(2,1)}, u32[]{:S(2)}) copy-start(bf16[16,32,256]{2,1,0:T(8,128)(2,1)} %param.23) | copy-start | bytes 786436
  4.4 10.1 %copy-start.6 = (bf16[16,32,256]{2,1,0:T(8,128)(2,1)S(1)}, bf16[16,32,256]{2,1,0:T(8,128)(2,1)}, u32[]{:S(2)}) copy-start(bf16[16,32,256]{2,1,0:T(8,128)(2,1)} %param.24) | copy-start | bytes 786436
  4.4 10.7 %copy-start.7 = (bf16[16,32,256]{2,1,0:T(8,128)(2,1)S(1)}, bf16[16,32,256]{2,1,0:T(8,128)(2,1)}, u32[]{:S(2)}) copy-start(bf16[16,32,256]{2,1,0:T(8,128)(2,1)} %param.25) | copy-start | bytes 786436
  4.4 33.6 %all-to-all-start = ((bf16[32,16,1664]{2,1,0:T(8,128)(2,1)}), bf16[32,16,1664]{2,1,0:T(8,128)(2,1)}, u32[]{:S(2)}, u32[]{:S(2)}) async-start(bf16[32,16,1664]{2,1,0:T(8,128)(2,1)} %broadcast_in_dim.20), calls=%async_computation | async-start | bytes 3407872 | tf_op jit(solution)/shard_map/all_to_all | solution.py:375
  17.4 25.0 %copy-start.15 = (bf16[128,1024]{1,0:T(8,128)(2,1)S(1)}, bf16[128,1024]{1,0:T(8,128)(2,1)}, u32[]{:S(2)}) copy-start(bf16[128,1024]{1,0:T(8,128)(2,1)} %cot_own.1) | copy-start | bytes 786436
  17.4 28.0 %copy-start.9 = (s32[256,8]{0,1:T(8,128)S(1)}, s32[256,8]{0,1:T(8,128)}, u32[]{:S(2)}) copy-start(s32[256,8]{0,1:T(8,128)} %param.14) | copy-start | bytes 24580
  38.0 19.0 %all-to-all-start.3 = ((bf16[16,2,16,768]{3,2,1,0:T(8,128)(2,1)}), bf16[16,2,16,768]{3,2,1,0:T(8,128)(2,1)S(1)}, u32[]{:S(2)}, u32[]{:S(2)}) async-start(bf16[16,2,16,768]{3,2,1,0:T(8,128)(2,1)} %reshape.73), calls=%async_computation.3 | async-start | bytes 1572864 | tf_op jit(solution)/shard_map/all_to_all | solution.py:391
  42.4 9.5 %collective-permute-start = (bf16[128,1024]{1,0:T(8,128)(2,1)S(1)}, bf16[128,1024]{1,0:T(8,128)(2,1)S(1)}, u32[]{:S(2)}, u32[]{:S(2)}) collective-permute-start(bf16[128,1024]{1,0:T(8,128)(2,1)S(1)} %copy-done.15), channel_id=1, source_target_pairs={{0,1},{1,0},{2,3},{3,2},{4,5},{5,4},{6,7},{7,6},{8,9},{9,8},{10,11... | collective-permute-start | bytes 786440 | tf_op jit(solution)/shard_map/ppermute | solution.py:344
  46.7 25.4 %collective-permute-start.2 = (bf16[32,16,1664]{2,1,0:T(8,128)(2,1)}, bf16[32,16,1664]{2,1,0:T(8,128)(2,1)}, u32[]{:S(2)}, u32[]{:S(2)}) collective-permute-start(bf16[32,16,1664]{2,1,0:T(8,128)(2,1)} %all-to-all-done.w_mine), channel_id=1, source_target_pairs={{0,2},{2,0},{1,3},{3,1},{4,6},{6,4},{5,7},{7,5},{8,10},{10,8},{9,1... | collective-permute-start | bytes 5111816 | tf_op jit(solution)/shard_map/ppermute | solution.py:344
  51.9 0.7 copy-start.17
  57.0 41.2 %all-to-all-start.2 = ((bf16[16,80,1024]{2,1,0:T(8,128)(2,1)}), bf16[16,80,1024]{2,1,0:T(8,128)(2,1)S(1)}, u32[]{:S(2)}, u32[]{:S(2)}) async-start(bf16[16,80,1024]{2,1,0:T(8,128)(2,1)} %bitcast.52), calls=%async_computation.2 | async-start | bytes 5242880 | tf_op jit(solution)/shard_map/all_to_all | solution.py:387
  63.8 8.4 %collective-permute-start.1 = (bf16[128,1024]{1,0:T(8,128)(2,1)}, bf16[128,1024]{1,0:T(8,128)(2,1)}, u32[]{:S(2)}, u32[]{:S(2)}) collective-permute-start(bf16[128,1024]{1,0:T(8,128)(2,1)} %tok.1), channel_id=1, source_target_pairs={{0,1},{1,0},{2,3},{3,2},{4,5},{5,4},{6,7},{7,6},{8,9},{9,8},{10,11... | collective-permute-start | bytes 786440 | tf_op jit(solution)/shard_map/ppermute | solution.py:344
  79.0 13.4 %collective-permute-start.3 = (bf16[256,1024]{1,0:T(8,128)(2,1)}, bf16[256,1024]{1,0:T(8,128)(2,1)S(1)}, u32[]{:S(2)}, u32[]{:S(2)}) collective-permute-start(bf16[256,1024]{1,0:T(8,128)(2,1)} %get-tuple-element.47.part_own), channel_id=1, source_target_pairs={{0,1},{1,0},{2,3},{3,2},{4,5},{5,4},{6,7},{7,6},{8,9},{9,8},{10,11... | collective-permute-start | bytes 1572872 | tf_op jit(solution)/shard_map/ppermute | solution.py:344
  92.4 0.8 copy-start.14
  98.2 1.5 copy-start.1
  99.7 42.9 %all-to-all-start.1 = ((bf16[16,80,1152]{2,1,0:T(8,128)(2,1)}), bf16[16,80,1152]{2,1,0:T(8,128)(2,1)}, u32[]{:S(2)}, u32[]{:S(2)}) async-start(bf16[16,80,1152]{2,1,0:T(8,128)(2,1)} %bitcast.47), calls=%async_computation.1 | async-start | bytes 5898240 | tf_op jit(solution)/shard_map/all_to_all | solution.py:415
  106.5 11.2 %collective-permute-start.4 = (bf16[16,16,768]{2,1,0:T(8,128)(2,1)S(1)}, bf16[16,16,768]{2,1,0:T(8,128)(2,1)S(1)}, u32[]{:S(2)}, u32[]{:S(2)}) collective-permute-start(bf16[16,16,768]{2,1,0:T(8,128)(2,1)S(1)} %get-tuple-element.86), channel_id=1, source_target_pairs={{0,1},{1,0},{2,3},{3,2},{4,5},{5,4},{6,7},{7,6},{8,9},{9,8},{10,11... | collective-permute-start | bytes 1179656 | tf_op jit(solution)/shard_map/ppermute | solution.py:344
  117.7 24.8 %copy-start.4 = (bf16[2,16,16,768]{3,2,1,0:T(8,128)(2,1)}, bf16[2,16,16,768]{3,2,1,0:T(8,128)(2,1)S(1)}, u32[]{:S(2)}) copy-start(bf16[2,16,16,768]{3,2,1,0:T(8,128)(2,1)S(1)} %pad_maximum_fusion.w_a) | copy-start | bytes 2359300
  117.7 13.7 %collective-permute-start.5 = (bf16[2,16,16,768]{3,2,1,0:T(8,128)(2,1)S(1)}, bf16[2,16,16,768]{3,2,1,0:T(8,128)(2,1)S(1)}, u32[]{:S(2)}, u32[]{:S(2)}) collective-permute-start(bf16[2,16,16,768]{3,2,1,0:T(8,128)(2,1)S(1)} %pad_maximum_fusion.w_a), channel_id=1, source_target_pairs={{0,64},{64,0},{1,65},{65,1},{2,66},{66,2},{3,67},{67,3},{4,68},{68... | collective-permute-start | bytes 2359304 | tf_op jit(solution)/shard_map/ppermute | solution.py:344
  117.8 13.7 %collective-permute-start.6 = (bf16[2,16,16,768]{3,2,1,0:T(8,128)(2,1)S(1)}, bf16[2,16,16,768]{3,2,1,0:T(8,128)(2,1)S(1)}, u32[]{:S(2)}, u32[]{:S(2)}) collective-permute-start(bf16[2,16,16,768]{3,2,1,0:T(8,128)(2,1)S(1)} %pad_maximum_fusion.w_a), channel_id=1, source_target_pairs={{0,2},{2,0},{1,3},{3,1},{4,6},{6,4},{5,7},{7,5},{8,10},{10,8},{9,1... | collective-permute-start | bytes 2359304 | tf_op jit(solution)/shard_map/ppermute | solution.py:344
  131.5 11.1 %copy-start.10 = (bf16[2,16,16,768]{3,2,1,0:T(8,128)(2,1)}, bf16[2,16,16,768]{3,2,1,0:T(8,128)(2,1)S(1)}, u32[]{:S(2)}) copy-start(bf16[2,16,16,768]{3,2,1,0:T(8,128)(2,1)S(1)} %collective-permute-done.5.w_b) | copy-start | bytes 2359300
  131.5 2.3 collective-permute-start.7
  131.5 11.1 %copy-start.11 = (bf16[2,16,16,768]{3,2,1,0:T(8,128)(2,1)}, bf16[2,16,16,768]{3,2,1,0:T(8,128)(2,1)S(1)}, u32[]{:S(2)}) copy-start(bf16[2,16,16,768]{3,2,1,0:T(8,128)(2,1)S(1)} %collective-permute-done.6.w_c) | copy-start | bytes 2359300
  133.8 8.8 %copy-start.12 = (bf16[2,16,16,768]{3,2,1,0:T(8,128)(2,1)}, bf16[2,16,16,768]{3,2,1,0:T(8,128)(2,1)S(1)}, u32[]{:S(2)}) copy-start(bf16[2,16,16,768]{3,2,1,0:T(8,128)(2,1)S(1)} %collective-permute-done.7.w_d) | copy-start | bytes 2359300
  155.2 44.0 %all-to-all-start.5 = ((bf16[16,80,1152]{2,1,0:T(8,128)(2,1)}), bf16[16,80,1152]{2,1,0:T(8,128)(2,1)S(1)}, u32[]{:S(2)}, u32[]{:S(2)}) async-start(bf16[16,80,1152]{2,1,0:T(8,128)(2,1)} %bitcast.48), calls=%async_computation.5 | async-start | bytes 5898240 | tf_op jit(solution)/shard_map/all_to_all | solution.py:432
  170.4 42.2 %collective-permute-start.13 = (bf16[32,16,1536]{2,1,0:T(8,128)(2,1)}, bf16[32,16,1536]{2,1,0:T(8,128)(2,1)}, u32[]{:S(2)}, u32[]{:S(2)}) collective-permute-start(bf16[32,16,1536]{2,1,0:T(8,128)(2,1)} %get-tuple-element.77), channel_id=1, source_target_pairs={{0,2},{2,0},{1,3},{3,1},{4,6},{6,4},{5,7},{7,5},{8,10},{10,8},{9,1... | collective-permute-start | bytes 4718600 | tf_op jit(solution)/shard_map/ppermute | solution.py:344
  199.1 1.6 copy-start
  200.7 56.8 %all-to-all-start.4 = ((bf16[16,80,1024]{2,1,0:T(8,128)(2,1)}), bf16[16,80,1024]{2,1,0:T(8,128)(2,1)}, u32[]{:S(2)}, u32[]{:S(2)}) async-start(bf16[16,80,1024]{2,1,0:T(8,128)(2,1)} %bitcast.51), calls=%async_computation.4 | async-start | bytes 5242880 | tf_op jit(solution)/shard_map/all_to_all | solution.py:447
  205.3 7.3 %copy-start.3 = (bf16[32,16,1536]{2,1,0:T(8,128)(2,1)S(1)}, bf16[32,16,1536]{2,1,0:T(8,128)(2,1)}, u32[]{:S(2)}) copy-start(bf16[32,16,1536]{2,1,0:T(8,128)(2,1)} %get-tuple-element.76) | copy-start | bytes 4718596
  209.4 18.0 %collective-permute-start.9 = (bf16[256,1152]{1,0:T(8,128)(2,1)}, bf16[256,1152]{1,0:T(8,128)(2,1)S(1)}, u32[]{:S(2)}, u32[]{:S(2)}) collective-permute-start(bf16[256,1152]{1,0:T(8,128)(2,1)} %shard_map.226.comb_own), channel_id=1, source_target_pairs={{0,1},{1,0},{2,3},{3,2},{4,5},{5,4},{6,7},{7,6},{8,9},{9,8},{10,11... | collective-permute-start | bytes 1769480 | tf_op jit(solution)/shard_map/ppermute | solution.py:344
  214.6 25.9 %collective-permute-start.14 = (bf16[16,16,1536]{2,1,0:T(8,128)(2,1)S(1)}, bf16[16,16,1536]{2,1,0:T(8,128)(2,1)S(1)}, u32[]{:S(2)}, u32[]{:S(2)}) collective-permute-start(bf16[16,16,1536]{2,1,0:T(8,128)(2,1)S(1)} %dynamic-slice_bitcast_fusion), channel_id=1, source_target_pairs={{0,64},{64,0},{1,65},{65,1},{2,66},{66,2},{3,67},{67,3},{4,68},{68... | collective-permute-start | bytes 2359304 | tf_op jit(solution)/shard_map/ppermute | solution.py:344
  227.4 0.9 copy-start.13
  240.5 24.3 %collective-permute-start.11 = (bf16[32,16,1664]{2,1,0:T(8,128)(2,1)}, bf16[32,16,1664]{2,1,0:T(8,128)(2,1)}, u32[]{:S(2)}, u32[]{:S(2)}) collective-permute-start(bf16[32,16,1664]{2,1,0:T(8,128)(2,1)} %get-tuple-element.75), channel_id=1, source_target_pairs={{0,2},{2,0},{1,3},{3,1},{4,6},{6,4},{5,7},{7,5},{8,10},{10,8},{9,1... | collective-permute-start | bytes 5111816 | tf_op jit(solution)/shard_map/ppermute | solution.py:344
  242.7 13.1 %collective-permute-start.15 = (bf16[16,16,3,256]{3,1,2,0:T(8,128)(2,1)S(1)}, bf16[16,16,3,256]{3,1,2,0:T(8,128)(2,1)S(1)}, u32[]{:S(2)}, u32[]{:S(2)}) collective-permute-start(bf16[16,16,3,256]{3,1,2,0:T(8,128)(2,1)S(1)} %bitcast.59), channel_id=1, source_target_pairs={{0,1},{1,0},{2,3},{3,2},{4,5},{5,4},{6,7},{7,6},{8,9},{9,8},{10,11... | collective-permute-start | bytes 1179656 | tf_op jit(solution)/shard_map/ppermute | solution.py:344
  255.9 8.9 %copy-start.2 = (bf16[32,16,1664]{2,1,0:T(8,128)(2,1)S(1)}, bf16[32,16,1664]{2,1,0:T(8,128)(2,1)}, u32[]{:S(2)}) copy-start(bf16[32,16,1664]{2,1,0:T(8,128)(2,1)} %get-tuple-element.74) | copy-start | bytes 5111812
  257.6 21.4 %all-to-all-start.7 = ((bf16[16,2,16,3,256]{4,1,2,3,0:T(2,128)(2,1)}), bf16[16,2,16,3,256]{4,1,2,3,0:T(2,128)(2,1)S(1)}, u32[]{:S(2)}, u32[]{:S(2)}) async-start(bf16[16,2,16,3,256]{4,1,2,3,0:T(2,128)(2,1)} %copy.80), calls=%async_computation.7 | async-start | bytes 1572864 | tf_op jit(solution)/shard_map/all_to_all | solution.py:469
  278.9 43.0 %all-to-all-start.6 = ((bf16[32,16,1664]{2,1,0:T(8,128)(2,1)}), bf16[32,16,1664]{2,1,0:T(8,128)(2,1)S(1)}, u32[]{:S(2)}, u32[]{:S(2)}) async-start(bf16[32,16,1664]{2,1,0:T(8,128)(2,1)} %add_convert_fusion), calls=%async_computation.6 | async-start | bytes 3407872 | tf_op jit(solution)/shard_map/all_to_all | solution.py:484
  282.9 27.9 %copy-start.16 = (bf16[128,1024]{1,0:T(8,128)(2,1)S(1)}, bf16[128,1024]{1,0:T(8,128)(2,1)}, u32[]{:S(2)}) copy-start(bf16[128,1024]{1,0:T(8,128)(2,1)} %get-tuple-element.73) | copy-start | bytes 786436
  287.0 22.0 %collective-permute-start.8 = (bf16[128,1024]{1,0:T(8,128)(2,1)}, bf16[128,1024]{1,0:T(8,128)(2,1)S(1)}, u32[]{:S(2)}, u32[]{:S(2)}) collective-permute-start(bf16[128,1024]{1,0:T(8,128)(2,1)} %get-tuple-element.59), channel_id=1, source_target_pairs={{0,1},{1,0},{2,3},{3,2},{4,5},{5,4},{6,7},{7,6},{8,9},{9,8},{10,11... | collective-permute-start | bytes 786440 | tf_op jit(solution)/shard_map/ppermute | solution.py:344
  310.8 7.9 %collective-permute-start.10 = (bf16[128,1024]{1,0:T(8,128)(2,1)S(1)}, bf16[128,1024]{1,0:T(8,128)(2,1)S(1)}, u32[]{:S(2)}, u32[]{:S(2)}) collective-permute-start(bf16[128,1024]{1,0:T(8,128)(2,1)S(1)} %copy-done.16), channel_id=1, source_target_pairs={{0,1},{1,0},{2,3},{3,2},{4,5},{5,4},{6,7},{7,6},{8,9},{9,8},{10,11... | collective-permute-start | bytes 786440 | tf_op jit(solution)/shard_map/ppermute | solution.py:344
  318.7 0.7 copy-start.8
  324.1 5.0 %collective-permute-start.12 = (f32[16]{0:T(128)S(1)}, f32[16]{0:T(128)S(1)}, u32[]{:S(2)}, u32[]{:S(2)}) collective-permute-start(f32[16]{0:T(128)S(1)} %get-tuple-element.79), channel_id=1, source_target_pairs={{0,1},{1,0},{2,3},{3,2},{4,5},{5,4},{6,7},{7,6},{8,9},{9,8},{10,11... | collective-permute-start | bytes 200 | tf_op jit(solution)/shard_map/ppermute | solution.py:344

commit v2 on v1

v2 whole, which is shorter than its diff:
```python
import functools

import jax
import jax.numpy as jnp
from jax import lax
from jax.experimental import pallas as pl
from jax.experimental.pallas import tpu as pltpu
from jax.sharding import Mesh, PartitionSpec as P

bf16 = jnp.bfloat16
f32 = jnp.float32

D = 1024
HDIM = 64
SEQ = 256
HALF = 128
EXPERTS = 32
CAP = 80
SLOTS = 16 * CAP
EXT = D + 128
ROWS = 8 * CAP
PACK = 1664
W_ROWS = 208
NORM_EPS = 1e-06
ROPE_BASE = 10000.0
SCALE = 0.125
PLANE = ("x", "z")
NT = (((1,), (1,)), ((), ()))
TN = (((0,), (0,)), ((), ()))
VMEM_BYTES = 65000 * 1024


def mo(value, by):
    return pl.multiple_of(value, by)


def dot(a, b, dims=(((1,), (0,)), ((), ()))):
    return lax.dot_general(a, b, dims, preferred_element_type=f32)


def split(value):
    high = value.astype(bf16)
    return high, (value - high.astype(f32)).astype(bf16)


def iota(shape, dim):
    return lax.broadcasted_iota(jnp.int32, shape, dim)


def call(kernel, outs, args, scratch=(), grid=None, in_specs=None, out_specs=None, us=1, late_from=None, prefetch=False):
    smem = pl.BlockSpec(memory_space=pltpu.SMEM)
    params = pltpu.CompilerParams(vmem_limit_bytes=VMEM_BYTES)
    out_shape = [jax.ShapeDtypeStruct(shape, kind) for shape, kind in outs]
    nbytes = sum(a.size * a.dtype.itemsize for a in args) + sum(
        o.size * jnp.dtype(o.dtype).itemsize for o in out_shape
    )
    cost = pl.CostEstimate(flops=int(us * 1.15e9) + 1000, bytes_accessed=nbytes if us else 1000, transcendentals=0)
    if grid is None:
        vmem = pl.BlockSpec(memory_space=pltpu.VMEM)
        early = len(args) if late_from is None else late_from
        in_specs = [smem] + [vmem] * (early - 1) + [pl.BlockSpec(memory_space=pl.ANY)] * (len(args) - early)
        out_specs = [vmem] * len(outs)
        return pl.pallas_call(
            kernel,
            out_shape=out_shape,
            in_specs=in_specs,
            out_specs=out_specs,
            scratch_shapes=scratch,
            compiler_params=params,
            cost_estimate=cost,
        )(*args)
    if not prefetch:
        return pl.pallas_call(
            kernel,
            grid=grid,
            out_shape=out_shape,
            in_specs=[smem] + in_specs,
            out_specs=out_specs,
            scratch_shapes=scratch,
            compiler_params=params,
            cost_estimate=cost,
        )(*args)
    return pl.pallas_call(
        kernel,
        grid_spec=pltpu.PrefetchScalarGridSpec(
            num_scalar_prefetch=1, grid=grid, in_specs=in_specs, out_specs=out_specs, scratch_shapes=scratch
        ),
        out_shape=out_shape,
        compiler_params=params,
        cost_estimate=cost,
    )(*args)


def route_kernel(pos, routes, cot_own, cot_oth, packed, tab, tab_t, mask_out, grad, sent, turned):
    half = pos[0]
    named = routes[...]
    lane = iota((SEQ, 128), 1)
    mask = jnp.zeros((SEQ, 128), f32)
    for k in range(named.shape[1]):
        mask = mask + jnp.where(named[:, k : k + 1] == lane, 1.0, 0.0)
    mask_out[...] = mask
    below = jnp.where(iota((SEQ, SEQ), 0) > iota((SEQ, SEQ), 1), 1.0, 0.0).astype(bf16)
    place = dot(below, mask.astype(bf16))
    turned[...] = jnp.where(mask > 0.0, place, -1.0).T
    slot = iota((CAP, SEQ), 0).astype(f32)
    for i in range(16):
        row = turned[pl.ds(half * 16 + i, 1), :]
        tab[i * CAP : (i + 1) * CAP, :] = jnp.where(slot == row, 1.0, 0.0).astype(bf16)
    for n in range(SLOTS // 128):
        cols = slice(n * 128, (n + 1) * 128)
        tab_t[:, cols] = tab[cols, :].astype(f32).T.astype(bf16)
    grad[pl.ds(mo(half * HALF, HALF), HALF), :] = cot_own[...]
    grad[pl.ds(mo((1 - half) * HALF, HALF), HALF), :] = cot_oth[...]
    for n in range(4):
        spread_blocks(sent, n, dot(tab[...], grad[:, n * 256 : (n + 1) * 256]).astype(bf16), 16)
    sent[:, ROWS : ROWS + 192, :] = packed[...]


def spread_blocks(dst, n, value, peers):
    for i in range(peers):
        for j in range(2):
            at = (2 * n + j) * CAP
            dst[i, at : at + CAP, :] = value[i * CAP : (i + 1) * CAP, j * 128 : (j + 1) * 128]


def gather_blocks(dst, src, peers, blocks):
    for i in range(peers):
        for j in range(blocks):
            dst[i * CAP : (i + 1) * CAP, j * 128 : (j + 1) * 128] = src[i, j * CAP : (j + 1) * CAP, :]


def pick(rows, value, other):
    return jnp.where(rows == 0, value, jnp.where(rows == 1, other, 0.0))


def swap_halves(u, low):
    return jnp.where(low, pltpu.roll(u, 224, 1), pltpu.roll(u, 32, 1))


def doubled(tile, low, which):
    other = pltpu.roll(tile, 64, 1)
    return jnp.where(low, tile, other) if which == 0 else jnp.where(low, other, tile)


def stacked(tile, low):
    zero = jnp.zeros_like(tile)
    return jnp.concatenate([jnp.where(low, tile, zero), jnp.where(low, zero, tile)], axis=0)


def attn_kernel(
    pos, tok_own, tok_oth, w_a, w_b, w_c, w_d, cos, sin,
    rows, w, w_o, aux, attn_in, q_out, k_out, v_out, ctx, lse_out, part, small,
):
    half, core, late = pos[0], pos[1], pos[2]
    rows[pl.ds(mo(half * HALF, HALF), HALF), :] = tok_own[...]
    rows[pl.ds(mo((1 - half) * HALF, HALF), HALF), :] = tok_oth[...]
    for src, at_late, at_core in (
        (w_a, late, core),
        (w_b, 1 - late, core),
        (w_c, late, 1 - core),
        (w_d, 1 - late, 1 - core),
    ):
        for i in range(16):
            at = pl.ds(mo((at_late * 16 + i) * 32 + at_core * 16, 16), 16)
            w[at, :] = src[i, :, :1024]
            w_o[at, :] = src[i, :, 1024:1536]
            small[at, :] = src[i, :, 1536:PACK]
    aux[...] = small[...].astype(f32).T
    x = rows[...].astype(f32)
    factor = lax.rsqrt(jnp.mean(x * x, axis=1, keepdims=True) + NORM_EPS)
    attn_in[...] = (x * factor * aux[32:33, :]).astype(bf16)
    low32 = iota((SEQ, 256), 1) % 64 < 32
    low = iota((SEQ, 128), 1) < 64
    for n in range(4):
        lin = dot(attn_in[...], w[:, n * 256 : (n + 1) * 256])
        if n < 3:
            lin = lin * cos[...] + swap_halves(lin, low32) * sin[...]
        if n < 2:
            q_out[:, n * 256 : (n + 1) * 256] = lin.astype(bf16)
        else:
            dst = k_out if n == 2 else v_out
            for m in range(4):
                tile = lin[:, (m // 2) * 128 : (m // 2) * 128 + 128]
                dst[:, m * 128 : (m + 1) * 128] = doubled(tile, low, m % 2).astype(bf16)
    allowed = iota((2 * SEQ, SEQ), 0) % SEQ >= iota((2 * SEQ, SEQ), 1)
    for m in range(4):
        cols = slice(m * 128, (m + 1) * 128)
        scores = dot(stacked(q_out[:, cols], low), k_out[:, cols], NT) * SCALE
        scores = jnp.where(allowed, scores, -1e30)
        peak = jnp.max(scores, axis=1, keepdims=True)
        raised = jnp.exp(scores - peak)
        total = jnp.sum(raised, axis=1, keepdims=True)
        lse_out[m] = jnp.broadcast_to(peak + jnp.log(total), (2 * SEQ, 128))
        probs = (raised * (1.0 / total)).astype(bf16)
        both = dot(probs, v_out[:, cols])
        ctx[:, cols] = jnp.where(low, both[:SEQ], both[SEQ:]).astype(bf16)
    for n in range(4):
        outs = slice(n * 256, (n + 1) * 256)
        part[:, outs] = dot(ctx[...], w_o[outs, :], NT).astype(bf16)


def mid_kernel(pos, rows, part_own, part_oth, aux, tab, mask, middle, moe_in, gates_out, sent, turned):
    half = pos[0]
    value = rows[...].astype(f32) + (part_own[...].astype(f32) + part_oth[...].astype(f32))
    middle[...] = value
    factor = lax.rsqrt(jnp.mean(value * value, axis=1, keepdims=True) + NORM_EPS)
    moe_in[...] = (value * factor * aux[33:34, :]).astype(bf16)
    logits = dot(moe_in[...], aux[...].astype(bf16), NT)
    chosen = jnp.where(mask[...] > 0.0, logits, -1e30)
    raised = jnp.exp(chosen - jnp.max(chosen, axis=1, keepdims=True)) * mask[...]
    gates = raised / jnp.sum(raised, axis=1, keepdims=True)
    gates_out[...] = gates
    turned[...] = gates.T
    for n in range(4):
        spread_blocks(sent, n, dot(tab[...], moe_in[:, n * 256 : (n + 1) * 256]).astype(bf16), 16)
    lane = iota((CAP, 128), 1)
    slots = jnp.zeros((CAP, 128), f32)
    for i in range(16):
        row = turned[pl.ds(half * 16 + i, 1), :]
        found = jnp.sum(tab[i * CAP : (i + 1) * CAP, :].astype(f32) * row, axis=1, keepdims=True)
        slots = jnp.where(lane == i, found, slots)
    slots = jnp.concatenate([slots, jnp.zeros((128 - CAP, 128), f32)], axis=0).T
    at = iota((16, 128), 0)
    for i in range(16):
        line = slots[i : i + 1, :]
        high = line.astype(bf16).astype(f32)
        sent[i, ROWS : ROWS + 16, :] = pick(at, high, line - high).astype(bf16)


def weights_kernel(pos, a0, a1, a2, a3, b0, b1, b2, b3, w_gate, w_up, w_down):
    core, late = pos[1], pos[2]
    for srcs, at_core in (((a0, a1, a2, a3), core), ((b0, b1, b2, b3), 1 - core)):
        for src, at_late, f in zip(srcs, (late, 1 - late, late, 1 - late), (0, 0, 1, 1)):
            for i in range(16):
                rows = pl.ds(mo((at_late * 16 + i) * 32 + at_core * 16, 16), 16)
                for j, dst in enumerate((w_gate, w_up, w_down)):
                    for h in range(2):
                        cols = slice(f * 256 + h * 128, f * 256 + h * 128 + 128)
                        dst[rows, cols] = src[i, (j * 2 + h) * 16 : (j * 2 + h + 1) * 16, :]


def expert_kernel(pos, x, c, w_gate, w_up, w_down, dx, gate_g, up_g, scaled, xs, cs):
    gather_blocks(xs, x, 4, 8)
    gather_blocks(cs, c, 4, 8)
    lines = x[:, ROWS : ROWS + 16, :].astype(f32).reshape(64, 128)
    lines = jnp.concatenate([lines, jnp.zeros((64, 128), f32)], axis=0).T[:CAP]
    gate = jnp.concatenate(
        [lines[:, 16 * i : 16 * i + 1] + lines[:, 16 * i + 1 : 16 * i + 2] for i in range(4)], axis=0
    )
    g = dot(xs[...], w_gate[...])
    u = dot(xs[...], w_up[...])
    sig = jax.nn.sigmoid(g)
    silu = g * sig
    hidden = (silu * u).astype(bf16).astype(f32)
    raw = dot(cs[...], w_down[...])
    gate_grad = jnp.sum(hidden * raw, axis=1, keepdims=True)
    back = gate * raw
    gate_g[...] = (back * u * sig * (1.0 + g * (1.0 - sig))).astype(bf16)
    up_g[...] = (back * silu).astype(bf16)
    scaled[...] = (gate * hidden).astype(bf16)
    for n in range(4):
        cols = slice(n * 256, (n + 1) * 256)
        value = dot(gate_g[...], w_gate[cols, :], NT) + dot(up_g[...], w_up[cols, :], NT)
        spread_blocks(dx, n, value.astype(bf16), 4)
    high = gate_grad.astype(bf16).astype(f32)
    lane = iota((CAP, 128), 1)
    slots = jnp.zeros((CAP, 128), f32)
    for i in range(4):
        rows = slice(i * CAP, (i + 1) * CAP)
        slots = slots + pick(lane - 16 * i, high[rows], gate_grad[rows] - high[rows])
    slots = jnp.concatenate([slots, jnp.zeros((128 - CAP, 128), f32)], axis=0).T
    for i in range(4):
        dx[i, ROWS : ROWS + 16, :] = slots[16 * i : 16 * (i + 1), :].astype(bf16)


def expert_grad_kernel(pos, x, c, gate_g, up_g, scaled, mine, sent, xs, cs, held):
    core = pos[1]
    gather_blocks(xs, x, 16, 2)
    gather_blocks(cs, c, 16, 2)
    for j, (lhs, rhs) in enumerate(((xs, gate_g), (xs, up_g), (cs, scaled))):
        held[...] = dot(lhs[...], rhs[...], TN).astype(bf16)
        for i in range(8):
            for dst, at_core in ((mine, core), (sent, 1 - core)):
                rows = pl.ds(mo(i * 32 + at_core * 16, 16), 16)
                for f in range(2):
                    for h in range(2):
                        cols = slice(f * 256 + h * 128, f * 256 + h * 128 + 128)
                        dst[0, f, i, (j * 2 + h) * 16 : (j * 2 + h + 1) * 16, :] = held[rows, cols]


def expert_out_kernel(pos, scaled, w_down, y):
    value = dot(scaled[...], w_down[...], NT).astype(bf16)
    for i in range(16):
        for j in range(2):
            y[i, j * CAP : (j + 1) * CAP, :] = value[i * CAP : (i + 1) * CAP, j * 128 : (j + 1) * 128]


def expert_sum_kernel(pos, mine, got, got_yl, got_yh, got_diag, out):
    out[:, :96, :] = (mine[0, 0].astype(f32) + got[0, 0].astype(f32) + got_yl[...].astype(f32)).astype(bf16)
    out[:, 96:, :] = (got_yh[...].astype(f32) + got_diag[...].astype(f32)).astype(bf16)


def expert_final_kernel(pos, got, *outs):
    half = pos[0]
    for part, at_half in enumerate((half, 1 - half)):
        for j in range(6):
            at = part * 96 + j * 16
            value = jnp.swapaxes(got[:, at : at + 16, :].astype(f32), 0, 1)
            cols = slice((j % 2) * 128, (j % 2) * 128 + 128)
            outs[j // 2][:, pl.ds(mo(at_half * 16, 16), 16), cols] = value


def combine_kernel(pos, tab_t, got, out, held):
    half = pos[0]
    gather_blocks(held, got, 16, 8)
    lines = got[:, ROWS : ROWS + 16, :].astype(f32).reshape(256, 128).T[:CAP]
    lane = iota((CAP, 128), 1)
    for i in range(16):
        e = half * 16 + i
        high, low = lines[:, 16 * i : 16 * i + 1], lines[:, 16 * i + 1 : 16 * i + 2]
        extra = jnp.where(lane == e, high, jnp.where(lane == e + EXPERTS, low, 0.0))
        held[i * CAP : (i + 1) * CAP, D:EXT] = extra.astype(bf16)
    for start in range(0, EXT, 256):
        cols = slice(start, min(start + 256, EXT))
        out[:, cols] = dot(tab_t[...], held[:, cols]).astype(bf16)


def finish_kernel(pos, tab_t, got, middle, own, sent, gathered, held):
    half = pos[0]
    gather_blocks(gathered, got, 16, 8)
    for n in range(4):
        cols = slice(n * 256, (n + 1) * 256)
        held[:, cols] = dot(tab_t[...], gathered[:, cols])
    mine = pl.ds(mo(half * HALF, HALF), HALF)
    own[...] = middle[mine, :] + held[mine, :]
    sent[...] = held[pl.ds(mo((1 - half) * HALF, HALF), HALF), :].astype(bf16)


def cut_rows(mine, sent, held, late, core, blocks):
    for i in range(32):
        at_late = late if i < 16 else 1 - late
        for dst, at_core in ((mine, core), (sent, 1 - core)):
            rows = pl.ds(mo((at_late * 16 + i % 16) * 32 + at_core * 16, 16), 16)
            for b in range(blocks):
                dst[i, b * 16 : (b + 1) * 16, :] = held[rows, b * 128 : (b + 1) * 128]


def back_kernel(
    pos, comb_own, comb_oth, middle, moe_in, gates, aux, grad,
    w_o_at, ctx_at, q_at, k_at, v_at, lse_at, cos_at, sin_at, attn_in_at, w_at, rows_at,
    mg_own, part_own, part_sent, mine, sent, gains,
    w_o, ctx, q, k, v, lse, cos, sin, attn_in, w, rows, sems, mg, aog, pack, cgrad, dlin, apart,
):
    half, core, late = pos[0], pos[1], pos[2]
    pairs = (
        (w_o_at, w_o), (ctx_at, ctx), (q_at, q), (k_at, k), (v_at, v), (lse_at, lse), (cos_at, cos), (sin_at, sin),
        (attn_in_at, attn_in), (w_at, w), (rows_at, rows),
    )
    loads = [pltpu.make_async_copy(src, dst, sems.at[i]) for i, (src, dst) in enumerate(pairs)]
    for load in loads:
        load.start()
    gg = comb_own[:, D:EXT].astype(f32) + comb_oth[:, D:EXT].astype(f32)
    gg = gg + pltpu.roll(gg, 96, 1)
    gate = gates[...]
    logit_grad = gate * (gg - jnp.sum(gate * gg, axis=1, keepdims=True))
    lg_high, lg_low = split(logit_grad)
    router_t = aux[...].astype(bf16)
    moe_grad = comb_own[:, :D].astype(f32) + comb_oth[:, :D].astype(f32)
    moe_grad = moe_grad + dot(lg_high, router_t) + dot(lg_low, router_t)
    value = middle[...]
    factor = lax.rsqrt(jnp.mean(value * value, axis=1, keepdims=True) + NORM_EPS)
    normed = value * factor
    gain_two = jnp.sum(moe_grad * normed, axis=0, keepdims=True)
    inner = moe_grad * aux[33:34, :]
    mg[...] = grad[...].astype(f32) + factor * (
        inner - normed * jnp.mean(inner * normed, axis=1, keepdims=True)
    )
    mg_own[...] = mg[pl.ds(mo(half * HALF, HALF), HALF), :]
    aog[...] = mg[...].astype(bf16)
    for load in loads[:2]:
        load.wait()
    for n in range(2):
        cols = slice(n * 256, (n + 1) * 256)
        cgrad[:, cols] = dot(aog[...], w_o[:, cols]).astype(bf16)
        pack[:, 1024 + n * 256 : 1280 + n * 256] = dot(aog[...], ctx[:, cols], TN).astype(bf16)
    router_grad = dot(lg_high, moe_in[...], TN) + dot(lg_low, moe_in[...], TN)
    low32 = iota((SEQ, 256), 1) % 64 < 32
    low = iota((SEQ, 128), 1) < 64
    allowed = iota((2 * SEQ, SEQ), 0) % SEQ >= iota((2 * SEQ, SEQ), 1)
    for load in loads[2:]:
        load.wait()
    for m in range(4):
        cols = slice(m * 128, (m + 1) * 128)
        qs = stacked(q[:, cols], low)
        cs = stacked(cgrad[:, cols], low)
        scores = dot(qs, k[:, cols], NT) * SCALE
        probs = jnp.where(allowed, jnp.exp(scores - lse[m][:, :1]), 0.0)
        back = dot(cs, v[:, cols], NT)
        spread = jnp.sum(probs * back, axis=1, keepdims=True)
        sg = (probs * (back - spread)).astype(bf16)
        dq = dot(sg, k[:, cols])
        dlin[:, cols] = jnp.where(low, dq[:SEQ], dq[SEQ:]) * SCALE
        dk = dot(sg, qs, TN) * SCALE
        dv = dot(probs.astype(bf16), cs, TN)
        dk = dk + pltpu.roll(dk, 64, 1)
        dv = dv + pltpu.roll(dv, 64, 1)
        for base, val in ((512, dk), (768, dv)):
            at = slice(base + (m // 2) * 128, base + (m // 2) * 128 + 128)
            if m % 2 == 0:
                dlin[:, at] = val
            else:
                dlin[:, at] = jnp.where(low, dlin[:, at], val)
    lows = []
    for n in range(4):
        cols = slice(n * 256, (n + 1) * 256)
        lin = dlin[:, cols]
        if n < 3:
            lin = lin * cos[...] - swap_halves(lin, low32) * sin[...]
        lin = lin.astype(bf16)
        lows.append(lin)
        pack[:, cols] = dot(attn_in[...], lin, TN).astype(bf16)
    lows = jnp.concatenate(lows, axis=1)
    for n in range(4):
        cols = slice(n * 256, (n + 1) * 256)
        apart[:, cols] = dot(lows, w[cols, :], NT)
    part_own[...] = apart[pl.ds(mo(half * HALF, HALF), HALF), :]
    part_sent[...] = apart[pl.ds(mo((1 - half) * HALF, HALF), HALF), :].astype(bf16)
    x = rows[...].astype(f32)
    normed_one = x * lax.rsqrt(jnp.mean(x * x, axis=1, keepdims=True) + NORM_EPS)
    gain_one = jnp.sum(apart[...] * normed_one, axis=0, keepdims=True)
    lines = jnp.concatenate([gain_one[:, n * 128 : (n + 1) * 128] for n in range(8)], axis=0)
    high = lines.astype(bf16).astype(f32)
    gains[...] = jnp.concatenate([high, lines - high], axis=0).astype(bf16)
    pack[:, 1536:PACK] = jnp.where(iota((128, D), 0) == 33, gain_two, router_grad).T.astype(bf16)
    cut_rows(mine, sent, pack, late, core, 13)


def input_kernel(pos, tok, aux, mg, part_own, part_oth, out):
    x = tok[...].astype(f32)
    factor = lax.rsqrt(jnp.mean(x * x, axis=1, keepdims=True) + NORM_EPS)
    normed = x * factor
    inner = (part_own[...] + part_oth[...].astype(f32)) * aux[32:33, :]
    inner = factor * (inner - normed * jnp.mean(inner * normed, axis=1, keepdims=True))
    out[...] = (mg[...] + inner).astype(bf16)


def final_kernel(pos, got, w_query, w_key, w_value, w_out, w_router, gain_two, gain_one):
    total = got[0].astype(f32)
    for i in range(1, 16):
        total = total + got[i].astype(f32)
    for base, dst, blocks in ((0, w_query, 4), (4, w_key, 2), (6, w_value, 2), (8, w_out, 4)):
        for b in range(blocks):
            at = (base + b) * 16
            dst[:, b * 128 : (b + 1) * 128] = total[at : at + 16, :]
    w_router[...] = total[192:208, :32]
    turned = jnp.concatenate([total[192:208, :], jnp.zeros((112, 128), f32)], axis=0).T
    gain_two[...] = turned[33:34, :16]
    gains = total[208:216, :] + total[216:224, :]
    at = pos[4]
    row = jnp.sum(jnp.where(iota((8, 128), 0) == at // 8, gains, 0.0), axis=0, keepdims=True)
    lanes = pltpu.roll(jnp.broadcast_to(row, (8, 128)), (128 - (at % 8) * 16) % 128, 1)
    gain_one[...] = lanes[0:1, :16]


def rotary_tables():
    column = iota((SEQ, 256), 1)
    frequency = ROPE_BASE ** (-((column % (HDIM // 2)).astype(f32) * 2.0 / HDIM))
    angles = iota((SEQ, 256), 0).astype(f32) * frequency
    sin = jnp.sin(angles)
    return jnp.cos(angles), jnp.where(column % HDIM < HDIM // 2, -sin, sin)


def swap(value, axis):
    if axis == "diag":
        return lax.ppermute(value, ("yl", "yh"), [(0, 3), (3, 0), (1, 2), (2, 1)])
    return lax.ppermute(value, axis, [(0, 1), (1, 0)])


def plane(value):
    return lax.all_to_all(value, PLANE, 0, 0, tiled=True)


def added(*values, gate=None):
    total = (values[0] if gate is None else after(values[0], gate)).astype(f32)
    for value in values[1:]:
        total = total + value.astype(f32)
    return total.astype(bf16)


def after(value, *others):
    return lax.optimization_barrier((value, *others))[0]


def at_index(value, i):
    return lax.dynamic_index_in_dim(value, i, 0, keepdims=False)


def body(
    tokens,
    routes,
    cotangent,
    attn_gain,
    query_weight,
    key_weight,
    value_weight,
    out_weight,
    moe_gain,
    router_weight,
    expert_gate,
    expert_up,
    expert_down,
):
    half, core, late = lax.axis_index("yh"), lax.axis_index("c"), lax.axis_index("yl")
    place = lax.axis_index("x") * 4 + lax.axis_index("z")
    pos = jnp.stack([half, core, late, half * 16 + place, (late * 16 + place) * 2 + core]).astype(jnp.int32)
    cos, sin = rotary_tables()

    packed = jnp.concatenate(
        [
            query_weight, key_weight, value_weight, out_weight, router_weight,
            attn_gain[:, None], moe_gain[:, None], jnp.zeros((16, 94), bf16),
        ],
        axis=1,
    )
    w_a = plane(jnp.broadcast_to(packed[None], (16, 16, PACK)))
    tok_oth = swap(tokens, "yh")
    cot_oth = swap(cotangent, "yh")
    cot_oth, tok_oth, cos, sin = lax.optimization_barrier((cot_oth, tok_oth, cos, sin))

    experts = jnp.stack([expert_gate, expert_up, expert_down])
    experts = experts.reshape(3, 16, 2, 16, 2, 128).transpose(3, 2, 0, 4, 1, 5).reshape(16, 192, 128)
    tab, tab_t, mask, grad, cot_sent = call(
        route_kernel,
        [
            ((SLOTS, SEQ), bf16), ((SEQ, SLOTS), bf16), ((SEQ, 128), f32), ((SEQ, D), bf16),
            ((16, ROWS + 192, 128), bf16),
        ],
        [pos, routes, cotangent, cot_oth, experts],
        scratch=[pltpu.VMEM((128, SEQ), f32)],
        us=5,
    )
    w_a = after(w_a, cot_sent)
    w_b = swap(w_a, "yl")
    w_c = swap(w_a, "c")
    w_d = swap(w_b, "c")
    cot_slots = plane(after(cot_sent, w_c))

    e_own = lax.dynamic_slice_in_dim(cot_slots, ROWS + 96 * half, 96, 1)
    e_oth = lax.dynamic_slice_in_dim(cot_slots, ROWS + 96 * (1 - half), 96, 1)
    pieces = [e_own, swap(e_own, "yl"), swap(e_oth, "yh"), swap(e_oth, "diag")]
    pieces = pieces + [swap(piece, "c") for piece in pieces]
    w_gate, w_up, w_down = call(weights_kernel, [((D, 512), bf16)] * 3, [pos] + pieces, us=4)

    rows, w, w_o, aux, attn_in, q, k, v, ctx, lse, part = call(
        attn_kernel,
        [
            ((SEQ, D), bf16), ((D, D), bf16), ((D, 512), bf16), ((128, D), f32), ((SEQ, D), bf16),
            ((SEQ, 512), bf16), ((SEQ, 512), bf16), ((SEQ, 512), bf16), ((SEQ, 512), bf16), ((4, 512, 128), f32),
            ((SEQ, D), bf16),
        ],
        [pos, tokens, tok_oth, w_a, w_b, w_c, w_d, cos, sin],
        scratch=[pltpu.VMEM((D, 128), bf16)],
        us=7,
    )
    part_oth = swap(part, "yh")
    middle, moe_in, gates, x_sent = call(
        mid_kernel,
        [((SEQ, D), f32), ((SEQ, D), bf16), ((SEQ, 128), f32), ((16, ROWS + 16, 128), bf16)],
        [pos, rows, part, part_oth, aux, tab, mask],
        scratch=[pltpu.VMEM((128, SEQ), f32)],
        us=3,
    )
    x_slots = plane(x_sent)

    whole = pl.BlockSpec((D, 512), lambda i, *pos: (0, 0))
    by_row = pl.BlockSpec((4 * CAP, 512), lambda i, *pos: (i, 0))
    by_peer = lambda rows: pl.BlockSpec((4, rows, 128), lambda i, *pos: (i, 0, 0))
    dx, gate_g, up_g, scaled = call(
        expert_kernel,
        [((16, ROWS + 16, 128), bf16), ((SLOTS, 512), bf16), ((SLOTS, 512), bf16), ((SLOTS, 512), bf16)],
        [pos, x_slots, cot_slots, w_gate, w_up, w_down],
        scratch=[pltpu.VMEM((4 * CAP, D), bf16), pltpu.VMEM((4 * CAP, D), bf16)],
        grid=(4,),
        in_specs=[by_peer(ROWS + 16), by_peer(ROWS), whole, whole, whole],
        out_specs=[by_peer(ROWS + 16), by_row, by_row, by_row],
        us=12,
    )
    dx_back = plane(dx)

    full = pl.BlockSpec((SLOTS, 512), lambda i, *pos: (0, 0))
    by_col = pl.BlockSpec((16, 2 * CAP, 128), lambda i, *pos: (0, i, 0))
    by_owner = pl.BlockSpec((1, 2, 8, 96, 128), lambda i, pos: ((i // 2 + pos[2]) % 2, 0, i % 2, 0, 0))
    e_mine, e_sent = call(
        expert_grad_kernel,
        [((2, 2, 16, 96, 128), bf16), ((2, 2, 16, 96, 128), bf16)],
        [pos, x_slots, cot_slots, gate_g, up_g, scaled],
        scratch=[
            pltpu.VMEM((SLOTS, 256), bf16), pltpu.VMEM((SLOTS, 256), bf16), pltpu.VMEM((256, 512), bf16),
        ],
        grid=(4,),
        in_specs=[by_col, by_col, full, full, full],
        out_specs=[by_owner, by_owner],
        us=0,
        prefetch=True,
    )


    e_got = swap(e_sent, "c")
    e_yl, e_yh, e_diag = (
        swap(added(e_mine[i, j], e_got[i, j]), axis) for i, j, axis in ((1, 0, "yl"), (0, 1, "yh"), (1, 1, "diag"))
    )
    (y,) = call(
        expert_out_kernel,
        [((16, ROWS, 128), bf16)],
        [pos, after(scaled, e_got), w_down],
        grid=(4,),
        in_specs=[full, pl.BlockSpec((256, 512), lambda i, *pos: (i, 0))],
        out_specs=[by_col],
        us=0,
    )
    dx_back = after(dx_back, e_yl)
    (comb,) = call(
        combine_kernel, [((SEQ, EXT), bf16)], [pos, tab_t, dx_back],
        scratch=[pltpu.VMEM((SLOTS, EXT), bf16)], us=0,
    )
    comb = after(comb, e_yh, e_diag)
    comb_oth = swap(comb, "yh")
    y_back = plane(y)
    by_first = pl.BlockSpec((1, 1, 16, 96, 128), lambda i, *pos: (0, 0, 0, 0, 0))
    by_third = pl.BlockSpec((16, 96, 128), lambda i, *pos: (0, 0, 0))
    (e_cat,) = call(
        expert_sum_kernel,
        [((16, 192, 128), bf16)],
        [pos, after(e_mine, comb), e_got, e_yl, e_yh, e_diag],
        grid=(1,),
        in_specs=[by_first, by_first, by_third, by_third, by_third],
        out_specs=[pl.BlockSpec((16, 192, 128), lambda i, *pos: (0, 0, 0))],
        us=0,
    )
    comb_oth = after(comb_oth, e_cat)
    mg_own, part_own, part_sent, a_mine, a_sent, gains = call(
        back_kernel,
        [
            ((HALF, D), f32), ((HALF, D), f32), ((HALF, D), bf16), ((32, W_ROWS, 128), bf16),
            ((32, W_ROWS, 128), bf16), ((16, 128), bf16),
        ],
        [
            pos, comb, comb_oth, middle, moe_in, gates, aux, grad,
            w_o, ctx, q, k, v, lse, cos, sin, attn_in, w, rows,
        ],
        late_from=8,
        scratch=[
            pltpu.VMEM((D, 512), bf16), pltpu.VMEM((SEQ, 512), bf16), pltpu.VMEM((SEQ, 512), bf16),
            pltpu.VMEM((SEQ, 512), bf16), pltpu.VMEM((SEQ, 512), bf16), pltpu.VMEM((4, 512, 128), f32),
            pltpu.VMEM((SEQ, 256), f32), pltpu.VMEM((SEQ, 256), f32), pltpu.VMEM((SEQ, D), bf16),
            pltpu.VMEM((D, D), bf16), pltpu.VMEM((SEQ, D), bf16), pltpu.SemaphoreType.DMA((11,)),
            pltpu.VMEM((SEQ, D), f32), pltpu.VMEM((SEQ, D), bf16), pltpu.VMEM((D, PACK), bf16),
            pltpu.VMEM((SEQ, 512), bf16), pltpu.VMEM((SEQ, D), f32), pltpu.VMEM((SEQ, D), f32),
        ],
        us=0,
    )

    a_got = swap(a_sent, "c")
    gains = gains.astype(f32)
    gains = gains[:8] + gains[8:]
    for axis in ("yh", "c"):
        gains = gains + swap(gains, axis)
    high = gains.astype(bf16)
    gains = jnp.concatenate([high, (gains - high.astype(f32)).astype(bf16)], axis=0)
    gains = jnp.broadcast_to(gains[None], (16, 16, 128))
    a_move = jnp.concatenate([added(a_mine[16:], a_got[16:], gate=y_back), gains], axis=1)
    a_yl = swap(a_move, "yl")
    out_own, out_sent = call(
        finish_kernel,
        [((HALF, D), f32), ((HALF, D), bf16)],
        [pos, tab_t, after(y_back, a_move), middle],
        scratch=[pltpu.VMEM((SLOTS, D), bf16), pltpu.VMEM((SEQ, D), f32)],
        us=0,
    )
    e_back = plane(after(e_cat, out_sent))
    a_sum = [added(a_mine[:16], a_got[:16], a_yl[:, :W_ROWS]), added(gains, a_yl[:, W_ROWS:])]
    a_sum = jnp.concatenate(a_sum, axis=1)
    total = plane(after(a_sum, e_back))

    part_oth = swap(after(part_sent, a_sum), "yh")
    (input_grad,) = call(
        input_kernel, [((HALF, D), bf16)], [pos, tokens, aux, mg_own, part_own, part_oth], us=0
    )
    w_query, w_key, w_value, w_out, w_router, gain_two, gain_one = call(
        final_kernel,
        [((16, n), f32) for n in (512, 256, 256, 512, 32)] + [((1, 16), f32)] * 2,
        [pos, total],
        us=2,
    )

    grad_gate, grad_up, grad_down = call(
        expert_final_kernel, [((16, EXPERTS, 256), f32)] * 3, [pos, after(e_back, input_grad)], us=0
    )

    output = (out_own + swap(after(out_sent, a_sum), "yh").astype(f32)).astype(bf16)
    return (
        output,
        input_grad,
        gain_one.reshape(16),
        w_query,
        w_key,
        w_value,
        w_out,
        gain_two.reshape(16),
        w_router,
        grad_gate,
        grad_up,
        grad_down,
    )


def solution(mesh):
    fine = Mesh(mesh.devices.reshape(2, 4, 4, 2, 2), ("yl", "x", "z", "c", "yh"))
    dp, every = ("yl", "x", "z", "c"), ("yl", "x", "z", "c", "yh")
    in_specs = (
        P(every, None),
        P(dp, None),
        P(every, None),
        P(dp),
        P(dp, "yh"),
        P(dp, "yh"),
        P(dp, "yh"),
        P(dp, "yh"),
        P(dp),
        P(dp, None),
        P(dp, None, "yh"),
        P(dp, None, "yh"),
        P(dp, None, "yh"),
    )
    out_specs = (
        P(every, None),
        P(every, None),
        P(dp),
        P(dp, "yh"),
        P(dp, "yh"),
        P(dp, "yh"),
        P(dp, "yh"),
        P(dp),
        P(dp, None),
        P(dp, None, "yh"),
        P(dp, None, "yh"),
        P(dp, None, "yh"),
    )
    return jax.shard_map(body, mesh=fine, in_specs=in_specs, out_specs=out_specs, check_vma=False)
```

time: 332 us -> 282 us (0.85)
  waiting for transfers between devices: 158 us -> 98.5 us
  Pallas kernels: 61.3 us -> 78.5 us
  local copies, waits for them, and re-layouts: 26.7 us -> 11.7 us
  starting transfers between devices: 70.8 us -> 76.7 us
    all_to_all x8 -> x7, waiting for transfers between devices: 67.9 us -> 20.3 us  [plane(): return lax.all_to_all(value, PLANE, 0, 0, tiled=True)]
    ppermute x16 -> x22, waiting for transfers between devices: 90.1 us -> 62.6 us  [swap(): return lax.ppermute(value, axis, [(0, 1), (1, 0)])]
    ppermute x0 -> x2, waiting for transfers between devices: none -> 15.6 us  [swap(): return lax.ppermute(value, ('yl', 'yh'), [(0, 3), (3, 0), (1, 2), (2, 1)])]
    pallas_call x7 -> x10, Pallas kernels: 38.7 us -> 48.8 us  [call(): pl.pallas_call(kernel, out_shape=out_shape, in_specs=in_specs, out_specs=...]
    pallas_call x0 -> x1, Pallas kernels: none -> 9.85 us  [call(): pl.pallas_call(kernel, grid_spec=pltpu.PrefetchScalarGridSpec(num_scalar_...]
    another operation x6 -> x1, local copies, waits for them, and re-layouts: 6.77 us -> 0.6 us  [body(): jnp.stack([half, core, late, half * 16 + place, (late * 16 + place) * 2 +...]
    ppermute x0 -> x2, starting transfers between devices: none -> 5.2 us  [swap(): return lax.ppermute(value, ('yl', 'yh'), [(0, 3), (3, 0), (1, 2), (2, 1)])]
    slice x8 -> x1, local copies, waits for them, and re-layouts: 5.55 us -> 1.21 us  [body(): a_mine[16:]]
  transfers between devices with their start and end apart: 24 -> 31, of which waited for: 17 -> 18; matrix products, arithmetic and copies ran while one was open for 8% -> 7% of each run, Pallas kernels for 15% -> 23%
where the time goes in v2:
time: 282 us; the launch traced here: 280 us
  waiting for transfers between devices  98.5 us (35%)
  Pallas kernels  78.5 us (28%)
  starting transfers between devices  76.7 us (27%)
  other arithmetic  13.5 us (5%)
  local copies, waits for them, and re-layouts  11.7 us (4%)
    ppermute x22, waiting for transfers between devices, swap(): return lax.ppermute(value, axis, [(0, 1), (1, 0)])  62.6 us
    pallas_call x10, Pallas kernels, call(): pl.pallas_call(kernel, out_shape=out_shape, in_specs=in_specs, out_specs=...  48.8 us
    all_to_all x7, starting transfers between devices, plane(): return lax.all_to_all(value, PLANE, 0, 0, tiled=True)  47.3 us
    ppermute x22, starting transfers between devices, swap(): return lax.ppermute(value, axis, [(0, 1), (1, 0)])  24.2 us
    all_to_all x7, waiting for transfers between devices, plane(): return lax.all_to_all(value, PLANE, 0, 0, tiled=True)  20.3 us
    pallas_call x3, Pallas kernels, call(): pl.pallas_call(kernel, grid=grid, out_shape=out_shape, in_specs=[smem] +...  19.8 us
    ppermute x2, waiting for transfers between devices, swap(): return lax.ppermute(value, ('yl', 'yh'), [(0, 3), (3, 0), (1, 2), (2, 1)])  15.6 us
    pallas_call x1, Pallas kernels, call(): pl.pallas_call(kernel, grid_spec=pltpu.PrefetchScalarGridSpec(num_scalar_...  9.85 us
  transfers between devices with their start and end apart: 31, of which 18 were waited for; matrix products, arithmetic and copies ran while one was open for 7% of the time, Pallas kernels for 23%

profile of v2, /device:TPU:0, one launch (start us, length us, event | category | flops | bytes accessed | tf_op | source)
XLA Modules:
  0.0 279.9 jit_solution(17158148811803171151)
XLA Ops:
  0.7 3.4 %collective-permute-start = (bf16[128,1024]{1,0:T(8,128)(2,1)}, bf16[128,1024]{1,0:T(8,128)(2,1)S(1)}, u32[]{:S(2)}, u32[]{:S(2)}) collective-permute-start(bf16[128,1024]{1,0:T(8,128)(2,1)} %cot_own.1), channel_id=1, source_target_pairs={{0,1},{1,0},{2,3},{3,2},{4,5},{5,4},{6,7},{7,6},{8,9},{9,8},{10,11... | collective-permute-start | bytes 786440 | tf_op jit(solution)/shard_map/ppermute | solution.py:476
  7.7 8.1 %all-to-all-start = ((bf16[16,16,1664]{2,1,0:T(8,128)(2,1)}), bf16[16,16,1664]{2,1,0:T(8,128)(2,1)}, u32[]{:S(2)}, u32[]{:S(2)}) async-start(bf16[16,16,1664]{2,1,0:T(8,128)(2,1)} %broadcast_in_dim.26), calls=%async_computation | async-start | bytes 1703936 | tf_op jit(solution)/shard_map/all_to_all | solution.py:480
  19.4 1.8 negate_select_fusion
  21.9 5.0 %shard_map.220 = (bf16[1280,256]{1,0:T(8,128)(2,1)}, bf16[256,1280]{1,0:T(8,128)(2,1)}, f32[256,128]{1,0:T(8,128)}, bf16[256,1024]{1,0:T(8,128)(2,1)}, bf16[16,832,128]{2,1,0:T(8,128)(2,1)}) custom-call(s32[5]{0:T(128)} %stack.35.pos, s32[256,8]{1,0:T(8,128)} %copy.28.routes, bf16[128,1024]{1,0:T(8,128)(2,1)} %cot_own.1, bf16[128,1024]{1,0:T(8,128)(2,1)} %copy-done.17, ...), custom_call_target="tpu_custom_call" | custom-call | flops 5750001152 | bytes 6692884 | tf_op jit(solution)/shard_map/pallas_call | solution.py:63
  27.0 3.4 %all-to-all-done.w_a = bf16[16,16,1664]{2,1,0:T(8,128)(2,1)} async-done(((bf16[16,16,1664]{2,1,0:T(8,128)(2,1)}), bf16[16,16,1664]{2,1,0:T(8,128)(2,1)}, u32[]{:S(2)}, u32[]{:S(2)}) %all-to-all-start) | async-done | bytes 852000 | tf_op jit(solution)/shard_map/all_to_all | solution.py:480
  30.3 1.5 collective-permute-start.2
  33.1 4.5 %all-to-all-start.2 = ((bf16[16,832,128]{2,1,0:T(8,128)(2,1)}), bf16[16,832,128]{2,1,0:T(8,128)(2,1)}, u32[]{:S(2)}, u32[]{:S(2)}) async-start(bf16[16,832,128]{2,1,0:T(8,128)(2,1)} %get-tuple-element.90), calls=%async_computation.2 | async-start | bytes 6815744 | tf_op jit(solution)/shard_map/all_to_all | solution.py:480
  37.6 14.3 %collective-permute-done.2.w_b = bf16[16,16,1664]{2,1,0:T(8,128)(2,1)S(1)} collective-permute-done((bf16[16,16,1664]{2,1,0:T(8,128)(2,1)}, bf16[16,16,1664]{2,1,0:T(8,128)(2,1)S(1)}, u32[]{:S(2)}, u32[]{:S(2)}) %collective-permute-start.2) | collective-permute-done | bytes 852000 | tf_op jit(solution)/shard_map/ppermute | solution.py:476
  52.8 2.5 collective-permute-done.4.w_d
  55.3 7.6 %shard_map.221 = (bf16[256,1024]{1,0:T(8,128)(2,1)}, bf16[1024,1024]{1,0:T(8,128)(2,1)}, bf16[1024,512]{1,0:T(8,128)(2,1)}, f32[128,1024]{1,0:T(8,128)}, bf16[25...) custom-call(s32[5]{0:T(128)} %stack.35.pos, ...), custom_call_target="tpu_custom_call" | custom-call | flops 8050000896 | bytes 11796500 | tf_op jit(solution)/shard_map/pallas_call | solution.py:63
  62.9 3.2 %collective-permute-start.5 = (bf16[256,1024]{1,0:T(8,128)(2,1)}, bf16[256,1024]{1,0:T(8,128)(2,1)}, u32[]{:S(2)}, u32[]{:S(2)}) collective-permute-start(bf16[256,1024]{1,0:T(8,128)(2,1)} %get-tuple-element.85.part_own), channel_id=1, source_target_pairs={{0,1},{1,0},{2,3},{3,2},{4,5},{5,4},{6,7},{7,6},{8,9},{9,8},{10,11... | collective-permute-start | bytes 1572872 | tf_op jit(solution)/shard_map/ppermute | solution.py:476
  66.0 12.6 %collective-permute-done.5.part_oth = bf16[256,1024]{1,0:T(8,128)(2,1)} collective-permute-done((bf16[256,1024]{1,0:T(8,128)(2,1)}, bf16[256,1024]{1,0:T(8,128)(2,1)}, u32[]{:S(2)}, u32[]{:S(2)}) %collective-permute-start.5) | collective-permute-done | bytes 524320 | tf_op jit(solution)/shard_map/ppermute | solution.py:476
  78.7 4.8 %shard_map.222 = (f32[256,1024]{1,0:T(8,128)}, bf16[256,1024]{1,0:T(8,128)(2,1)}, f32[256,128]{1,0:T(8,128)}, bf16[16,656,128]{2,1,0:T(8,128)(2,1)}) custom-call(s32[5]{0:T(128)} %stack.35.pos, bf16[256,1024]{1,0:T(8,128)(2,1)} %get-tuple-element.84.rows.rows_at, bf16[256,1024]{1,0:T(8,128)(2,1)} %get-tuple-element.85.part_own, ...), custom_call_target="tpu_custom_call" | custom-call | flops 3450000896 | bytes 7274516 | tf_op jit(solution)/shard_map/pallas_call | solution.py:63
  83.9 11.8 %all-to-all-start.1 = ((bf16[16,656,128]{2,1,0:T(8,128)(2,1)}), bf16[16,656,128]{2,1,0:T(8,128)(2,1)}, u32[]{:S(2)}, u32[]{:S(2)}) async-start(bf16[16,656,128]{2,1,0:T(8,128)(2,1)} %get-tuple-element.89), calls=%async_computation.1 | async-start | bytes 5373952 | tf_op jit(solution)/shard_map/all_to_all | solution.py:480
  96.9 3.1 %collective-permute-start.8 = (bf16[16,96,128]{2,1,0:T(8,128)(2,1)S(1)}, bf16[16,96,128]{2,1,0:T(8,128)(2,1)S(1)}, u32[]{:S(2)}, u32[]{:S(2)}) collective-permute-start(bf16[16,96,128]{2,1,0:T(8,128)(2,1)S(1)} %get-tuple-element.142), channel_id=1, source_target_pairs={{0,65},{65,0},{1,64},{64,1},{2,67},{67,2},{3,66},{66,3},{4,69},{69... | collective-permute-start | bytes 1179656 | tf_op jit(solution)/shard_map/ppermute | solution.py:475
  101.1 15.6 %collective-permute-done.8.a3 = bf16[16,96,128]{2,1,0:T(8,128)(2,1)S(1)} collective-permute-done((bf16[16,96,128]{2,1,0:T(8,128)(2,1)S(1)}, bf16[16,96,128]{2,1,0:T(8,128)(2,1)S(1)}, u32[]{:S(2)}, u32[]{:S(2)}) %collective-permute-start.8) | collective-permute-done | bytes 393248 | tf_op jit(solution)/shard_map/ppermute | solution.py:475
  120.0 4.2 %shard_map.223 = (bf16[1024,512]{1,0:T(8,128)(2,1)}, bf16[1024,512]{1,0:T(8,128)(2,1)}, bf16[1024,512]{1,0:T(8,128)(2,1)}) custom-call(s32[5]{0:T(128)} %stack.35.pos, bf16[16,96,128]{2,1,0:T(8,128)(2,1)} %copy-done.3, bf16[16,96,128]{2,1,0:T(8,128)(2,1)} %copy-done.12, bf16[16,96,128]{2,1,0:T(8,128)(2,1)} %copy-done.11, bf16[16,96,128]{2,1,0:T(8,128)(2,1)} %copy-done.10, ...), custom_call_target="tpu_custom_call" | custom-call | flops 4600001024 | bytes 6291476 | tf_op jit(solution)/shard_map/pallas_call | solution.py:63
  124.2 8.4 %all-to-all-done.1.x = bf16[16,656,128]{2,1,0:T(8,128)(2,1)} async-done(((bf16[16,656,128]{2,1,0:T(8,128)(2,1)}), bf16[16,656,128]{2,1,0:T(8,128)(2,1)}, u32[]{:S(2)}, u32[]{:S(2)}) %all-to-all-start.1) | async-done | bytes 2687008 | tf_op jit(solution)/shard_map/all_to_all | solution.py:480
  132.6 12.1 %shard_map.224 = (bf16[16,656,128]{2,1,0:T(8,128)(2,1)}, bf16[1280,512]{1,0:T(8,128)(2,1)}, bf16[1280,512]{1,0:T(8,128)(2,1)}, bf16[1280,512]{1,0:T(8,128)(2,1)}) custom-call(s32[5]{0:T(128)} %stack.35.pos, bf16[16,656,128]{2,1,0:T(8,128)(2,1)} %all-to-all-done.1.x, bf16[16,832,128]{2,1,0:T(8,128)(2,1)} %all-to-all-done.2.c, ...), custom_call_target="tpu_custom_call" | custom-call | flops 13800000512 | bytes 15859732 | tf_op jit(solution)/shard_map/pallas_call | solution.py:73
  144.7 4.5 %all-to-all-start.4 = ((bf16[16,656,128]{2,1,0:T(8,128)(2,1)}), bf16[16,656,128]{2,1,0:T(8,128)(2,1)}, u32[]{:S(2)}, u32[]{:S(2)}) async-start(bf16[16,656,128]{2,1,0:T(8,128)(2,1)} %get-tuple-element.99), calls=%async_computation.4 | async-start | bytes 5373952 | tf_op jit(solution)/shard_map/all_to_all | solution.py:480
  149.2 9.8 %shard_map.225 = (bf16[2,2,16,96,128]{4,3,2,1,0:T(8,128)(2,1)}, bf16[2,2,16,96,128]{4,3,2,1,0:T(8,128)(2,1)}) custom-call(s32[5]{0:T(128)} %stack.35.pos, bf16[16,656,128]{2,1,0:T(8,128)(2,1)} %all-to-all-done.1.x, bf16[16,832,128]{2,1,0:T(8,128)(2,1)} %all-to-all-done.2.c, bf16[1280,512]{1,0:T(8,128)(2,1)} %get-tuple-element.95.gate_g, ...), custom_call_target="tpu_custom_call" | custom-call | flops 1000 | bytes 1000 | tf_op jit(solution)/shard_map/pallas_call | solution.py:83
  159.0 3.6 %collective-permute-done.13.got = bf16[2,2,16,96,128]{4,3,2,1,0:T(8,128)(2,1)S(1)} collective-permute-done((bf16[2,2,16,96,128]{4,3,2,1,0:T(8,128)(2,1)}, bf16[2,2,16,96,128]{4,3,2,1,0:T(8,128)(2,1)S(1)}, u32[]{:S(2)}, u32[]{:S(2)}) %collective-permute-start.13) | collective-permute-done | bytes 1572896 | tf_op jit(solution)/shard_map/ppermute | solution.py:476
  162.6 3.0 %fusion.2 = (bf16[16,96,128]{2,1,0:T(8,128)(2,1)}, bf16[16,96,128]{2,1,0:T(8,128)(2,1)S(1)}, bf16[16,96,128]{2,1,0:T(8,128)(2,1)}) fusion(bf16[2,2,16,96,128]{4,3,2,1,0:T(8,128)(2,1)S(1)} %collective-permute-done.13.got, bf16[2,2,16,96,128]{4,3,2,1,0:T(8,128)(2,1)} %get-tuple-element.103.mine), kind=kLoop, calls=%fused_computation.11 | loop fusion | flops 2359296 | bytes 3538944 | tf_op jit(solution)/shard_map/convert_element_type | solution.py:487
  165.6 1.6 collective-permute-start.14
  167.2 2.1 collective-permute-start.16
  170.1 5.2 %shard_map.226 = bf16[16,640,128]{2,1,0:T(8,128)(2,1)} custom-call(s32[5]{0:T(128)} %stack.35.pos, bf16[1280,512]{1,0:T(8,128)(2,1)} %get-tuple-element.98.scaled, bf16[1024,512]{1,0:T(8,128)(2,1)} %get-tuple-element.93.w_down), custom_call_target="tpu_custom_call" | custom-call | flops 1000 | bytes 1000 | tf_op jit(solution)/shard_map/pallas_call | solution.py:73
  175.3 7.0 %all-to-all-done.4.got = bf16[16,656,128]{2,1,0:T(8,128)(2,1)} async-done(((bf16[16,656,128]{2,1,0:T(8,128)(2,1)}), bf16[16,656,128]{2,1,0:T(8,128)(2,1)}, u32[]{:S(2)}, u32[]{:S(2)}) %all-to-all-start.4) | async-done | bytes 2687008 | tf_op jit(solution)/shard_map/all_to_all | solution.py:480
  182.3 5.5 %all-to-all-start.3 = ((bf16[16,640,128]{2,1,0:T(8,128)(2,1)}), bf16[16,640,128]{2,1,0:T(8,128)(2,1)}, u32[]{:S(2)}, u32[]{:S(2)}) async-start(bf16[16,640,128]{2,1,0:T(8,128)(2,1)} %shard_map.226), calls=%async_computation.3 | async-start | bytes 5242880 | tf_op jit(solution)/shard_map/all_to_all | solution.py:480
  187.8 4.2 %shard_map.227.comb_own = bf16[256,1152]{1,0:T(8,128)(2,1)} custom-call(s32[5]{0:T(128)} %stack.35.pos, bf16[256,1280]{1,0:T(8,128)(2,1)} %get-tuple-element.78.tab_t, bf16[16,656,128]{2,1,0:T(8,128)(2,1)} %all-to-all-done.4.got), custom_call_target="tpu_custom_call" | custom-call | flops 1000 | bytes 1000 | tf_op jit(solution)/shard_map/pallas_call | solution.py:63
  191.9 3.5 %collective-permute-start.17 = (bf16[256,1152]{1,0:T(8,128)(2,1)}, bf16[256,1152]{1,0:T(8,128)(2,1)}, u32[]{:S(2)}, u32[]{:S(2)}) collective-permute-start(bf16[256,1152]{1,0:T(8,128)(2,1)} %shard_map.227.comb_own), channel_id=1, source_target_pairs={{0,1},{1,0},{2,3},{3,2},{4,5},{5,4},{6,7},{7,6},{8,9},{9,8},{10,11... | collective-permute-start | bytes 1769480 | tf_op jit(solution)/shard_map/ppermute | solution.py:476
  195.4 2.6 shard_map.228
  198.0 7.1 %collective-permute-done.17.comb_oth = bf16[256,1152]{1,0:T(8,128)(2,1)} collective-permute-done((bf16[256,1152]{1,0:T(8,128)(2,1)}, bf16[256,1152]{1,0:T(8,128)(2,1)}, u32[]{:S(2)}, u32[]{:S(2)}) %collective-permute-start.17) | collective-permute-done | bytes 589856 | tf_op jit(solution)/shard_map/ppermute | solution.py:476
  205.1 12.1 %shard_map.229 = (f32[128,1024]{1,0:T(8,128)}, f32[128,1024]{1,0:T(8,128)}, bf16[128,1024]{1,0:T(8,128)(2,1)}, bf16[32,208,128]{2,1,0:T(8,128)(2,1)}, bf16[32,20...) custom-call(s32[5]{0:T(128)} %stack.35.pos, bf16[256,1152]{1,0:T(8,128)(2,1)} %shard_map.227.comb_own, ...), custom_call_target="tpu_custom_call" | custom-call | flops 1000 | bytes 1000 | tf_op jit(solution)/shard_map/pallas_call | solution.py:63
  218.0 3.2 %collective-permute-start.19 = (f32[8,128]{1,0:T(8,128)S(1)}, f32[8,128]{1,0:T(8,128)S(1)}, u32[]{:S(2)}, u32[]{:S(2)}) collective-permute-start(f32[8,128]{1,0:T(8,128)S(1)} %slice_add_fusion), channel_id=1, source_target_pairs={{0,1},{1,0},{2,3},{3,2},{4,5},{5,4},{6,7},{7,6},{8,9},{9,8},{10,11... | collective-permute-start | bytes 12296 | tf_op jit(solution)/shard_map/ppermute | solution.py:476
  221.2 1.9 collective-permute-done.19
  224.6 1.3 pad_maximum_fusion
  226.0 1.6 collective-permute-start.21
  227.5 4.1 %shard_map.230 = (f32[128,1024]{1,0:T(8,128)}, bf16[128,1024]{1,0:T(8,128)(2,1)}) custom-call(s32[5]{0:T(128)} %stack.35.pos, bf16[256,1280]{1,0:T(8,128)(2,1)} %get-tuple-element.78.tab_t, bf16[16,640,128]{2,1,0:T(8,128)(2,1)} %all-to-all-done.3.got, f32[256,1024]{1,0:T(8,128)} %get-tuple-element.105.middle), custom_call_target="tpu_custom_call" | custom-call | flops 1000 | bytes 1000 | tf_op jit(solution)/shard_map/pallas_call | solution.py:63
  231.6 7.1 %all-to-all-start.5 = ((bf16[16,192,128]{2,1,0:T(8,128)(2,1)}), bf16[16,192,128]{2,1,0:T(8,128)(2,1)}, u32[]{:S(2)}, u32[]{:S(2)}) async-start(bf16[16,192,128]{2,1,0:T(8,128)(2,1)} %shard_map.228), calls=%async_computation.5 | async-start | bytes 1572864 | tf_op jit(solution)/shard_map/all_to_all | solution.py:480
  238.7 10.4 %collective-permute-done.21 = bf16[16,224,128]{2,1,0:T(8,128)(2,1)} collective-permute-done((bf16[16,224,128]{2,1,0:T(8,128)(2,1)}, bf16[16,224,128]{2,1,0:T(8,128)(2,1)}, u32[]{:S(2)}, u32[]{:S(2)}) %collective-permute-start.21) | collective-permute-done | bytes 917536 | tf_op jit(solution)/shard_map/ppermute | solution.py:476
  249.9 1.8 add_convert_fusion
  253.8 5.8 %all-to-all-start.6 = ((bf16[16,224,128]{2,1,0:T(8,128)(2,1)}), bf16[16,224,128]{2,1,0:T(8,128)(2,1)}, u32[]{:S(2)}, u32[]{:S(2)}) async-start(bf16[16,224,128]{2,1,0:T(8,128)(2,1)} %pad_maximum_fusion.1), calls=%async_computation.6 | async-start | bytes 1835008 | tf_op jit(solution)/shard_map/all_to_all | solution.py:480
  259.6 3.3 %collective-permute-start.23 = (bf16[128,1024]{1,0:T(8,128)(2,1)S(1)}, bf16[128,1024]{1,0:T(8,128)(2,1)S(1)}, u32[]{:S(2)}, u32[]{:S(2)}) collective-permute-start(bf16[128,1024]{1,0:T(8,128)(2,1)S(1)} %copy-done.18), channel_id=1, source_target_pairs={{0,1},{1,0},{2,3},{3,2},{4,5},{5,4},{6,7},{7,6},{8,9},{9,8},{10,11... | collective-permute-start | bytes 786440 | tf_op jit(solution)/shard_map/ppermute | solution.py:476
  263.2 7.2 %collective-permute-done.23.part_oth = bf16[128,1024]{1,0:T(8,128)(2,1)S(1)} collective-permute-done((bf16[128,1024]{1,0:T(8,128)(2,1)S(1)}, bf16[128,1024]{1,0:T(8,128)(2,1)S(1)}, u32[]{:S(2)}, u32[]{:S(2)}) %collective-permute-start.23) | collective-permute-done | bytes 262176 | tf_op jit(solution)/shard_map/ppermute | solution.py:476
  271.1 2.5 shard_map.231
  273.6 2.5 shard_map.233
  276.1 1.9 add_convert_fusion.5
  278.0 1.9 shard_map.232
  (100 shorter events, 22.9 us)
Async XLA Ops:
  0.6 15.2 %copy-start.5 = (bf16[16,32,256]{2,1,0:T(8,128)(2,1)S(1)}, bf16[16,32,256]{2,1,0:T(8,128)(2,1)}, u32[]{:S(2)}) copy-start(bf16[16,32,256]{2,1,0:T(8,128)(2,1)} %param.23) | copy-start | bytes 786436
  0.7 20.6 %collective-permute-start = (bf16[128,1024]{1,0:T(8,128)(2,1)}, bf16[128,1024]{1,0:T(8,128)(2,1)S(1)}, u32[]{:S(2)}, u32[]{:S(2)}) collective-permute-start(bf16[128,1024]{1,0:T(8,128)(2,1)} %cot_own.1), channel_id=1, source_target_pairs={{0,1},{1,0},{2,3},{3,2},{4,5},{5,4},{6,7},{7,6},{8,9},{9,8},{10,11... | collective-permute-start | bytes 786440 | tf_op jit(solution)/shard_map/ppermute | solution.py:476
  4.0 17.2 %collective-permute-start.1 = (bf16[128,1024]{1,0:T(8,128)(2,1)}, bf16[128,1024]{1,0:T(8,128)(2,1)S(1)}, u32[]{:S(2)}, u32[]{:S(2)}) collective-permute-start(bf16[128,1024]{1,0:T(8,128)(2,1)} %tok.1), channel_id=1, source_target_pairs={{0,1},{1,0},{2,3},{3,2},{4,5},{5,4},{6,7},{7,6},{8,9},{9,8},{10,11... | collective-permute-start | bytes 786440 | tf_op jit(solution)/shard_map/ppermute | solution.py:476
  6.6 9.6 %copy-start.6 = (bf16[16,32,256]{2,1,0:T(8,128)(2,1)S(1)}, bf16[16,32,256]{2,1,0:T(8,128)(2,1)}, u32[]{:S(2)}) copy-start(bf16[16,32,256]{2,1,0:T(8,128)(2,1)} %param.24) | copy-start | bytes 786436
  7.6 9.0 %copy-start.7 = (bf16[16,32,256]{2,1,0:T(8,128)(2,1)S(1)}, bf16[16,32,256]{2,1,0:T(8,128)(2,1)}, u32[]{:S(2)}) copy-start(bf16[16,32,256]{2,1,0:T(8,128)(2,1)} %param.25) | copy-start | bytes 786436
  7.7 22.7 %all-to-all-start = ((bf16[16,16,1664]{2,1,0:T(8,128)(2,1)}), bf16[16,16,1664]{2,1,0:T(8,128)(2,1)}, u32[]{:S(2)}, u32[]{:S(2)}) async-start(bf16[16,16,1664]{2,1,0:T(8,128)(2,1)} %broadcast_in_dim.26), calls=%async_computation | async-start | bytes 1703936 | tf_op jit(solution)/shard_map/all_to_all | solution.py:480
  16.3 1.7 copy-start.8
  21.9 5.0 %copy-start.16 = (bf16[128,1024]{1,0:T(8,128)(2,1)}, bf16[128,1024]{1,0:T(8,128)(2,1)S(1)}, u32[]{:S(2)}) copy-start(bf16[128,1024]{1,0:T(8,128)(2,1)S(1)} %collective-permute-done.1.tok_oth) | copy-start | bytes 786436
  30.3 2.7 collective-permute-start.3
  30.3 21.6 %collective-permute-start.2 = (bf16[16,16,1664]{2,1,0:T(8,128)(2,1)}, bf16[16,16,1664]{2,1,0:T(8,128)(2,1)S(1)}, u32[]{:S(2)}, u32[]{:S(2)}) collective-permute-start(bf16[16,16,1664]{2,1,0:T(8,128)(2,1)} %all-to-all-done.w_a), channel_id=1, source_target_pairs={{0,64},{64,0},{1,65},{65,1},{2,66},{66,2},{3,67},{67,3},{4,68},{68... | collective-permute-start | bytes 2555912 | tf_op jit(solution)/shard_map/ppermute | solution.py:476
  33.1 50.9 %all-to-all-start.2 = ((bf16[16,832,128]{2,1,0:T(8,128)(2,1)}), bf16[16,832,128]{2,1,0:T(8,128)(2,1)}, u32[]{:S(2)}, u32[]{:S(2)}) async-start(bf16[16,832,128]{2,1,0:T(8,128)(2,1)} %get-tuple-element.90), calls=%async_computation.2 | async-start | bytes 6815744 | tf_op jit(solution)/shard_map/all_to_all | solution.py:480
  51.9 0.9 copy-start.9
  52.8 2.5 collective-permute-start.4
  62.9 15.8 %collective-permute-start.5 = (bf16[256,1024]{1,0:T(8,128)(2,1)}, bf16[256,1024]{1,0:T(8,128)(2,1)}, u32[]{:S(2)}, u32[]{:S(2)}) collective-permute-start(bf16[256,1024]{1,0:T(8,128)(2,1)} %get-tuple-element.85.part_own), channel_id=1, source_target_pairs={{0,1},{1,0},{2,3},{3,2},{4,5},{5,4},{6,7},{7,6},{8,9},{9,8},{10,11... | collective-permute-start | bytes 1572872 | tf_op jit(solution)/shard_map/ppermute | solution.py:476
  83.9 48.7 %all-to-all-start.1 = ((bf16[16,656,128]{2,1,0:T(8,128)(2,1)}), bf16[16,656,128]{2,1,0:T(8,128)(2,1)}, u32[]{:S(2)}, u32[]{:S(2)}) async-start(bf16[16,656,128]{2,1,0:T(8,128)(2,1)} %get-tuple-element.89), calls=%async_computation.1 | async-start | bytes 5373952 | tf_op jit(solution)/shard_map/all_to_all | solution.py:480
  96.9 23.1 %copy-start.3 = (bf16[16,96,128]{2,1,0:T(8,128)(2,1)}, bf16[16,96,128]{2,1,0:T(8,128)(2,1)S(1)}, u32[]{:S(2)}) copy-start(bf16[16,96,128]{2,1,0:T(8,128)(2,1)S(1)} %get-tuple-element.143.a0) | copy-start | bytes 1179652
  96.9 19.8 %collective-permute-start.8 = (bf16[16,96,128]{2,1,0:T(8,128)(2,1)S(1)}, bf16[16,96,128]{2,1,0:T(8,128)(2,1)S(1)}, u32[]{:S(2)}, u32[]{:S(2)}) collective-permute-start(bf16[16,96,128]{2,1,0:T(8,128)(2,1)S(1)} %get-tuple-element.142), channel_id=1, source_target_pairs={{0,65},{65,0},{1,64},{64,1},{2,67},{67,2},{3,66},{66,3},{4,69},{69... | collective-permute-start | bytes 1179656 | tf_op jit(solution)/shard_map/ppermute | solution.py:475
  100.0 16.7 %collective-permute-start.7 = (bf16[16,96,128]{2,1,0:T(8,128)(2,1)S(1)}, bf16[16,96,128]{2,1,0:T(8,128)(2,1)S(1)}, u32[]{:S(2)}, u32[]{:S(2)}) collective-permute-start(bf16[16,96,128]{2,1,0:T(8,128)(2,1)S(1)} %get-tuple-element.142), channel_id=1, source_target_pairs={{0,1},{1,0},{2,3},{3,2},{4,5},{5,4},{6,7},{7,6},{8,9},{9,8},{10,11... | collective-permute-start | bytes 1179656 | tf_op jit(solution)/shard_map/ppermute | solution.py:476
  100.6 16.8 %collective-permute-start.6 = (bf16[16,96,128]{2,1,0:T(8,128)(2,1)S(1)}, bf16[16,96,128]{2,1,0:T(8,128)(2,1)S(1)}, u32[]{:S(2)}, u32[]{:S(2)}) collective-permute-start(bf16[16,96,128]{2,1,0:T(8,128)(2,1)S(1)} %get-tuple-element.143.a0), channel_id=1, source_target_pairs={{0,64},{64,0},{1,65},{65,1},{2,66},{66,2},{3,67},{67,3},{4,68},{68... | collective-permute-start | bytes 1179656 | tf_op jit(solution)/shard_map/ppermute | solution.py:476
  101.1 16.3 %collective-permute-start.9 = (bf16[16,96,128]{2,1,0:T(8,128)(2,1)S(1)}, bf16[16,96,128]{2,1,0:T(8,128)(2,1)S(1)}, u32[]{:S(2)}, u32[]{:S(2)}) collective-permute-start(bf16[16,96,128]{2,1,0:T(8,128)(2,1)S(1)} %get-tuple-element.143.a0), channel_id=1, source_target_pairs={{0,2},{2,0},{1,3},{3,1},{4,6},{6,4},{5,7},{7,5},{8,10},{10,8},{9,1... | collective-permute-start | bytes 1179656 | tf_op jit(solution)/shard_map/ppermute | solution.py:476
  116.7 0.8 copy-start.10
  116.7 1.7 collective-permute-start.12
  116.7 1.7 copy-start.11
  116.7 2.3 collective-permute-start.11
  117.4 1.6 copy-start.12
  117.4 2.5 collective-permute-start.10
  117.5 1.5 copy-start.13
  118.5 0.8 copy-start.14
  119.2 0.8 copy-start.15
  144.7 37.6 %all-to-all-start.4 = ((bf16[16,656,128]{2,1,0:T(8,128)(2,1)}), bf16[16,656,128]{2,1,0:T(8,128)(2,1)}, u32[]{:S(2)}, u32[]{:S(2)}) async-start(bf16[16,656,128]{2,1,0:T(8,128)(2,1)} %get-tuple-element.99), calls=%async_computation.4 | async-start | bytes 5373952 | tf_op jit(solution)/shard_map/all_to_all | solution.py:480
  159.0 3.6 %collective-permute-start.13 = (bf16[2,2,16,96,128]{4,3,2,1,0:T(8,128)(2,1)}, bf16[2,2,16,96,128]{4,3,2,1,0:T(8,128)(2,1)S(1)}, u32[]{:S(2)}, u32[]{:S(2)}) collective-permute-start(bf16[2,2,16,96,128]{4,3,2,1,0:T(8,128)(2,1)} %get-tuple-element.97), channel_id=1, source_target_pairs={{0,2},{2,0},{1,3},{3,1},{4,6},{6,4},{5,7},{7,5},{8,10},{10,8},{9,1... | collective-permute-start | bytes 4718600 | tf_op jit(solution)/shard_map/ppermute | solution.py:476
  162.6 3.0 %copy-start = (bf16[2,2,16,96,128]{4,3,2,1,0:T(8,128)(2,1)}, bf16[2,2,16,96,128]{4,3,2,1,0:T(8,128)(2,1)S(1)}, u32[]{:S(2)}) copy-start(bf16[2,2,16,96,128]{4,3,2,1,0:T(8,128)(2,1)S(1)} %collective-permute-done.13.got) | copy-start | bytes 4718596
  165.6 22.2 %collective-permute-start.14 = (bf16[16,96,128]{2,1,0:T(8,128)(2,1)}, bf16[16,96,128]{2,1,0:T(8,128)(2,1)}, u32[]{:S(2)}, u32[]{:S(2)}) collective-permute-start(bf16[16,96,128]{2,1,0:T(8,128)(2,1)} %get-tuple-element.146), channel_id=1, source_target_pairs={{0,64},{64,0},{1,65},{65,1},{2,66},{66,2},{3,67},{67,3},{4,68},{68... | collective-permute-start | bytes 1179656 | tf_op jit(solution)/shard_map/ppermute | solution.py:476
  167.2 24.7 %collective-permute-start.16 = (bf16[16,96,128]{2,1,0:T(8,128)(2,1)}, bf16[16,96,128]{2,1,0:T(8,128)(2,1)}, u32[]{:S(2)}, u32[]{:S(2)}) collective-permute-start(bf16[16,96,128]{2,1,0:T(8,128)(2,1)} %get-tuple-element.144), channel_id=1, source_target_pairs={{0,65},{65,0},{1,64},{64,1},{2,67},{67,2},{3,66},{66,3},{4,69},{69... | collective-permute-start | bytes 1179656 | tf_op jit(solution)/shard_map/ppermute | solution.py:475
  169.4 22.6 %collective-permute-start.15 = (bf16[16,96,128]{2,1,0:T(8,128)(2,1)S(1)}, bf16[16,96,128]{2,1,0:T(8,128)(2,1)}, u32[]{:S(2)}, u32[]{:S(2)}) collective-permute-start(bf16[16,96,128]{2,1,0:T(8,128)(2,1)S(1)} %get-tuple-element.145), channel_id=1, source_target_pairs={{0,1},{1,0},{2,3},{3,2},{4,5},{5,4},{6,7},{7,6},{8,9},{9,8},{10,11... | collective-permute-start | bytes 1179656 | tf_op jit(solution)/shard_map/ppermute | solution.py:476
  182.3 42.0 %all-to-all-start.3 = ((bf16[16,640,128]{2,1,0:T(8,128)(2,1)}), bf16[16,640,128]{2,1,0:T(8,128)(2,1)}, u32[]{:S(2)}, u32[]{:S(2)}) async-start(bf16[16,640,128]{2,1,0:T(8,128)(2,1)} %shard_map.226), calls=%async_computation.3 | async-start | bytes 5242880 | tf_op jit(solution)/shard_map/all_to_all | solution.py:480
  191.9 13.1 %collective-permute-start.17 = (bf16[256,1152]{1,0:T(8,128)(2,1)}, bf16[256,1152]{1,0:T(8,128)(2,1)}, u32[]{:S(2)}, u32[]{:S(2)}) collective-permute-start(bf16[256,1152]{1,0:T(8,128)(2,1)} %shard_map.227.comb_own), channel_id=1, source_target_pairs={{0,1},{1,0},{2,3},{3,2},{4,5},{5,4},{6,7},{7,6},{8,9},{9,8},{10,11... | collective-permute-start | bytes 1769480 | tf_op jit(solution)/shard_map/ppermute | solution.py:476
  217.2 7.2 %collective-permute-start.18 = (bf16[32,208,128]{2,1,0:T(8,128)(2,1)}, bf16[32,208,128]{2,1,0:T(8,128)(2,1)S(1)}, u32[]{:S(2)}, u32[]{:S(2)}) collective-permute-start(bf16[32,208,128]{2,1,0:T(8,128)(2,1)} %get-tuple-element.119), channel_id=1, source_target_pairs={{0,2},{2,0},{1,3},{3,1},{4,6},{6,4},{5,7},{7,5},{8,10},{10,8},{9,1... | collective-permute-start | bytes 5111816 | tf_op jit(solution)/shard_map/ppermute | solution.py:476
  218.0 5.1 %collective-permute-start.19 = (f32[8,128]{1,0:T(8,128)S(1)}, f32[8,128]{1,0:T(8,128)S(1)}, u32[]{:S(2)}, u32[]{:S(2)}) collective-permute-start(f32[8,128]{1,0:T(8,128)S(1)} %slice_add_fusion), channel_id=1, source_target_pairs={{0,1},{1,0},{2,3},{3,2},{4,5},{5,4},{6,7},{7,6},{8,9},{9,8},{10,11... | collective-permute-start | bytes 12296 | tf_op jit(solution)/shard_map/ppermute | solution.py:476
  223.1 1.2 collective-permute-start.20
  224.4 1.6 copy-start.1
  226.0 23.1 %collective-permute-start.21 = (bf16[16,224,128]{2,1,0:T(8,128)(2,1)}, bf16[16,224,128]{2,1,0:T(8,128)(2,1)}, u32[]{:S(2)}, u32[]{:S(2)}) collective-permute-start(bf16[16,224,128]{2,1,0:T(8,128)(2,1)} %pad_maximum_fusion), channel_id=1, source_target_pairs={{0,64},{64,0},{1,65},{65,1},{2,66},{66,2},{3,67},{67,3},{4,68},{68... | collective-permute-start | bytes 2752520 | tf_op jit(solution)/shard_map/ppermute | solution.py:476
  231.6 18.3 %copy-start.2 = (bf16[32,208,128]{2,1,0:T(8,128)(2,1)S(1)}, bf16[32,208,128]{2,1,0:T(8,128)(2,1)}, u32[]{:S(2)}) copy-start(bf16[32,208,128]{2,1,0:T(8,128)(2,1)} %copy-done.1) | copy-start | bytes 5111812
  231.6 22.1 %all-to-all-start.5 = ((bf16[16,192,128]{2,1,0:T(8,128)(2,1)}), bf16[16,192,128]{2,1,0:T(8,128)(2,1)}, u32[]{:S(2)}, u32[]{:S(2)}) async-start(bf16[16,192,128]{2,1,0:T(8,128)(2,1)} %shard_map.228), calls=%async_computation.5 | async-start | bytes 1572864 | tf_op jit(solution)/shard_map/all_to_all | solution.py:480
  251.7 7.9 %copy-start.18 = (bf16[128,1024]{1,0:T(8,128)(2,1)S(1)}, bf16[128,1024]{1,0:T(8,128)(2,1)}, u32[]{:S(2)}) copy-start(bf16[128,1024]{1,0:T(8,128)(2,1)} %get-tuple-element.128) | copy-start | bytes 786436
  253.8 24.2 %all-to-all-start.6 = ((bf16[16,224,128]{2,1,0:T(8,128)(2,1)}), bf16[16,224,128]{2,1,0:T(8,128)(2,1)}, u32[]{:S(2)}, u32[]{:S(2)}) async-start(bf16[16,224,128]{2,1,0:T(8,128)(2,1)} %pad_maximum_fusion.1), calls=%async_computation.6 | async-start | bytes 1835008 | tf_op jit(solution)/shard_map/all_to_all | solution.py:480
  259.6 10.8 %collective-permute-start.23 = (bf16[128,1024]{1,0:T(8,128)(2,1)S(1)}, bf16[128,1024]{1,0:T(8,128)(2,1)S(1)}, u32[]{:S(2)}, u32[]{:S(2)}) collective-permute-start(bf16[128,1024]{1,0:T(8,128)(2,1)S(1)} %copy-done.18), channel_id=1, source_target_pairs={{0,1},{1,0},{2,3},{3,2},{4,5},{5,4},{6,7},{7,6},{8,9},{9,8},{10,11... | collective-permute-start | bytes 786440 | tf_op jit(solution)/shard_map/ppermute | solution.py:476
  262.9 13.2 %collective-permute-start.22 = (bf16[128,1024]{1,0:T(8,128)(2,1)}, bf16[128,1024]{1,0:T(8,128)(2,1)}, u32[]{:S(2)}, u32[]{:S(2)}) collective-permute-start(bf16[128,1024]{1,0:T(8,128)(2,1)} %get-tuple-element.124), channel_id=1, source_target_pairs={{0,1},{1,0},{2,3},{3,2},{4,5},{5,4},{6,7},{7,6},{8,9},{9,8},{10,11... | collective-permute-start | bytes 786440 | tf_op jit(solution)/shard_map/ppermute | solution.py:476
  (2 other events, 1.4 us)

commit v3 on v2

--- a/solution.py
+++ b/solution.py
@@ -20,14 +20,13 @@
 EXT = D + 128
 ROWS = 8 * CAP
 PACK = 1664
-W_ROWS = 208
 NORM_EPS = 1e-06
 ROPE_BASE = 10000.0
 SCALE = 0.125
 PLANE = ("x", "z")
 NT = (((1,), (1,)), ((), ()))
 TN = (((0,), (0,)), ((), ()))
-VMEM_BYTES = 65000 * 1024
+VMEM_BYTES = 65472 * 1024
 
 
 def mo(value, by):
@@ -47,7 +46,7 @@
     return lax.broadcasted_iota(jnp.int32, shape, dim)
 
 
-def call(kernel, outs, args, scratch=(), grid=None, in_specs=None, out_specs=None, us=1, late_from=None, prefetch=False):
+def call(kernel, outs, args, scratch=(), grid=None, in_specs=None, out_specs=None, us=1, late_from=None, late_outs=0, prefetch=False):
     smem = pl.BlockSpec(memory_space=pltpu.SMEM)
     params = pltpu.CompilerParams(vmem_limit_bytes=VMEM_BYTES)
     out_shape = [jax.ShapeDtypeStruct(shape, kind) for shape, kind in outs]
@@ -59,7 +58,7 @@
         vmem = pl.BlockSpec(memory_space=pltpu.VMEM)
         early = len(args) if late_from is None else late_from
         in_specs = [smem] + [vmem] * (early - 1) + [pl.BlockSpec(memory_space=pl.ANY)] * (len(args) - early)
-        out_specs = [vmem] * len(outs)
+        out_specs = [vmem] * (len(outs) - late_outs) + [pl.BlockSpec(memory_space=pl.ANY)] * late_outs
         return pl.pallas_call(
             kernel,
             out_shape=out_shape,
@@ -91,7 +90,46 @@
     )(*args)
 
 
-def route_kernel(pos, routes, cot_own, cot_oth, packed, tab, tab_t, mask_out, grad, sent, turned):
+def copies(pairs, sems, first=0):
+    return [pltpu.make_async_copy(src, dst, sems.at[first + i]) for i, (src, dst) in enumerate(pairs)]
+
+
+def start(loads):
+    for load in loads:
+        load.start()
+
+
+def wait(loads):
+    for load in loads:
+        load.wait()
+
+
+def place_rows(w, pieces, late, core):
+    at = ((late, core), (1 - late, core), (late, 1 - core), (1 - late, 1 - core))
+    return [(src, w.at[at_late, :, at_core]) for src, (at_late, at_core) in zip(pieces, at)]
+
+
+def flat(w, first, last):
+    return w[:, :, :, :, first:last].reshape(D, last - first)
+
+
+def pack_kernel(pos, w_query, w_key, w_value, w_out, router, gain_one, gain_two, out):
+    at = iota((128, 128), 0)
+    rest = jnp.zeros((1, 112), f32)
+    first, second = (jnp.concatenate([gain[...].astype(f32), rest], axis=1) for gain in (gain_one, gain_two))
+    gains = pick(at, first, second)
+    gains = gains.T[:16]
+    wide = jnp.concatenate([router[...].astype(f32), jnp.zeros((16, 96), f32)], axis=1)
+    small = (wide + pltpu.roll(gains, EXPERTS, 1)).astype(bf16)
+    for i in range(16):
+        out[i, :, :512] = w_query[...]
+        out[i, :, 512:768] = w_key[...]
+        out[i, :, 768:1024] = w_value[...]
+        out[i, :, 1024:1536] = w_out[...]
+        out[i, :, 1536:] = small
+
+
+def route_kernel(pos, routes, tab, tab_t, mask_out, turned):
     half = pos[0]
     named = routes[...]
     lane = iota((SEQ, 128), 1)
@@ -109,11 +147,15 @@
     for n in range(SLOTS // 128):
         cols = slice(n * 128, (n + 1) * 128)
         tab_t[:, cols] = tab[cols, :].astype(f32).T.astype(bf16)
+
+
+def dispatch_kernel(pos, tab, cot_own, cot_oth, packed, grad, sent):
+    half = pos[0]
+    sent[:, ROWS : ROWS + 192, :] = packed[...]
     grad[pl.ds(mo(half * HALF, HALF), HALF), :] = cot_own[...]
     grad[pl.ds(mo((1 - half) * HALF, HALF), HALF), :] = cot_oth[...]
     for n in range(4):
         spread_blocks(sent, n, dot(tab[...], grad[:, n * 256 : (n + 1) * 256]).astype(bf16), 16)
-    sent[:, ROWS : ROWS + 192, :] = packed[...]
 
 
 def spread_blocks(dst, n, value, peers):
@@ -148,31 +190,24 @@
 
 
 def attn_kernel(
-    pos, tok_own, tok_oth, w_a, w_b, w_c, w_d, cos, sin,
-    rows, w, w_o, aux, attn_in, q_out, k_out, v_out, ctx, lse_out, part, small,
+    pos, tok_own, tok_oth, cos, sin, w_a, w_b, w_c, w_d,
+    part, rows_at, aux_at, attn_in_at, q_at, k_at, v_at, ctx_at, lse_at,
+    rows, aux, attn_in, q_out, k_out, v_out, ctx, lse_out, w, sems,
 ):
     half, core, late = pos[0], pos[1], pos[2]
+    loads = copies(place_rows(w, (w_a, w_b, w_c, w_d), late, core), sems)
+    start(loads)
     rows[pl.ds(mo(half * HALF, HALF), HALF), :] = tok_own[...]
     rows[pl.ds(mo((1 - half) * HALF, HALF), HALF), :] = tok_oth[...]
-    for src, at_late, at_core in (
-        (w_a, late, core),
-        (w_b, 1 - late, core),
-        (w_c, late, 1 - core),
-        (w_d, 1 - late, 1 - core),
-    ):
-        for i in range(16):
-            at = pl.ds(mo((at_late * 16 + i) * 32 + at_core * 16, 16), 16)
-            w[at, :] = src[i, :, :1024]
-            w_o[at, :] = src[i, :, 1024:1536]
-            small[at, :] = src[i, :, 1536:PACK]
-    aux[...] = small[...].astype(f32).T
     x = rows[...].astype(f32)
-    factor = lax.rsqrt(jnp.mean(x * x, axis=1, keepdims=True) + NORM_EPS)
-    attn_in[...] = (x * factor * aux[32:33, :]).astype(bf16)
+    normed = x * lax.rsqrt(jnp.mean(x * x, axis=1, keepdims=True) + NORM_EPS)
+    wait(loads)
+    aux[...] = flat(w, 1536, PACK).astype(f32).T
+    attn_in[...] = (normed * aux[32:33, :]).astype(bf16)
     low32 = iota((SEQ, 256), 1) % 64 < 32
     low = iota((SEQ, 128), 1) < 64
     for n in range(4):
-        lin = dot(attn_in[...], w[:, n * 256 : (n + 1) * 256])
+        lin = dot(attn_in[...], flat(w, n * 256, (n + 1) * 256))
         if n < 3:
             lin = lin * cos[...] + swap_halves(lin, low32) * sin[...]
         if n < 2:
@@ -182,6 +217,9 @@
             for m in range(4):
                 tile = lin[:, (m // 2) * 128 : (m // 2) * 128 + 128]
                 dst[:, m * 128 : (m + 1) * 128] = doubled(tile, low, m % 2).astype(bf16)
+    pairs = [(rows, rows_at), (aux, aux_at), (attn_in, attn_in_at), (q_out, q_at), (k_out, k_at), (v_out, v_at)]
+    stores = copies(pairs, sems, 4)
+    start(stores)
     allowed = iota((2 * SEQ, SEQ), 0) % SEQ >= iota((2 * SEQ, SEQ), 1)
     for m in range(4):
         cols = slice(m * 128, (m + 1) * 128)
@@ -194,17 +232,25 @@
         probs = (raised * (1.0 / total)).astype(bf16)
         both = dot(probs, v_out[:, cols])
         ctx[:, cols] = jnp.where(low, both[:SEQ], both[SEQ:]).astype(bf16)
+    more = copies([(ctx, ctx_at), (lse_out, lse_at)], sems, 10)
+    start(more)
     for n in range(4):
         outs = slice(n * 256, (n + 1) * 256)
-        part[:, outs] = dot(ctx[...], w_o[outs, :], NT).astype(bf16)
-
-
-def mid_kernel(pos, rows, part_own, part_oth, aux, tab, mask, middle, moe_in, gates_out, sent, turned):
+        part[:, outs] = dot(ctx[...], w[n // 2, (n % 2) * 8 : (n % 2) * 8 + 8, :, :, 1024:1536].reshape(256, 512), NT).astype(bf16)
+    wait(stores + more)
+
+
+def mid_kernel(
+    pos, rows, part_own, part_oth, aux, tab, mask,
+    gates_out, middle_at, moe_in_at, sent_at, turned, middle, moe_in, sent, sems,
+):
     half = pos[0]
     value = rows[...].astype(f32) + (part_own[...].astype(f32) + part_oth[...].astype(f32))
     middle[...] = value
     factor = lax.rsqrt(jnp.mean(value * value, axis=1, keepdims=True) + NORM_EPS)
     moe_in[...] = (value * factor * aux[33:34, :]).astype(bf16)
+    moves = copies([(middle, middle_at), (moe_in, moe_in_at)], sems)
+    start(moves)
     logits = dot(moe_in[...], aux[...].astype(bf16), NT)
     chosen = jnp.where(mask[...] > 0.0, logits, -1e30)
     raised = jnp.exp(chosen - jnp.max(chosen, axis=1, keepdims=True)) * mask[...]
@@ -213,6 +259,10 @@
     turned[...] = gates.T
     for n in range(4):
         spread_blocks(sent, n, dot(tab[...], moe_in[:, n * 256 : (n + 1) * 256]).astype(bf16), 16)
+        at = slice(n * 160, (n + 1) * 160)
+        (move,) = copies([(sent.at[:, at], sent_at.at[:, at])], sems, 2 + n)
+        move.start()
+        moves.append(move)
     lane = iota((CAP, 128), 1)
     slots = jnp.zeros((CAP, 128), f32)
     for i in range(16):
@@ -225,6 +275,10 @@
         line = slots[i : i + 1, :]
         high = line.astype(bf16).astype(f32)
         sent[i, ROWS : ROWS + 16, :] = pick(at, high, line - high).astype(bf16)
+    at = slice(ROWS, ROWS + 16)
+    (move,) = copies([(sent.at[:, at], sent_at.at[:, at])], sems, 6)
+    move.start()
+    wait(moves + [move])
 
 
 def weights_kernel(pos, a0, a1, a2, a3, b0, b1, b2, b3, w_gate, w_up, w_down):
@@ -325,7 +379,7 @@
         out[:, cols] = dot(tab_t[...], held[:, cols]).astype(bf16)
 
 
-def finish_kernel(pos, tab_t, got, middle, own, sent, gathered, held):
+def finish_kernel(pos, tab_t, middle, got, own, sent, gathered, held):
     half = pos[0]
     gather_blocks(gathered, got, 16, 8)
     for n in range(4):
@@ -336,29 +390,24 @@
     sent[...] = held[pl.ds(mo((1 - half) * HALF, HALF), HALF), :].astype(bf16)
 
 
-def cut_rows(mine, sent, held, late, core, blocks):
-    for i in range(32):
-        at_late = late if i < 16 else 1 - late
-        for dst, at_core in ((mine, core), (sent, 1 - core)):
-            rows = pl.ds(mo((at_late * 16 + i % 16) * 32 + at_core * 16, 16), 16)
-            for b in range(blocks):
-                dst[i, b * 16 : (b + 1) * 16, :] = held[rows, b * 128 : (b + 1) * 128]
+def put(pack, first, value):
+    width = value.shape[1]
+    pack[:, :, :, :, first : first + width] = value.astype(bf16).reshape(2, 16, 2, 16, width)
 
 
 def back_kernel(
     pos, comb_own, comb_oth, middle, moe_in, gates, aux, grad,
-    w_o_at, ctx_at, q_at, k_at, v_at, lse_at, cos_at, sin_at, attn_in_at, w_at, rows_at,
-    mg_own, part_own, part_sent, mine, sent, gains,
-    w_o, ctx, q, k, v, lse, cos, sin, attn_in, w, rows, sems, mg, aog, pack, cgrad, dlin, apart,
+    w_a, w_b, w_c, w_d, ctx_at, q_at, k_at, v_at, lse_at, cos_at, sin_at, attn_in_at, rows_at,
+    part_sent, gains, mg_own, part_own, mine, sent,
+    w, ctx, q, k, v, lse, cos, sin, attn_in, rows, sems, mg, aog, pack, cgrad, dlin, apart,
 ):
     half, core, late = pos[0], pos[1], pos[2]
-    pairs = (
-        (w_o_at, w_o), (ctx_at, ctx), (q_at, q), (k_at, k), (v_at, v), (lse_at, lse), (cos_at, cos), (sin_at, sin),
-        (attn_in_at, attn_in), (w_at, w), (rows_at, rows),
-    )
-    loads = [pltpu.make_async_copy(src, dst, sems.at[i]) for i, (src, dst) in enumerate(pairs)]
-    for load in loads:
-        load.start()
+    pairs = place_rows(w, (w_a, w_b, w_c, w_d), late, core) + [
+        (ctx_at, ctx), (q_at, q), (k_at, k), (v_at, v), (lse_at, lse), (cos_at, cos), (sin_at, sin),
+        (attn_in_at, attn_in), (rows_at, rows),
+    ]
+    loads = copies(pairs, sems)
+    start(loads)
     gg = comb_own[:, D:EXT].astype(f32) + comb_oth[:, D:EXT].astype(f32)
     gg = gg + pltpu.roll(gg, 96, 1)
     gate = gates[...]
@@ -375,20 +424,21 @@
     mg[...] = grad[...].astype(f32) + factor * (
         inner - normed * jnp.mean(inner * normed, axis=1, keepdims=True)
     )
-    mg_own[...] = mg[pl.ds(mo(half * HALF, HALF), HALF), :]
+    own = pl.ds(mo(half * HALF, HALF), HALF)
+    stores = copies([(mg.at[own], mg_own)], sems, 13)
+    start(stores)
     aog[...] = mg[...].astype(bf16)
-    for load in loads[:2]:
-        load.wait()
+    wait(loads[:5])
     for n in range(2):
         cols = slice(n * 256, (n + 1) * 256)
-        cgrad[:, cols] = dot(aog[...], w_o[:, cols]).astype(bf16)
-        pack[:, 1024 + n * 256 : 1280 + n * 256] = dot(aog[...], ctx[:, cols], TN).astype(bf16)
+        cgrad[:, cols] = dot(aog[...], flat(w, 1024 + n * 256, 1280 + n * 256)).astype(bf16)
+        put(pack, 1024 + n * 256, dot(aog[...], ctx[:, cols], TN))
     router_grad = dot(lg_high, moe_in[...], TN) + dot(lg_low, moe_in[...], TN)
+    put(pack, 1536, jnp.where(iota((128, D), 0) == 33, gain_two, router_grad).T)
     low32 = iota((SEQ, 256), 1) % 64 < 32
     low = iota((SEQ, 128), 1) < 64
     allowed = iota((2 * SEQ, SEQ), 0) % SEQ >= iota((2 * SEQ, SEQ), 1)
-    for load in loads[2:]:
-        load.wait()
+    wait(loads[5:])
     for m in range(4):
         cols = slice(m * 128, (m + 1) * 128)
         qs = stacked(q[:, cols], low)
@@ -418,44 +468,92 @@
             lin = lin * cos[...] - swap_halves(lin, low32) * sin[...]
         lin = lin.astype(bf16)
         lows.append(lin)
-        pack[:, cols] = dot(attn_in[...], lin, TN).astype(bf16)
+        put(pack, n * 256, dot(attn_in[...], lin, TN))
+    pairs = [
+        (pack.at[at_late, :, at_core], dst.at[i])
+        for dst, at_core in ((sent, 1 - core), (mine, core))
+        for i, at_late in enumerate((late, 1 - late))
+    ]
+    moves = copies(pairs, sems, 14)
+    start(moves)
+    stores = stores + moves
     lows = jnp.concatenate(lows, axis=1)
     for n in range(4):
         cols = slice(n * 256, (n + 1) * 256)
-        apart[:, cols] = dot(lows, w[cols, :], NT)
-    part_own[...] = apart[pl.ds(mo(half * HALF, HALF), HALF), :]
+        block = w[n // 2, (n % 2) * 8 : (n % 2) * 8 + 8, :, :, :1024].reshape(256, 1024)
+        apart[:, cols] = dot(lows, block, NT)
+    moves = copies([(apart.at[own], part_own)], sems, 18)
+    start(moves)
     part_sent[...] = apart[pl.ds(mo((1 - half) * HALF, HALF), HALF), :].astype(bf16)
     x = rows[...].astype(f32)
     normed_one = x * lax.rsqrt(jnp.mean(x * x, axis=1, keepdims=True) + NORM_EPS)
     gain_one = jnp.sum(apart[...] * normed_one, axis=0, keepdims=True)
     lines = jnp.concatenate([gain_one[:, n * 128 : (n + 1) * 128] for n in range(8)], axis=0)
-    high = lines.astype(bf16).astype(f32)
-    gains[...] = jnp.concatenate([high, lines - high], axis=0).astype(bf16)
-    pack[:, 1536:PACK] = jnp.where(iota((128, D), 0) == 33, gain_two, router_grad).T.astype(bf16)
-    cut_rows(mine, sent, pack, late, core, 13)
-
-
-def input_kernel(pos, tok, aux, mg, part_own, part_oth, out):
+    gains[...] = lines
+    wait(stores + moves)
+
+
+def gain_lines(gain):
+    high = gain.astype(bf16).astype(f32)
+    return jnp.concatenate([high, (gain - high).astype(bf16).astype(f32)], axis=0)
+
+
+def halves(pairs, sems):
+    loads = []
+    for part in range(2):
+        at = slice(part * 8, part * 8 + 8)
+        loads.append(copies([(src.at[at], dst.at[at]) for src, dst in pairs], sems, part * len(pairs)))
+        start(loads[-1])
+    return loads
+
+
+def move_kernel(pos, g_own, g_yh, g_core, g_twist, mine_at, got_at, out, gain_out, mine, got, sems):
+    loads = halves([(mine_at.at[1], mine), (got_at.at[1], got)], sems)
+    lines = gain_lines((g_own[...] + g_yh[...]) + (g_core[...] + g_twist[...]))
+    gain_out[...] = lines
+    for part in range(2):
+        wait(loads[part])
+        at = slice(part * 8, part * 8 + 8)
+        out[at, :, :PACK] = (mine[at].astype(f32) + got[at].astype(f32)).astype(bf16)
+    for i in range(16):
+        out[i, :, PACK:] = lines.astype(bf16)
+
+
+def sum_kernel(pos, gain, mine_at, got_at, got_yl_at, out, mine, got, got_yl, sems):
+    loads = halves([(mine_at.at[0], mine), (got_at.at[0], got), (got_yl_at, got_yl)], sems)
+    for part in range(2):
+        wait(loads[part])
+        at = slice(part * 8, part * 8 + 8)
+        total = mine[at].astype(f32) + got[at].astype(f32) + got_yl[at, :, :PACK].astype(f32)
+        out[at, :, :PACK] = total.astype(bf16)
+    total = gain[...] + got_yl[0, :, PACK:].astype(f32)
+    lines = gain_lines(total[:8] + total[8:]).astype(bf16)
+    for i in range(16):
+        out[i, :, PACK:] = lines
+
+
+def rows_kernel(pos, tok, aux, mg, part_own, part_oth, out_own, out_oth, out, rows_out):
     x = tok[...].astype(f32)
     factor = lax.rsqrt(jnp.mean(x * x, axis=1, keepdims=True) + NORM_EPS)
     normed = x * factor
     inner = (part_own[...] + part_oth[...].astype(f32)) * aux[32:33, :]
     inner = factor * (inner - normed * jnp.mean(inner * normed, axis=1, keepdims=True))
     out[...] = (mg[...] + inner).astype(bf16)
+    rows_out[...] = (out_own[...] + out_oth[...].astype(f32)).astype(bf16)
 
 
 def final_kernel(pos, got, w_query, w_key, w_value, w_out, w_router, gain_two, gain_one):
     total = got[0].astype(f32)
     for i in range(1, 16):
         total = total + got[i].astype(f32)
-    for base, dst, blocks in ((0, w_query, 4), (4, w_key, 2), (6, w_value, 2), (8, w_out, 4)):
-        for b in range(blocks):
-            at = (base + b) * 16
-            dst[:, b * 128 : (b + 1) * 128] = total[at : at + 16, :]
-    w_router[...] = total[192:208, :32]
-    turned = jnp.concatenate([total[192:208, :], jnp.zeros((112, 128), f32)], axis=0).T
+    w_query[...] = total[:, :512]
+    w_key[...] = total[:, 512:768]
+    w_value[...] = total[:, 768:1024]
+    w_out[...] = total[:, 1024:1536]
+    w_router[...] = total[:, 1536 : 1536 + EXPERTS]
+    turned = jnp.concatenate([total[:, 1536:PACK], jnp.zeros((112, 128), f32)], axis=0).T
     gain_two[...] = turned[33:34, :16]
-    gains = total[208:216, :] + total[216:224, :]
+    gains = total[:8, PACK:] + total[8:, PACK:]
     at = pos[4]
     row = jnp.sum(jnp.where(iota((8, 128), 0) == at // 8, gains, 0.0), axis=0, keepdims=True)
     lanes = pltpu.roll(jnp.broadcast_to(row, (8, 128)), (128 - (at % 8) * 16) % 128, 1)
@@ -471,9 +569,15 @@
 
 
 def swap(value, axis):
+    if axis == "twist":
+        return lax.ppermute(value, ("c", "yh"), [(0, 3), (3, 0), (1, 2), (2, 1)])
     if axis == "diag":
         return lax.ppermute(value, ("yl", "yh"), [(0, 3), (3, 0), (1, 2), (2, 1)])
     return lax.ppermute(value, axis, [(0, 1), (1, 0)])
+
+
+def ring(value, axis, step):
+    return lax.ppermute(value, axis, [(i, (i + step) % 4) for i in range(4)])
 
 
 def plane(value):
@@ -512,34 +616,38 @@
 ):
     half, core, late = lax.axis_index("yh"), lax.axis_index("c"), lax.axis_index("yl")
     place = lax.axis_index("x") * 4 + lax.axis_index("z")
-    pos = jnp.stack([half, core, late, half * 16 + place, (late * 16 + place) * 2 + core]).astype(jnp.int32)
+    pos = jnp.stack([half, core, late, half * 16 + place, (late * 16 + place) * 2 + core, lax.axis_index("x"), lax.axis_index("z")]).astype(jnp.int32)
     cos, sin = rotary_tables()
 
-    packed = jnp.concatenate(
+    (packed,) = call(
+        pack_kernel,
+        [((16, 16, PACK), bf16)],
         [
-            query_weight, key_weight, value_weight, out_weight, router_weight,
-            attn_gain[:, None], moe_gain[:, None], jnp.zeros((16, 94), bf16),
+            pos, query_weight, key_weight, value_weight, out_weight, router_weight,
+            attn_gain.reshape(1, 16), moe_gain.reshape(1, 16),
         ],
-        axis=1,
-    )
-    w_a = plane(jnp.broadcast_to(packed[None], (16, 16, PACK)))
+        us=0,
+    )
+    w_a = plane(packed)
     tok_oth = swap(tokens, "yh")
     cot_oth = swap(cotangent, "yh")
-    cot_oth, tok_oth, cos, sin = lax.optimization_barrier((cot_oth, tok_oth, cos, sin))
 
     experts = jnp.stack([expert_gate, expert_up, expert_down])
     experts = experts.reshape(3, 16, 2, 16, 2, 128).transpose(3, 2, 0, 4, 1, 5).reshape(16, 192, 128)
-    tab, tab_t, mask, grad, cot_sent = call(
+    tab, tab_t, mask = call(
         route_kernel,
-        [
-            ((SLOTS, SEQ), bf16), ((SEQ, SLOTS), bf16), ((SEQ, 128), f32), ((SEQ, D), bf16),
-            ((16, ROWS + 192, 128), bf16),
-        ],
-        [pos, routes, cotangent, cot_oth, experts],
+        [((SLOTS, SEQ), bf16), ((SEQ, SLOTS), bf16), ((SEQ, 128), f32)],
+        [pos, routes],
         scratch=[pltpu.VMEM((128, SEQ), f32)],
-        us=5,
-    )
-    w_a = after(w_a, cot_sent)
+        us=0,
+    )
+    grad, cot_sent = call(
+        dispatch_kernel,
+        [((SEQ, D), bf16), ((16, ROWS + 192, 128), bf16)],
+        [pos, tab, cotangent, cot_oth, experts],
+        us=3,
+    )
+    w_a = after(w_a, experts, cot_sent, tok_oth)
     w_b = swap(w_a, "yl")
     w_c = swap(w_a, "c")
     w_d = swap(w_b, "c")
@@ -551,23 +659,30 @@
     pieces = pieces + [swap(piece, "c") for piece in pieces]
     w_gate, w_up, w_down = call(weights_kernel, [((D, 512), bf16)] * 3, [pos] + pieces, us=4)
 
-    rows, w, w_o, aux, attn_in, q, k, v, ctx, lse, part = call(
+    kept = [
+        ((SEQ, D), bf16), ((128, D), f32), ((SEQ, D), bf16), ((SEQ, 512), bf16), ((SEQ, 512), bf16),
+        ((SEQ, 512), bf16), ((SEQ, 512), bf16), ((4, 512, 128), f32),
+    ]
+    part, rows, aux, attn_in, q, k, v, ctx, lse = call(
         attn_kernel,
-        [
-            ((SEQ, D), bf16), ((D, D), bf16), ((D, 512), bf16), ((128, D), f32), ((SEQ, D), bf16),
-            ((SEQ, 512), bf16), ((SEQ, 512), bf16), ((SEQ, 512), bf16), ((SEQ, 512), bf16), ((4, 512, 128), f32),
-            ((SEQ, D), bf16),
-        ],
-        [pos, tokens, tok_oth, w_a, w_b, w_c, w_d, cos, sin],
-        scratch=[pltpu.VMEM((D, 128), bf16)],
+        [((SEQ, D), bf16)] + kept,
+        [pos, tokens, tok_oth, cos, sin, w_a, w_b, w_c, w_d],
+        late_from=5,
+        late_outs=8,
+        scratch=[pltpu.VMEM(shape, kind) for shape, kind in kept]
+        + [pltpu.VMEM((2, 16, 2, 16, PACK), bf16), pltpu.SemaphoreType.DMA((12,))],
         us=7,
     )
     part_oth = swap(part, "yh")
-    middle, moe_in, gates, x_sent = call(
+    kept = [((SEQ, D), f32), ((SEQ, D), bf16), ((16, ROWS + 16, 128), bf16)]
+    gates, middle, moe_in, x_sent = call(
         mid_kernel,
-        [((SEQ, D), f32), ((SEQ, D), bf16), ((SEQ, 128), f32), ((16, ROWS + 16, 128), bf16)],
+        [((SEQ, 128), f32)] + kept,
         [pos, rows, part, part_oth, aux, tab, mask],
-        scratch=[pltpu.VMEM((128, SEQ), f32)],
+        late_outs=3,
+        scratch=[pltpu.VMEM((128, SEQ), f32)]
+        + [pltpu.VMEM(shape, kind) for shape, kind in kept]
+        + [pltpu.SemaphoreType.DMA((7,))],
         us=3,
     )
     x_slots = plane(x_sent)
@@ -618,7 +733,7 @@
         out_specs=[by_col],
         us=0,
     )
-    dx_back = after(dx_back, e_yl)
+    dx_back = after(dx_back, e_yl, y)
     (comb,) = call(
         combine_kernel, [((SEQ, EXT), bf16)], [pos, tab_t, dx_back],
         scratch=[pltpu.VMEM((SLOTS, EXT), bf16)], us=0,
@@ -638,66 +753,79 @@
         us=0,
     )
     comb_oth = after(comb_oth, e_cat)
-    mg_own, part_own, part_sent, a_mine, a_sent, gains = call(
+    part_sent, gains, mg_own, part_own, a_mine, a_sent = call(
         back_kernel,
         [
-            ((HALF, D), f32), ((HALF, D), f32), ((HALF, D), bf16), ((32, W_ROWS, 128), bf16),
-            ((32, W_ROWS, 128), bf16), ((16, 128), bf16),
+            ((HALF, D), bf16), ((8, 128), f32), ((HALF, D), f32), ((HALF, D), f32),
+            ((2, 16, 16, PACK), bf16), ((2, 16, 16, PACK), bf16),
         ],
         [
             pos, comb, comb_oth, middle, moe_in, gates, aux, grad,
-            w_o, ctx, q, k, v, lse, cos, sin, attn_in, w, rows,
+            w_a, w_b, w_c, w_d, ctx, q, k, v, lse, cos, sin, attn_in, rows,
         ],
         late_from=8,
+        late_outs=4,
         scratch=[
-            pltpu.VMEM((D, 512), bf16), pltpu.VMEM((SEQ, 512), bf16), pltpu.VMEM((SEQ, 512), bf16),
+            pltpu.VMEM((2, 16, 2, 16, PACK), bf16), pltpu.VMEM((SEQ, 512), bf16), pltpu.VMEM((SEQ, 512), bf16),
             pltpu.VMEM((SEQ, 512), bf16), pltpu.VMEM((SEQ, 512), bf16), pltpu.VMEM((4, 512, 128), f32),
             pltpu.VMEM((SEQ, 256), f32), pltpu.VMEM((SEQ, 256), f32), pltpu.VMEM((SEQ, D), bf16),
-            pltpu.VMEM((D, D), bf16), pltpu.VMEM((SEQ, D), bf16), pltpu.SemaphoreType.DMA((11,)),
-            pltpu.VMEM((SEQ, D), f32), pltpu.VMEM((SEQ, D), bf16), pltpu.VMEM((D, PACK), bf16),
+            pltpu.VMEM((SEQ, D), bf16), pltpu.SemaphoreType.DMA((19,)),
+            pltpu.VMEM((SEQ, D), f32), pltpu.VMEM((SEQ, D), bf16), pltpu.VMEM((2, 16, 2, 16, PACK), bf16),
             pltpu.VMEM((SEQ, 512), bf16), pltpu.VMEM((SEQ, D), f32), pltpu.VMEM((SEQ, D), f32),
         ],
         us=0,
     )
 
     a_got = swap(a_sent, "c")
-    gains = gains.astype(f32)
-    gains = gains[:8] + gains[8:]
-    for axis in ("yh", "c"):
-        gains = gains + swap(gains, axis)
-    high = gains.astype(bf16)
-    gains = jnp.concatenate([high, (gains - high.astype(f32)).astype(bf16)], axis=0)
-    gains = jnp.broadcast_to(gains[None], (16, 16, 128))
-    a_move = jnp.concatenate([added(a_mine[16:], a_got[16:], gate=y_back), gains], axis=1)
+    block = pltpu.VMEM((16, 16, PACK), bf16)
+    wide = pltpu.VMEM((16, 16, PACK + 128), bf16)
+    a_move, gains = call(
+        move_kernel,
+        [((16, 16, PACK + 128), bf16), ((16, 128), f32)],
+        [pos, gains] + [swap(gains, axis) for axis in ("yh", "c", "twist")] + [a_mine, a_got],
+        late_from=5,
+        scratch=[block, block, pltpu.SemaphoreType.DMA((4,))],
+        us=0,
+    )
     a_yl = swap(a_move, "yl")
+    e_back = plane(after(e_cat, y_back))
     out_own, out_sent = call(
         finish_kernel,
         [((HALF, D), f32), ((HALF, D), bf16)],
-        [pos, tab_t, after(y_back, a_move), middle],
+        [pos, tab_t, middle, after(y_back, a_move)],
         scratch=[pltpu.VMEM((SLOTS, D), bf16), pltpu.VMEM((SEQ, D), f32)],
         us=0,
     )
-    e_back = plane(after(e_cat, out_sent))
-    a_sum = [added(a_mine[:16], a_got[:16], a_yl[:, :W_ROWS]), added(gains, a_yl[:, W_ROWS:])]
-    a_sum = jnp.concatenate(a_sum, axis=1)
+    a_yl = after(a_yl, out_sent)
+    (a_sum,) = call(
+        sum_kernel,
+        [((16, 16, PACK + 128), bf16)],
+        [pos, gains, a_mine, a_got, a_yl],
+        late_from=2,
+        scratch=[block, block, wide, pltpu.SemaphoreType.DMA((6,))],
+        us=0,
+    )
     total = plane(after(a_sum, e_back))
-
-    part_oth = swap(after(part_sent, a_sum), "yh")
-    (input_grad,) = call(
-        input_kernel, [((HALF, D), bf16)], [pos, tokens, aux, mg_own, part_own, part_oth], us=0
+    part_oth = swap(after(part_sent, a_move, y_back), "yh")
+    grad_gate, grad_up, grad_down = call(
+        expert_final_kernel, [((16, EXPERTS, 256), f32)] * 3, [pos, after(e_back, a_sum)], us=0
+    )
+
+    out_oth = swap(after(out_sent, a_sum), "yh")
+    part_oth = after(part_oth, grad_gate)
+    input_grad, output = call(
+        rows_kernel,
+        [((HALF, D), bf16), ((HALF, D), bf16)],
+        [pos, tokens, aux, mg_own, part_own, part_oth, out_own, out_oth],
+        us=0,
     )
     w_query, w_key, w_value, w_out, w_router, gain_two, gain_one = call(
         final_kernel,
         [((16, n), f32) for n in (512, 256, 256, 512, 32)] + [((1, 16), f32)] * 2,
         [pos, total],
-        us=2,
-    )
-
-    grad_gate, grad_up, grad_down = call(
-        expert_final_kernel, [((16, EXPERTS, 256), f32)] * 3, [pos, after(e_back, input_grad)], us=0
-    )
-
-    output = (out_own + swap(after(out_sent, a_sum), "yh").astype(f32)).astype(bf16)
+        us=0,
+    )
+
     return (
         output,
         input_grad,

time: 282 us -> 280 us (level)
  Pallas kernels: 78.5 us -> 90 us
  other arithmetic: 13.5 us -> 5.81 us
  waiting for transfers between devices: 98.5 us -> 93.5 us
  local copies, waits for them, and re-layouts: 11.7 us -> 8.68 us
  starting transfers between devices: 76.7 us -> 79.7 us
    pallas_call x10 -> x14, Pallas kernels: 48.8 us -> 60.3 us  [call(): pl.pallas_call(kernel, out_shape=out_shape, in_specs=in_specs, out_specs=...]
    ppermute x22, waiting for transfers between devices: 62.6 us -> 59 us  [swap(): return lax.ppermute(value, axis, [(0, 1), (1, 0)])]
    all_to_all x7, starting transfers between devices: 47.3 us -> 50.7 us  [plane(): return lax.all_to_all(value, PLANE, 0, 0, tiled=True)]
    convert_element_type x4 -> x1, other arithmetic: 5.81 us -> 2.99 us  [added(): return total.astype(bf16)]
  transfers between devices with their start and end apart: 31 -> 32, of which waited for: 18 -> 21; matrix products, arithmetic and copies ran while one was open for 7% -> 4% of each run, Pallas kernels for 23% -> 27%
where the time goes in v3:
time: 280 us; the launch traced here: 279 us
  waiting for transfers between devices  93.5 us (33%)
  Pallas kernels  90 us (32%)
  starting transfers between devices  79.7 us (28%)
  local copies, waits for them, and re-layouts  8.68 us (3%)
  other arithmetic  5.81 us (2%)
    pallas_call x14, Pallas kernels, call(): pl.pallas_call(kernel, out_shape=out_shape, in_specs=in_specs, out_specs=...  60.3 us
    ppermute x22, waiting for transfers between devices, swap(): return lax.ppermute(value, axis, [(0, 1), (1, 0)])  59 us
    all_to_all x7, starting transfers between devices, plane(): return lax.all_to_all(value, PLANE, 0, 0, tiled=True)  50.7 us
    ppermute x22, starting transfers between devices, swap(): return lax.ppermute(value, axis, [(0, 1), (1, 0)])  23 us
    pallas_call x3, Pallas kernels, call(): pl.pallas_call(kernel, grid=grid, out_shape=out_shape, in_specs=[smem] +...  19.8 us
    all_to_all x7, waiting for transfers between devices, plane(): return lax.all_to_all(value, PLANE, 0, 0, tiled=True)  17.9 us
    ppermute x2, waiting for transfers between devices, swap(): return lax.ppermute(value, ('yl', 'yh'), [(0, 3), (3, 0), (1, 2), (2, 1)])  15.3 us
    pallas_call x1, Pallas kernels, call(): pl.pallas_call(kernel, grid_spec=pltpu.PrefetchScalarGridSpec(num_scalar_...  9.85 us
  transfers between devices with their start and end apart: 32, of which 21 were waited for; matrix products, arithmetic and copies ran while one was open for 4% of the time, Pallas kernels for 27%

profile of v3, /device:TPU:0, one launch (start us, length us, event | category | flops | bytes accessed | tf_op | source)
XLA Modules:
  0.0 278.6 jit_solution(17731391540712659397)
XLA Ops:
  1.3 1.9 shard_map.220
  3.2 8.1 %all-to-all-start = ((bf16[16,16,1664]{2,1,0:T(8,128)(2,1)}), bf16[16,16,1664]{2,1,0:T(8,128)(2,1)}, u32[]{:S(2)}, u32[]{:S(2)}) async-start(bf16[16,16,1664]{2,1,0:T(8,128)(2,1)} %shard_map.220), calls=%async_computation | async-start | bytes 1703936 | tf_op jit(solution)/shard_map/all_to_all | solution.py:584
  11.4 3.3 %collective-permute-start.1 = (bf16[128,1024]{1,0:T(8,128)(2,1)}, bf16[128,1024]{1,0:T(8,128)(2,1)}, u32[]{:S(2)}, u32[]{:S(2)}) collective-permute-start(bf16[128,1024]{1,0:T(8,128)(2,1)} %cot_own.1), channel_id=1, source_target_pairs={{0,1},{1,0},{2,3},{3,2},{4,5},{5,4},{6,7},{7,6},{8,9},{9,8},{10,11... | collective-permute-start | bytes 786440 | tf_op jit(solution)/shard_map/ppermute | solution.py:576
  15.8 2.8 %shard_map.221 = (bf16[1280,256]{1,0:T(8,128)(2,1)}, bf16[256,1280]{1,0:T(8,128)(2,1)}, f32[256,128]{1,0:T(8,128)}) custom-call(s32[7]{0:T(128)} %stack.43.pos, s32[256,8]{1,0:T(8,128)} %copy.28.routes), custom_call_target="tpu_custom_call" | custom-call | flops 1000 | bytes 1000 | tf_op jit(solution)/shard_map/pallas_call | solution.py:62
  22.7 4.1 %shard_map.222 = (bf16[256,1024]{1,0:T(8,128)(2,1)}, bf16[16,832,128]{2,1,0:T(8,128)(2,1)}) custom-call(s32[7]{0:T(128)} %stack.43.pos, bf16[1280,256]{1,0:T(8,128)(2,1)} %get-tuple-element.76.tab, bf16[128,1024]{1,0:T(8,128)(2,1)} %cot_own.1, bf16[128,1024]{1,0:T(8,128)(2,1)} %collective-permute-done.1.cot_oth, bf16[16,192,128]{2,1,0:T(8,128)(2,1)} %bitcast.20), custom_call_target="tpu_custom_call" | custom-call | flops 3450000896 | bytes 5898268 | tf_op jit(solution)/shard_map/pallas_call | solution.py:62
  29.6 7.1 %all-to-all-start.2 = ((bf16[16,832,128]{2,1,0:T(8,128)(2,1)}), bf16[16,832,128]{2,1,0:T(8,128)(2,1)}, u32[]{:S(2)}, u32[]{:S(2)}) async-start(bf16[16,832,128]{2,1,0:T(8,128)(2,1)} %get-tuple-element.85), calls=%async_computation.2 | async-start | bytes 6815744 | tf_op jit(solution)/shard_map/all_to_all | solution.py:584
  36.7 11.7 %collective-permute-done.2.w_b = bf16[16,16,1664]{2,1,0:T(8,128)(2,1)S(1)} collective-permute-done((bf16[16,16,1664]{2,1,0:T(8,128)(2,1)}, bf16[16,16,1664]{2,1,0:T(8,128)(2,1)S(1)}, u32[]{:S(2)}, u32[]{:S(2)}) %collective-permute-start.2) | collective-permute-done | bytes 852000 | tf_op jit(solution)/shard_map/ppermute | solution.py:576
  49.4 1.8 negate_select_fusion
  52.8 8.0 %shard_map.223 = (bf16[256,1024]{1,0:T(8,128)(2,1)}, bf16[256,1024]{1,0:T(8,128)(2,1)}, f32[128,1024]{1,0:T(8,128)}, bf16[256,1024]{1,0:T(8,128)(2,1)}, bf16[256...) custom-call(s32[7]{0:T(128)} %stack.43.pos, ...), custom_call_target="tpu_custom_call" | custom-call | flops 8050000896 | bytes 8650780 | tf_op jit(solution)/shard_map/pallas_call | solution.py:62
  60.7 3.3 %collective-permute-start.5 = (bf16[256,1024]{1,0:T(8,128)(2,1)}, bf16[256,1024]{1,0:T(8,128)(2,1)}, u32[]{:S(2)}, u32[]{:S(2)}) collective-permute-start(bf16[256,1024]{1,0:T(8,128)(2,1)} %get-tuple-element.82.part_own), channel_id=1, source_target_pairs={{0,1},{1,0},{2,3},{3,2},{4,5},{5,4},{6,7},{7,6},{8,9},{9,8},{10,11... | collective-permute-start | bytes 1572872 | tf_op jit(solution)/shard_map/ppermute | solution.py:576
  64.0 12.6 %collective-permute-done.5.part_oth = bf16[256,1024]{1,0:T(8,128)(2,1)} collective-permute-done((bf16[256,1024]{1,0:T(8,128)(2,1)}, bf16[256,1024]{1,0:T(8,128)(2,1)}, u32[]{:S(2)}, u32[]{:S(2)}) %collective-permute-start.5) | collective-permute-done | bytes 524320 | tf_op jit(solution)/shard_map/ppermute | solution.py:576
  76.6 4.9 %shard_map.224 = (f32[256,128]{1,0:T(8,128)}, f32[256,1024]{1,0:T(8,128)}, bf16[256,1024]{1,0:T(8,128)(2,1)}, bf16[16,656,128]{2,1,0:T(8,128)(2,1)}) custom-call(s32[7]{0:T(128)} %stack.43.pos, bf16[256,1024]{1,0:T(8,128)(2,1)} %get-tuple-element.81.rows.rows_at, bf16[256,1024]{1,0:T(8,128)(2,1)} %get-tuple-element.82.part_own, ...), custom_call_target="tpu_custom_call" | custom-call | flops 3450000896 | bytes 7274524 | tf_op jit(solution)/shard_map/pallas_call | solution.py:62
  81.5 2.8 %all-to-all-done.2.c = bf16[16,832,128]{2,1,0:T(8,128)(2,1)} async-done(((bf16[16,832,128]{2,1,0:T(8,128)(2,1)}), bf16[16,832,128]{2,1,0:T(8,128)(2,1)}, u32[]{:S(2)}, u32[]{:S(2)}) %all-to-all-start.2) | async-done | bytes 3407904 | tf_op jit(solution)/shard_map/all_to_all | solution.py:584
  84.3 11.8 %all-to-all-start.1 = ((bf16[16,656,128]{2,1,0:T(8,128)(2,1)}), bf16[16,656,128]{2,1,0:T(8,128)(2,1)}, u32[]{:S(2)}, u32[]{:S(2)}) async-start(bf16[16,656,128]{2,1,0:T(8,128)(2,1)} %get-tuple-element.84), calls=%async_computation.1 | async-start | bytes 5373952 | tf_op jit(solution)/shard_map/all_to_all | solution.py:584
  97.4 3.1 %collective-permute-start.8 = (bf16[16,96,128]{2,1,0:T(8,128)(2,1)S(1)}, bf16[16,96,128]{2,1,0:T(8,128)(2,1)S(1)}, u32[]{:S(2)}, u32[]{:S(2)}) collective-permute-start(bf16[16,96,128]{2,1,0:T(8,128)(2,1)S(1)} %get-tuple-element.140), channel_id=1, source_target_pairs={{0,65},{65,0},{1,64},{64,1},{2,67},{67,2},{3,66},{66,3},{4,69},{69... | collective-permute-start | bytes 1179656 | tf_op jit(solution)/shard_map/ppermute | solution.py:575
  101.6 15.3 %collective-permute-done.8.a3 = bf16[16,96,128]{2,1,0:T(8,128)(2,1)S(1)} collective-permute-done((bf16[16,96,128]{2,1,0:T(8,128)(2,1)S(1)}, bf16[16,96,128]{2,1,0:T(8,128)(2,1)S(1)}, u32[]{:S(2)}, u32[]{:S(2)}) %collective-permute-start.8) | collective-permute-done | bytes 393248 | tf_op jit(solution)/shard_map/ppermute | solution.py:575
  120.1 4.1 %shard_map.225 = (bf16[1024,512]{1,0:T(8,128)(2,1)}, bf16[1024,512]{1,0:T(8,128)(2,1)}, bf16[1024,512]{1,0:T(8,128)(2,1)}) custom-call(s32[7]{0:T(128)} %stack.43.pos, bf16[16,96,128]{2,1,0:T(8,128)(2,1)} %copy-done.3, bf16[16,96,128]{2,1,0:T(8,128)(2,1)} %copy-done.8, bf16[16,96,128]{2,1,0:T(8,128)(2,1)} %copy-done.7, bf16[16,96,128]{2,1,0:T(8,128)(2,1)} %copy-done.6, ...), custom_call_target="tpu_custom_call" | custom-call | flops 4600001024 | bytes 6291484 | tf_op jit(solution)/shard_map/pallas_call | solution.py:62
  124.3 8.1 %all-to-all-done.1.x = bf16[16,656,128]{2,1,0:T(8,128)(2,1)} async-done(((bf16[16,656,128]{2,1,0:T(8,128)(2,1)}), bf16[16,656,128]{2,1,0:T(8,128)(2,1)}, u32[]{:S(2)}, u32[]{:S(2)}) %all-to-all-start.1) | async-done | bytes 2687008 | tf_op jit(solution)/shard_map/all_to_all | solution.py:584
  132.4 12.0 %shard_map.226 = (bf16[16,656,128]{2,1,0:T(8,128)(2,1)}, bf16[1280,512]{1,0:T(8,128)(2,1)}, bf16[1280,512]{1,0:T(8,128)(2,1)}, bf16[1280,512]{1,0:T(8,128)(2,1)}) custom-call(s32[7]{0:T(128)} %stack.43.pos, bf16[16,656,128]{2,1,0:T(8,128)(2,1)} %all-to-all-done.1.x, bf16[16,832,128]{2,1,0:T(8,128)(2,1)} %all-to-all-done.2.c, ...), custom_call_target="tpu_custom_call" | custom-call | flops 13800000512 | bytes 15859740 | tf_op jit(solution)/shard_map/pallas_call | solution.py:72
  144.4 4.5 %all-to-all-start.3 = ((bf16[16,656,128]{2,1,0:T(8,128)(2,1)}), bf16[16,656,128]{2,1,0:T(8,128)(2,1)}, u32[]{:S(2)}, u32[]{:S(2)}) async-start(bf16[16,656,128]{2,1,0:T(8,128)(2,1)} %get-tuple-element.89), calls=%async_computation.3 | async-start | bytes 5373952 | tf_op jit(solution)/shard_map/all_to_all | solution.py:584
  148.9 9.8 %shard_map.227 = (bf16[2,2,16,96,128]{4,3,2,1,0:T(8,128)(2,1)}, bf16[2,2,16,96,128]{4,3,2,1,0:T(8,128)(2,1)}) custom-call(s32[7]{0:T(128)} %stack.43.pos, bf16[16,656,128]{2,1,0:T(8,128)(2,1)} %all-to-all-done.1.x, bf16[16,832,128]{2,1,0:T(8,128)(2,1)} %all-to-all-done.2.c, bf16[1280,512]{1,0:T(8,128)(2,1)} %get-tuple-element.90.gate_g, ...), custom_call_target="tpu_custom_call" | custom-call | flops 1000 | bytes 1000 | tf_op jit(solution)/shard_map/pallas_call | solution.py:82
  158.8 3.6 %collective-permute-done.13.got = bf16[2,2,16,96,128]{4,3,2,1,0:T(8,128)(2,1)S(1)} collective-permute-done((bf16[2,2,16,96,128]{4,3,2,1,0:T(8,128)(2,1)}, bf16[2,2,16,96,128]{4,3,2,1,0:T(8,128)(2,1)S(1)}, u32[]{:S(2)}, u32[]{:S(2)}) %collective-permute-start.13) | collective-permute-done | bytes 1572896 | tf_op jit(solution)/shard_map/ppermute | solution.py:576
  162.4 3.0 %fusion.2 = (bf16[16,96,128]{2,1,0:T(8,128)(2,1)}, bf16[16,96,128]{2,1,0:T(8,128)(2,1)}, bf16[16,96,128]{2,1,0:T(8,128)(2,1)}) fusion(bf16[2,2,16,96,128]{4,3,2,1,0:T(8,128)(2,1)S(1)} %collective-permute-done.13.got, bf16[2,2,16,96,128]{4,3,2,1,0:T(8,128)(2,1)} %get-tuple-element.98.mine), kind=kLoop, calls=%fused_computation.6 | loop fusion | flops 2359296 | bytes 3538944 | tf_op jit(solution)/shard_map/convert_element_type | solution.py:591
  167.0 2.1 collective-permute-start.16
  169.9 5.2 %shard_map.228 = bf16[16,640,128]{2,1,0:T(8,128)(2,1)} custom-call(s32[7]{0:T(128)} %stack.43.pos, bf16[1280,512]{1,0:T(8,128)(2,1)} %get-tuple-element.95.scaled, bf16[1024,512]{1,0:T(8,128)(2,1)} %get-tuple-element.88.w_down), custom_call_target="tpu_custom_call" | custom-call | flops 1000 | bytes 1000 | tf_op jit(solution)/shard_map/pallas_call | solution.py:72
  175.1 2.6 collective-permute-done.14.got_yl
  177.7 4.5 %all-to-all-done.3.got = bf16[16,656,128]{2,1,0:T(8,128)(2,1)} async-done(((bf16[16,656,128]{2,1,0:T(8,128)(2,1)}), bf16[16,656,128]{2,1,0:T(8,128)(2,1)}, u32[]{:S(2)}, u32[]{:S(2)}) %all-to-all-start.3) | async-done | bytes 2687008 | tf_op jit(solution)/shard_map/all_to_all | solution.py:584
  182.2 4.1 %shard_map.229.comb_own = bf16[256,1152]{1,0:T(8,128)(2,1)} custom-call(s32[7]{0:T(128)} %stack.43.pos, bf16[256,1280]{1,0:T(8,128)(2,1)} %get-tuple-element.80.tab_t, bf16[16,656,128]{2,1,0:T(8,128)(2,1)} %all-to-all-done.3.got), custom_call_target="tpu_custom_call" | custom-call | flops 1000 | bytes 1000 | tf_op jit(solution)/shard_map/pallas_call | solution.py:62
  187.8 1.7 collective-permute-start.17
  189.5 7.2 %all-to-all-start.4 = ((bf16[16,640,128]{2,1,0:T(8,128)(2,1)}), bf16[16,640,128]{2,1,0:T(8,128)(2,1)}, u32[]{:S(2)}, u32[]{:S(2)}) async-start(bf16[16,640,128]{2,1,0:T(8,128)(2,1)} %shard_map.228), calls=%async_computation.4 | async-start | bytes 5242880 | tf_op jit(solution)/shard_map/all_to_all | solution.py:584
  196.7 2.6 shard_map.230
  199.3 4.8 %collective-permute-done.17.comb_oth = bf16[256,1152]{1,0:T(8,128)(2,1)} collective-permute-done((bf16[256,1152]{1,0:T(8,128)(2,1)}, bf16[256,1152]{1,0:T(8,128)(2,1)}, u32[]{:S(2)}, u32[]{:S(2)}) %collective-permute-start.17) | collective-permute-done | bytes 589856 | tf_op jit(solution)/shard_map/ppermute | solution.py:576
  204.1 12.1 %shard_map.231 = (bf16[128,1024]{1,0:T(8,128)(2,1)}, f32[8,128]{1,0:T(8,128)}, f32[128,1024]{1,0:T(8,128)}, f32[128,1024]{1,0:T(8,128)}, bf16[2,16,16,1664]{3,2,...) custom-call(s32[7]{0:T(128)} %stack.43.pos, bf16[256,1152]{1,0:T(8,128)(2,1)} %shard_map.229.comb_own, ...), custom_call_target="tpu_custom_call" | custom-call | flops 1000 | bytes 1000 | tf_op jit(solution)/shard_map/pallas_call | solution.py:62
  217.3 2.9 %collective-permute-start.18 = (f32[8,128]{1,0:T(8,128)}, f32[8,128]{1,0:T(8,128)}, u32[]{:S(2)}, u32[]{:S(2)}) collective-permute-start(f32[8,128]{1,0:T(8,128)} %get-tuple-element.113.g_own), channel_id=1, source_target_pairs={{0,1},{1,0},{2,3},{3,2},{4,5},{5,4},{6,7},{7,6},{8,9},{9,8},{10,11... | collective-permute-start | bytes 12296 | tf_op jit(solution)/shard_map/ppermute | solution.py:576
  222.7 3.3 %shard_map.232 = (bf16[16,16,1792]{2,1,0:T(8,128)(2,1)}, f32[16,128]{1,0:T(8,128)}) custom-call(s32[7]{0:T(128)} %stack.43.pos, f32[8,128]{1,0:T(8,128)} %get-tuple-element.113.g_own, f32[8,128]{1,0:T(8,128)} %collective-permute-done.18.g_yh, f32[8,128]{1,0:T(8,128)} %collective-permute-done.19.g_core, f32[8,128]{1,0:T(8,128)} %collective-permute-done.20.g_twist, ...), custom_call_target="tpu_custom_call" | custom-call | flops 1000 | bytes 1000 | tf_op jit(solution)/shard_map/pallas_call | solution.py:62
  226.1 2.1 collective-permute-start.23
  228.2 2.4 all-to-all-done.4.got
  230.6 4.7 %all-to-all-start.5 = ((bf16[16,192,128]{2,1,0:T(8,128)(2,1)}), bf16[16,192,128]{2,1,0:T(8,128)(2,1)}, u32[]{:S(2)}, u32[]{:S(2)}) async-start(bf16[16,192,128]{2,1,0:T(8,128)(2,1)} %shard_map.230), calls=%async_computation.5 | async-start | bytes 1572864 | tf_op jit(solution)/shard_map/all_to_all | solution.py:584
  235.3 4.1 %shard_map.233 = (f32[128,1024]{1,0:T(8,128)}, bf16[128,1024]{1,0:T(8,128)(2,1)}) custom-call(s32[7]{0:T(128)} %stack.43.pos, bf16[256,1280]{1,0:T(8,128)(2,1)} %get-tuple-element.80.tab_t, f32[256,1024]{1,0:T(8,128)} %get-tuple-element.100.middle, bf16[16,640,128]{2,1,0:T(8,128)(2,1)} %all-to-all-done.4.got), custom_call_target="tpu_custom_call" | custom-call | flops 1000 | bytes 1000 | tf_op jit(solution)/shard_map/pallas_call | solution.py:62
  239.5 9.1 %collective-permute-done.23.got_yl_at = bf16[16,16,1792]{2,1,0:T(8,128)(2,1)} collective-permute-done((bf16[16,16,1792]{2,1,0:T(8,128)(2,1)}, bf16[16,16,1792]{2,1,0:T(8,128)(2,1)}, u32[]{:S(2)}, u32[]{:S(2)}) %collective-permute-start.23) | collective-permute-done | bytes 917536 | tf_op jit(solution)/shard_map/ppermute | solution.py:576
  248.6 3.6 %shard_map.234 = bf16[16,16,1792]{2,1,0:T(8,128)(2,1)} custom-call(s32[7]{0:T(128)} %stack.43.pos, f32[16,128]{1,0:T(8,128)} %get-tuple-element.119.gain, bf16[2,16,16,1664]{3,2,1,0:T(8,128)(2,1)} %get-tuple-element.114.mine_at, bf16[2,16,16,1664]{3,2,1,0:T(8,128)(2,1)} %collective-permute-done.21.got_at, bf16[16,16,1792]{2,1,0:T(8,128)(2,1)} %collective-permute-done.23.got_yl_at), custom_call_target="tpu_custom_call" | custom-call | flops 1000 | bytes 1000 | tf_op jit(solution)/shard_map/pallas_call | solution.py:62
  252.2 7.2 %all-to-all-start.6 = ((bf16[16,16,1792]{2,1,0:T(8,128)(2,1)}), bf16[16,16,1792]{2,1,0:T(8,128)(2,1)}, u32[]{:S(2)}, u32[]{:S(2)}) async-start(bf16[16,16,1792]{2,1,0:T(8,128)(2,1)} %shard_map.234), calls=%async_computation.6 | async-start | bytes 1835008 | tf_op jit(solution)/shard_map/all_to_all | solution.py:584
  259.4 2.6 collective-permute-start.22
  263.0 2.5 shard_map.235
  265.5 5.0 %collective-permute-done.22.part_oth = bf16[128,1024]{1,0:T(8,128)(2,1)} collective-permute-done((bf16[128,1024]{1,0:T(8,128)(2,1)}, bf16[128,1024]{1,0:T(8,128)(2,1)}, u32[]{:S(2)}, u32[]{:S(2)}) %collective-permute-start.22) | collective-permute-done | bytes 262176 | tf_op jit(solution)/shard_map/ppermute | solution.py:576
  270.5 3.3 %collective-permute-done.24.out_oth = bf16[128,1024]{1,0:T(8,128)(2,1)} collective-permute-done((bf16[128,1024]{1,0:T(8,128)(2,1)}, bf16[128,1024]{1,0:T(8,128)(2,1)}, u32[]{:S(2)}, u32[]{:S(2)}) %collective-permute-start.24) | collective-permute-done | bytes 262176 | tf_op jit(solution)/shard_map/ppermute | solution.py:576
  273.8 2.8 %shard_map.236 = (bf16[128,1024]{1,0:T(8,128)(2,1)}, bf16[128,1024]{1,0:T(8,128)(2,1)}) custom-call(s32[7]{0:T(128)} %stack.43.pos, bf16[128,1024]{1,0:T(8,128)(2,1)} %tok.1, f32[128,1024]{1,0:T(8,128)} %get-tuple-element.79.aux, f32[128,1024]{1,0:T(8,128)} %get-tuple-element.110.mg, f32[128,1024]{1,0:T(8,128)} %get-tuple-element.111.part_own, ...), custom_call_target="tpu_custom_call" | custom-call | flops 1000 | bytes 1000 | tf_op jit(solution)/shard_map/pallas_call | solution.py:62
  276.7 1.9 shard_map.237
  (74 shorter events, 25.1 us)
Async XLA Ops:
  3.2 11.4 %copy-start.5 = (s32[256,8]{0,1:T(8,128)S(1)}, s32[256,8]{0,1:T(8,128)}, u32[]{:S(2)}) copy-start(s32[256,8]{0,1:T(8,128)} %param.14) | copy-start | bytes 24580
  3.2 23.6 %all-to-all-start = ((bf16[16,16,1664]{2,1,0:T(8,128)(2,1)}), bf16[16,16,1664]{2,1,0:T(8,128)(2,1)}, u32[]{:S(2)}, u32[]{:S(2)}) async-start(bf16[16,16,1664]{2,1,0:T(8,128)(2,1)} %shard_map.220), calls=%async_computation | async-start | bytes 1703936 | tf_op jit(solution)/shard_map/all_to_all | solution.py:584
  11.4 11.3 %collective-permute-start.1 = (bf16[128,1024]{1,0:T(8,128)(2,1)}, bf16[128,1024]{1,0:T(8,128)(2,1)}, u32[]{:S(2)}, u32[]{:S(2)}) collective-permute-start(bf16[128,1024]{1,0:T(8,128)(2,1)} %cot_own.1), channel_id=1, source_target_pairs={{0,1},{1,0},{2,3},{3,2},{4,5},{5,4},{6,7},{7,6},{8,9},{9,8},{10,11... | collective-permute-start | bytes 786440 | tf_op jit(solution)/shard_map/ppermute | solution.py:576
  15.4 11.4 %collective-permute-start = (bf16[128,1024]{1,0:T(8,128)(2,1)}, bf16[128,1024]{1,0:T(8,128)(2,1)}, u32[]{:S(2)}, u32[]{:S(2)}) collective-permute-start(bf16[128,1024]{1,0:T(8,128)(2,1)} %tok.1), channel_id=1, source_target_pairs={{0,1},{1,0},{2,3},{3,2},{4,5},{5,4},{6,7},{7,6},{8,9},{9,8},{10,11... | collective-permute-start | bytes 786440 | tf_op jit(solution)/shard_map/ppermute | solution.py:576
  18.6 2.7 copy-start.4
  26.8 2.8 %collective-permute-start.3 = (bf16[16,16,1664]{2,1,0:T(8,128)(2,1)}, bf16[16,16,1664]{2,1,0:T(8,128)(2,1)}, u32[]{:S(2)}, u32[]{:S(2)}) collective-permute-start(bf16[16,16,1664]{2,1,0:T(8,128)(2,1)} %all-to-all-done.w_a), channel_id=1, source_target_pairs={{0,2},{2,0},{1,3},{3,1},{4,6},{6,4},{5,7},{7,5},{8,10},{10,8},{9,1... | collective-permute-start | bytes 2555912 | tf_op jit(solution)/shard_map/ppermute | solution.py:576
  26.9 21.6 %collective-permute-start.2 = (bf16[16,16,1664]{2,1,0:T(8,128)(2,1)}, bf16[16,16,1664]{2,1,0:T(8,128)(2,1)S(1)}, u32[]{:S(2)}, u32[]{:S(2)}) collective-permute-start(bf16[16,16,1664]{2,1,0:T(8,128)(2,1)} %all-to-all-done.w_a), channel_id=1, source_target_pairs={{0,64},{64,0},{1,65},{65,1},{2,66},{66,2},{3,67},{67,3},{4,68},{68... | collective-permute-start | bytes 2555912 | tf_op jit(solution)/shard_map/ppermute | solution.py:576
  29.6 54.8 %all-to-all-start.2 = ((bf16[16,832,128]{2,1,0:T(8,128)(2,1)}), bf16[16,832,128]{2,1,0:T(8,128)(2,1)}, u32[]{:S(2)}, u32[]{:S(2)}) async-start(bf16[16,832,128]{2,1,0:T(8,128)(2,1)} %get-tuple-element.85), calls=%async_computation.2 | async-start | bytes 6815744 | tf_op jit(solution)/shard_map/all_to_all | solution.py:584
  48.5 0.9 copy-start.1
  49.4 2.4 collective-permute-start.4
  51.8 1.0 copy-start.2
  60.7 15.9 %collective-permute-start.5 = (bf16[256,1024]{1,0:T(8,128)(2,1)}, bf16[256,1024]{1,0:T(8,128)(2,1)}, u32[]{:S(2)}, u32[]{:S(2)}) collective-permute-start(bf16[256,1024]{1,0:T(8,128)(2,1)} %get-tuple-element.82.part_own), channel_id=1, source_target_pairs={{0,1},{1,0},{2,3},{3,2},{4,5},{5,4},{6,7},{7,6},{8,9},{9,8},{10,11... | collective-permute-start | bytes 1572872 | tf_op jit(solution)/shard_map/ppermute | solution.py:576
  84.3 48.1 %all-to-all-start.1 = ((bf16[16,656,128]{2,1,0:T(8,128)(2,1)}), bf16[16,656,128]{2,1,0:T(8,128)(2,1)}, u32[]{:S(2)}, u32[]{:S(2)}) async-start(bf16[16,656,128]{2,1,0:T(8,128)(2,1)} %get-tuple-element.84), calls=%async_computation.1 | async-start | bytes 5373952 | tf_op jit(solution)/shard_map/all_to_all | solution.py:584
  97.4 4.2 %copy-start.3 = (bf16[16,96,128]{2,1,0:T(8,128)(2,1)}, bf16[16,96,128]{2,1,0:T(8,128)(2,1)S(1)}, u32[]{:S(2)}) copy-start(bf16[16,96,128]{2,1,0:T(8,128)(2,1)S(1)} %get-tuple-element.141.a0) | copy-start | bytes 1179652
  97.4 19.5 %collective-permute-start.8 = (bf16[16,96,128]{2,1,0:T(8,128)(2,1)S(1)}, bf16[16,96,128]{2,1,0:T(8,128)(2,1)S(1)}, u32[]{:S(2)}, u32[]{:S(2)}) collective-permute-start(bf16[16,96,128]{2,1,0:T(8,128)(2,1)S(1)} %get-tuple-element.140), channel_id=1, source_target_pairs={{0,65},{65,0},{1,64},{64,1},{2,67},{67,2},{3,66},{66,3},{4,69},{69... | collective-permute-start | bytes 1179656 | tf_op jit(solution)/shard_map/ppermute | solution.py:575
  100.5 16.4 %collective-permute-start.7 = (bf16[16,96,128]{2,1,0:T(8,128)(2,1)S(1)}, bf16[16,96,128]{2,1,0:T(8,128)(2,1)S(1)}, u32[]{:S(2)}, u32[]{:S(2)}) collective-permute-start(bf16[16,96,128]{2,1,0:T(8,128)(2,1)S(1)} %get-tuple-element.140), channel_id=1, source_target_pairs={{0,1},{1,0},{2,3},{3,2},{4,5},{5,4},{6,7},{7,6},{8,9},{9,8},{10,11... | collective-permute-start | bytes 1179656 | tf_op jit(solution)/shard_map/ppermute | solution.py:576
  101.1 16.5 %collective-permute-start.6 = (bf16[16,96,128]{2,1,0:T(8,128)(2,1)S(1)}, bf16[16,96,128]{2,1,0:T(8,128)(2,1)S(1)}, u32[]{:S(2)}, u32[]{:S(2)}) collective-permute-start(bf16[16,96,128]{2,1,0:T(8,128)(2,1)S(1)} %get-tuple-element.141.a0), channel_id=1, source_target_pairs={{0,64},{64,0},{1,65},{65,1},{2,66},{66,2},{3,67},{67,3},{4,68},{68... | collective-permute-start | bytes 1179656 | tf_op jit(solution)/shard_map/ppermute | solution.py:576
  101.6 16.0 %collective-permute-start.9 = (bf16[16,96,128]{2,1,0:T(8,128)(2,1)S(1)}, bf16[16,96,128]{2,1,0:T(8,128)(2,1)S(1)}, u32[]{:S(2)}, u32[]{:S(2)}) collective-permute-start(bf16[16,96,128]{2,1,0:T(8,128)(2,1)S(1)} %get-tuple-element.141.a0), channel_id=1, source_target_pairs={{0,2},{2,0},{1,3},{3,1},{4,6},{6,4},{5,7},{7,5},{8,10},{10,8},{9,1... | collective-permute-start | bytes 1179656 | tf_op jit(solution)/shard_map/ppermute | solution.py:576
  116.9 0.8 copy-start.6
  116.9 1.7 collective-permute-start.12
  116.9 1.7 copy-start.7
  116.9 2.3 collective-permute-start.11
  117.6 1.6 copy-start.8
  117.6 2.5 collective-permute-start.10
  117.7 1.5 copy-start.9
  118.6 0.8 copy-start.10
  119.4 0.7 copy-start.11
  144.4 37.7 %all-to-all-start.3 = ((bf16[16,656,128]{2,1,0:T(8,128)(2,1)}), bf16[16,656,128]{2,1,0:T(8,128)(2,1)}, u32[]{:S(2)}, u32[]{:S(2)}) async-start(bf16[16,656,128]{2,1,0:T(8,128)(2,1)} %get-tuple-element.89), calls=%async_computation.3 | async-start | bytes 5373952 | tf_op jit(solution)/shard_map/all_to_all | solution.py:584
  158.8 3.6 %collective-permute-start.13 = (bf16[2,2,16,96,128]{4,3,2,1,0:T(8,128)(2,1)}, bf16[2,2,16,96,128]{4,3,2,1,0:T(8,128)(2,1)S(1)}, u32[]{:S(2)}, u32[]{:S(2)}) collective-permute-start(bf16[2,2,16,96,128]{4,3,2,1,0:T(8,128)(2,1)} %get-tuple-element.94), channel_id=1, source_target_pairs={{0,2},{2,0},{1,3},{3,1},{4,6},{6,4},{5,7},{7,5},{8,10},{10,8},{9,1... | collective-permute-start | bytes 4718600 | tf_op jit(solution)/shard_map/ppermute | solution.py:576
  162.4 3.0 %copy-start = (bf16[2,2,16,96,128]{4,3,2,1,0:T(8,128)(2,1)}, bf16[2,2,16,96,128]{4,3,2,1,0:T(8,128)(2,1)S(1)}, u32[]{:S(2)}) copy-start(bf16[2,2,16,96,128]{4,3,2,1,0:T(8,128)(2,1)S(1)} %collective-permute-done.13.got) | copy-start | bytes 4718596
  165.4 12.3 %collective-permute-start.14 = (bf16[16,96,128]{2,1,0:T(8,128)(2,1)}, bf16[16,96,128]{2,1,0:T(8,128)(2,1)}, u32[]{:S(2)}, u32[]{:S(2)}) collective-permute-start(bf16[16,96,128]{2,1,0:T(8,128)(2,1)} %get-tuple-element.144), channel_id=1, source_target_pairs={{0,64},{64,0},{1,65},{65,1},{2,66},{66,2},{3,67},{67,3},{4,68},{68... | collective-permute-start | bytes 1179656 | tf_op jit(solution)/shard_map/ppermute | solution.py:576
  167.0 19.3 %collective-permute-start.16 = (bf16[16,96,128]{2,1,0:T(8,128)(2,1)}, bf16[16,96,128]{2,1,0:T(8,128)(2,1)}, u32[]{:S(2)}, u32[]{:S(2)}) collective-permute-start(bf16[16,96,128]{2,1,0:T(8,128)(2,1)} %get-tuple-element.142), channel_id=1, source_target_pairs={{0,65},{65,0},{1,64},{64,1},{2,67},{67,2},{3,66},{66,3},{4,69},{69... | collective-permute-start | bytes 1179656 | tf_op jit(solution)/shard_map/ppermute | solution.py:575
  169.1 18.7 %collective-permute-start.15 = (bf16[16,96,128]{2,1,0:T(8,128)(2,1)}, bf16[16,96,128]{2,1,0:T(8,128)(2,1)}, u32[]{:S(2)}, u32[]{:S(2)}) collective-permute-start(bf16[16,96,128]{2,1,0:T(8,128)(2,1)} %get-tuple-element.143), channel_id=1, source_target_pairs={{0,1},{1,0},{2,3},{3,2},{4,5},{5,4},{6,7},{7,6},{8,9},{9,8},{10,11... | collective-permute-start | bytes 1179656 | tf_op jit(solution)/shard_map/ppermute | solution.py:576
  187.8 16.3 %collective-permute-start.17 = (bf16[256,1152]{1,0:T(8,128)(2,1)}, bf16[256,1152]{1,0:T(8,128)(2,1)}, u32[]{:S(2)}, u32[]{:S(2)}) collective-permute-start(bf16[256,1152]{1,0:T(8,128)(2,1)} %shard_map.229.comb_own), channel_id=1, source_target_pairs={{0,1},{1,0},{2,3},{3,2},{4,5},{5,4},{6,7},{7,6},{8,9},{9,8},{10,11... | collective-permute-start | bytes 1769480 | tf_op jit(solution)/shard_map/ppermute | solution.py:576
  189.5 41.1 %all-to-all-start.4 = ((bf16[16,640,128]{2,1,0:T(8,128)(2,1)}), bf16[16,640,128]{2,1,0:T(8,128)(2,1)}, u32[]{:S(2)}, u32[]{:S(2)}) async-start(bf16[16,640,128]{2,1,0:T(8,128)(2,1)} %shard_map.228), calls=%async_computation.4 | async-start | bytes 5242880 | tf_op jit(solution)/shard_map/all_to_all | solution.py:584
  216.3 6.4 %collective-permute-start.21 = (bf16[2,16,16,1664]{3,2,1,0:T(8,128)(2,1)}, bf16[2,16,16,1664]{3,2,1,0:T(8,128)(2,1)}, u32[]{:S(2)}, u32[]{:S(2)}) collective-permute-start(bf16[2,16,16,1664]{3,2,1,0:T(8,128)(2,1)} %get-tuple-element.115), channel_id=1, source_target_pairs={{0,2},{2,0},{1,3},{3,1},{4,6},{6,4},{5,7},{7,5},{8,10},{10,8},{9,1... | collective-permute-start | bytes 5111816 | tf_op jit(solution)/shard_map/ppermute | solution.py:576
  216.4 4.9 %collective-permute-start.20 = (f32[8,128]{1,0:T(8,128)}, f32[8,128]{1,0:T(8,128)}, u32[]{:S(2)}, u32[]{:S(2)}) collective-permute-start(f32[8,128]{1,0:T(8,128)} %get-tuple-element.113.g_own), channel_id=1, source_target_pairs={{0,3},{3,0},{1,2},{2,1},{4,7},{7,4},{5,6},{6,5},{8,11},{11,8},{9,1... | collective-permute-start | bytes 12296 | tf_op jit(solution)/shard_map/ppermute | solution.py:573
  217.2 4.1 %collective-permute-start.19 = (f32[8,128]{1,0:T(8,128)}, f32[8,128]{1,0:T(8,128)}, u32[]{:S(2)}, u32[]{:S(2)}) collective-permute-start(f32[8,128]{1,0:T(8,128)} %get-tuple-element.113.g_own), channel_id=1, source_target_pairs={{0,2},{2,0},{1,3},{3,1},{4,6},{6,4},{5,7},{7,5},{8,10},{10,8},{9,1... | collective-permute-start | bytes 12296 | tf_op jit(solution)/shard_map/ppermute | solution.py:576
  217.3 5.4 %collective-permute-start.18 = (f32[8,128]{1,0:T(8,128)}, f32[8,128]{1,0:T(8,128)}, u32[]{:S(2)}, u32[]{:S(2)}) collective-permute-start(f32[8,128]{1,0:T(8,128)} %get-tuple-element.113.g_own), channel_id=1, source_target_pairs={{0,1},{1,0},{2,3},{3,2},{4,5},{5,4},{6,7},{7,6},{8,9},{9,8},{10,11... | collective-permute-start | bytes 12296 | tf_op jit(solution)/shard_map/ppermute | solution.py:576
  226.1 22.5 %collective-permute-start.23 = (bf16[16,16,1792]{2,1,0:T(8,128)(2,1)}, bf16[16,16,1792]{2,1,0:T(8,128)(2,1)}, u32[]{:S(2)}, u32[]{:S(2)}) collective-permute-start(bf16[16,16,1792]{2,1,0:T(8,128)(2,1)} %get-tuple-element.116), channel_id=1, source_target_pairs={{0,64},{64,0},{1,65},{65,1},{2,66},{66,2},{3,67},{67,3},{4,68},{68... | collective-permute-start | bytes 2752520 | tf_op jit(solution)/shard_map/ppermute | solution.py:576
  230.6 21.6 %all-to-all-start.5 = ((bf16[16,192,128]{2,1,0:T(8,128)(2,1)}), bf16[16,192,128]{2,1,0:T(8,128)(2,1)}, u32[]{:S(2)}, u32[]{:S(2)}) async-start(bf16[16,192,128]{2,1,0:T(8,128)(2,1)} %shard_map.230), calls=%async_computation.5 | async-start | bytes 1572864 | tf_op jit(solution)/shard_map/all_to_all | solution.py:584
  252.2 24.4 %all-to-all-start.6 = ((bf16[16,16,1792]{2,1,0:T(8,128)(2,1)}), bf16[16,16,1792]{2,1,0:T(8,128)(2,1)}, u32[]{:S(2)}, u32[]{:S(2)}) async-start(bf16[16,16,1792]{2,1,0:T(8,128)(2,1)} %shard_map.234), calls=%async_computation.6 | async-start | bytes 1835008 | tf_op jit(solution)/shard_map/all_to_all | solution.py:584
  259.4 11.1 %collective-permute-start.22 = (bf16[128,1024]{1,0:T(8,128)(2,1)}, bf16[128,1024]{1,0:T(8,128)(2,1)}, u32[]{:S(2)}, u32[]{:S(2)}) collective-permute-start(bf16[128,1024]{1,0:T(8,128)(2,1)} %get-tuple-element.117), channel_id=1, source_target_pairs={{0,1},{1,0},{2,3},{3,2},{4,5},{5,4},{6,7},{7,6},{8,9},{9,8},{10,11... | collective-permute-start | bytes 786440 | tf_op jit(solution)/shard_map/ppermute | solution.py:576
  262.0 11.8 %collective-permute-start.24 = (bf16[128,1024]{1,0:T(8,128)(2,1)}, bf16[128,1024]{1,0:T(8,128)(2,1)}, u32[]{:S(2)}, u32[]{:S(2)}) collective-permute-start(bf16[128,1024]{1,0:T(8,128)(2,1)} %get-tuple-element.127), channel_id=1, source_target_pairs={{0,1},{1,0},{2,3},{3,2},{4,5},{5,4},{6,7},{7,6},{8,9},{9,8},{10,11... | collective-permute-start | bytes 786440 | tf_op jit(solution)/shard_map/ppermute | solution.py:576

commit v4 on v3

--- a/solution.py
+++ b/solution.py
@@ -1,4 +1,4 @@
-import functools
+import math
 
 import jax
 import jax.numpy as jnp
@@ -27,6 +27,7 @@
 NT = (((1,), (1,)), ((), ()))
 TN = (((0,), (0,)), ((), ()))
 VMEM_BYTES = 65472 * 1024
+PART_BYTES = 40 * 1024 * 1024
 
 
 def mo(value, by):
@@ -46,12 +47,12 @@
     return lax.broadcasted_iota(jnp.int32, shape, dim)
 
 
-def call(kernel, outs, args, scratch=(), grid=None, in_specs=None, out_specs=None, us=1, late_from=None, late_outs=0, prefetch=False):
+def call(kernel, outs, args, scratch=(), grid=None, in_specs=None, out_specs=None, us=1, late_from=None, late_outs=0, prefetch=False, vmem=VMEM_BYTES, hbm=False):
     smem = pl.BlockSpec(memory_space=pltpu.SMEM)
-    params = pltpu.CompilerParams(vmem_limit_bytes=VMEM_BYTES)
-    out_shape = [jax.ShapeDtypeStruct(shape, kind) for shape, kind in outs]
+    params = pltpu.CompilerParams(vmem_limit_bytes=vmem)
+    out_shape = [(pltpu.HBM if hbm else jax.ShapeDtypeStruct)(shape, kind) for shape, kind in outs]
     nbytes = sum(a.size * a.dtype.itemsize for a in args) + sum(
-        o.size * jnp.dtype(o.dtype).itemsize for o in out_shape
+        math.prod(shape) * jnp.dtype(kind).itemsize for shape, kind in outs
     )
     cost = pl.CostEstimate(flops=int(us * 1.15e9) + 1000, bytes_accessed=nbytes if us else 1000, transcendentals=0)
     if grid is None:
@@ -379,7 +380,7 @@
         out[:, cols] = dot(tab_t[...], held[:, cols]).astype(bf16)
 
 
-def finish_kernel(pos, tab_t, middle, got, own, sent, gathered, held):
+def finish_kernel(pos, tab_t, middle, got, part_sent, own, sent, gathered, held):
     half = pos[0]
     gather_blocks(gathered, got, 16, 8)
     for n in range(4):
@@ -387,7 +388,8 @@
         held[:, cols] = dot(tab_t[...], gathered[:, cols])
     mine = pl.ds(mo(half * HALF, HALF), HALF)
     own[...] = middle[mine, :] + held[mine, :]
-    sent[...] = held[pl.ds(mo((1 - half) * HALF, HALF), HALF), :].astype(bf16)
+    sent[0] = held[pl.ds(mo((1 - half) * HALF, HALF), HALF), :].astype(bf16)
+    sent[1] = part_sent[...]
 
 
 def put(pack, first, value):
@@ -532,14 +534,14 @@
         out[i, :, PACK:] = lines
 
 
-def rows_kernel(pos, tok, aux, mg, part_own, part_oth, out_own, out_oth, out, rows_out):
+def rows_kernel(pos, tok, aux, mg, part_own, out_own, got, out, rows_out):
     x = tok[...].astype(f32)
     factor = lax.rsqrt(jnp.mean(x * x, axis=1, keepdims=True) + NORM_EPS)
     normed = x * factor
-    inner = (part_own[...] + part_oth[...].astype(f32)) * aux[32:33, :]
+    inner = (part_own[...] + got[1].astype(f32)) * aux[32:33, :]
     inner = factor * (inner - normed * jnp.mean(inner * normed, axis=1, keepdims=True))
     out[...] = (mg[...] + inner).astype(bf16)
-    rows_out[...] = (out_own[...] + out_oth[...].astype(f32)).astype(bf16)
+    rows_out[...] = (out_own[...] + got[0].astype(f32)).astype(bf16)
 
 
 def final_kernel(pos, got, w_query, w_key, w_value, w_out, w_router, gain_two, gain_one):
@@ -589,6 +591,10 @@
     for value in values[1:]:
         total = total + value.astype(f32)
     return total.astype(bf16)
+
+
+def in_hbm(value):
+    return pltpu.with_memory_space_constraint(value, pltpu.HBM)
 
 
 def after(value, *others):
@@ -657,7 +663,7 @@
     e_oth = lax.dynamic_slice_in_dim(cot_slots, ROWS + 96 * (1 - half), 96, 1)
     pieces = [e_own, swap(e_own, "yl"), swap(e_oth, "yh"), swap(e_oth, "diag")]
     pieces = pieces + [swap(piece, "c") for piece in pieces]
-    w_gate, w_up, w_down = call(weights_kernel, [((D, 512), bf16)] * 3, [pos] + pieces, us=4)
+    w_gate, w_up, w_down = call(weights_kernel, [((D, 512), bf16)] * 3, [pos] + pieces, us=4, vmem=PART_BYTES)
 
     kept = [
         ((SEQ, D), bf16), ((128, D), f32), ((SEQ, D), bf16), ((SEQ, 512), bf16), ((SEQ, 512), bf16),
@@ -693,12 +699,14 @@
     dx, gate_g, up_g, scaled = call(
         expert_kernel,
         [((16, ROWS + 16, 128), bf16), ((SLOTS, 512), bf16), ((SLOTS, 512), bf16), ((SLOTS, 512), bf16)],
-        [pos, x_slots, cot_slots, w_gate, w_up, w_down],
+        [pos, in_hbm(x_slots), in_hbm(cot_slots), w_gate, w_up, w_down],
         scratch=[pltpu.VMEM((4 * CAP, D), bf16), pltpu.VMEM((4 * CAP, D), bf16)],
         grid=(4,),
         in_specs=[by_peer(ROWS + 16), by_peer(ROWS), whole, whole, whole],
         out_specs=[by_peer(ROWS + 16), by_row, by_row, by_row],
         us=12,
+        hbm=True,
+        vmem=PART_BYTES,
     )
     dx_back = plane(dx)
 
@@ -791,8 +799,8 @@
     e_back = plane(after(e_cat, y_back))
     out_own, out_sent = call(
         finish_kernel,
-        [((HALF, D), f32), ((HALF, D), bf16)],
-        [pos, tab_t, middle, after(y_back, a_move)],
+        [((HALF, D), f32), ((2, HALF, D), bf16)],
+        [pos, tab_t, middle, after(y_back, a_move), part_sent],
         scratch=[pltpu.VMEM((SLOTS, D), bf16), pltpu.VMEM((SEQ, D), f32)],
         us=0,
     )
@@ -806,17 +814,16 @@
         us=0,
     )
     total = plane(after(a_sum, e_back))
-    part_oth = swap(after(part_sent, a_move, y_back), "yh")
     grad_gate, grad_up, grad_down = call(
         expert_final_kernel, [((16, EXPERTS, 256), f32)] * 3, [pos, after(e_back, a_sum)], us=0
     )
 
-    out_oth = swap(after(out_sent, a_sum), "yh")
-    part_oth = after(part_oth, grad_gate)
+    rows_oth = swap(after(out_sent, a_sum), "yh")
+    rows_oth = after(rows_oth, grad_gate)
     input_grad, output = call(
         rows_kernel,
         [((HALF, D), bf16), ((HALF, D), bf16)],
-        [pos, tokens, aux, mg_own, part_own, part_oth, out_own, out_oth],
+        [pos, tokens, aux, mg_own, part_own, out_own, rows_oth],
         us=0,
     )
     w_query, w_key, w_value, w_out, w_router, gain_two, gain_one = call(

time: 280 us -> 280 us (level)
  waiting for transfers between devices: 93.5 us -> 98.2 us
  Pallas kernels: 90 us -> 86.6 us
    all_to_all x7, waiting for transfers between devices: 17.9 us -> 21.2 us  [plane(): return lax.all_to_all(value, PLANE, 0, 0, tiled=True)]
    pallas_call x14, Pallas kernels: 60.3 us -> 57.5 us  [call(): pl.pallas_call(kernel, out_shape=out_shape, in_specs=in_specs, out_specs=...]
    ppermute x22 -> x21, waiting for transfers between devices: 59 us -> 60.4 us  [swap(): return lax.ppermute(value, axis, [(0, 1), (1, 0)])]
    ppermute x22 -> x21, starting transfers between devices: 23 us -> 22.1 us  [swap(): return lax.ppermute(value, axis, [(0, 1), (1, 0)])]
  transfers between devices with their start and end apart: 32 -> 31, of which waited for: 21 -> 21; matrix products, arithmetic and copies ran while one was open for 4% -> 4% of each run, Pallas kernels for 27% -> 26%
where the time goes in v4:
time: 280 us; the launch traced here: 278 us
  waiting for transfers between devices  98.2 us (35%)
  Pallas kernels  86.6 us (31%)
  starting transfers between devices  78.9 us (28%)
  local copies, waits for them, and re-layouts  7.6 us (3%)
  other arithmetic  5.8 us (2%)
    ppermute x21, waiting for transfers between devices, swap(): return lax.ppermute(value, axis, [(0, 1), (1, 0)])  60.4 us
    pallas_call x14, Pallas kernels, call(): pl.pallas_call(kernel, out_shape=out_shape, in_specs=in_specs, out_specs=...  57.5 us
    all_to_all x7, starting transfers between devices, plane(): return lax.all_to_all(value, PLANE, 0, 0, tiled=True)  50.8 us
    ppermute x21, starting transfers between devices, swap(): return lax.ppermute(value, axis, [(0, 1), (1, 0)])  22.1 us
    all_to_all x7, waiting for transfers between devices, plane(): return lax.all_to_all(value, PLANE, 0, 0, tiled=True)  21.2 us
    pallas_call x3, Pallas kernels, call(): pl.pallas_call(kernel, grid=grid, out_shape=out_shape, in_specs=[smem] +...  19.3 us
    ppermute x2, waiting for transfers between devices, swap(): return lax.ppermute(value, ('yl', 'yh'), [(0, 3), (3, 0), (1, 2), (2, 1)])  15.3 us
    pallas_call x1, Pallas kernels, call(): pl.pallas_call(kernel, grid_spec=pltpu.PrefetchScalarGridSpec(num_scalar_...  9.83 us
  transfers between devices with their start and end apart: 31, of which 21 were waited for; matrix products, arithmetic and copies ran while one was open for 4% of the time, Pallas kernels for 26%

profile of v4, /device:TPU:0, one launch (start us, length us, event | category | flops | bytes accessed | tf_op | source)
XLA Modules:
  0.0 278.1 jit_solution(16299242636302176728)
XLA Ops:
  1.3 1.9 shard_map.220
  3.2 8.1 %all-to-all-start = ((bf16[16,16,1664]{2,1,0:T(8,128)(2,1)}), bf16[16,16,1664]{2,1,0:T(8,128)(2,1)}, u32[]{:S(2)}, u32[]{:S(2)}) async-start(bf16[16,16,1664]{2,1,0:T(8,128)(2,1)} %shard_map.220), calls=%async_computation | async-start | bytes 1703936 | tf_op jit(solution)/shard_map/all_to_all | solution.py:586
  11.3 3.3 %collective-permute-start.1 = (bf16[128,1024]{1,0:T(8,128)(2,1)}, bf16[128,1024]{1,0:T(8,128)(2,1)}, u32[]{:S(2)}, u32[]{:S(2)}) collective-permute-start(bf16[128,1024]{1,0:T(8,128)(2,1)} %cot_own.1), channel_id=1, source_target_pairs={{0,1},{1,0},{2,3},{3,2},{4,5},{5,4},{6,7},{7,6},{8,9},{9,8},{10,11... | collective-permute-start | bytes 786440 | tf_op jit(solution)/shard_map/ppermute | solution.py:578
  15.7 2.8 shard_map.221
  22.6 4.1 %shard_map.222 = (bf16[256,1024]{1,0:T(8,128)(2,1)}, bf16[16,832,128]{2,1,0:T(8,128)(2,1)}) custom-call(s32[7]{0:T(128)} %stack.43.pos, bf16[1280,256]{1,0:T(8,128)(2,1)} %get-tuple-element.75.tab, bf16[128,1024]{1,0:T(8,128)(2,1)} %cot_own.1, bf16[128,1024]{1,0:T(8,128)(2,1)} %collective-permute-done.1.cot_oth, bf16[16,192,128]{2,1,0:T(8,128)(2,1)} %bitcast.20), custom_call_target="tpu_custom_call" | custom-call | flops 3450000896 | bytes 5898268 | tf_op jit(solution)/shard_map/pallas_call | solution.py:63
  26.8 1.7 collective-permute-start.2
  29.5 7.1 %all-to-all-start.2 = ((bf16[16,832,128]{2,1,0:T(8,128)(2,1)}), bf16[16,832,128]{2,1,0:T(8,128)(2,1)}, u32[]{:S(2)}, u32[]{:S(2)}) async-start(bf16[16,832,128]{2,1,0:T(8,128)(2,1)} %get-tuple-element.84), calls=%async_computation.2 | async-start | bytes 6815744 | tf_op jit(solution)/shard_map/all_to_all | solution.py:586
  36.7 11.7 %collective-permute-done.2.w_b = bf16[16,16,1664]{2,1,0:T(8,128)(2,1)S(1)} collective-permute-done((bf16[16,16,1664]{2,1,0:T(8,128)(2,1)}, bf16[16,16,1664]{2,1,0:T(8,128)(2,1)S(1)}, u32[]{:S(2)}, u32[]{:S(2)}) %collective-permute-start.2) | collective-permute-done | bytes 852000 | tf_op jit(solution)/shard_map/ppermute | solution.py:578
  49.4 1.8 negate_select_fusion
  52.7 8.0 %shard_map.223 = (bf16[256,1024]{1,0:T(8,128)(2,1)}, bf16[256,1024]{1,0:T(8,128)(2,1)}, f32[128,1024]{1,0:T(8,128)}, bf16[256,1024]{1,0:T(8,128)(2,1)}, bf16[256...) custom-call(s32[7]{0:T(128)} %stack.43.pos, ...), custom_call_target="tpu_custom_call" | custom-call | flops 8050000896 | bytes 8650780 | tf_op jit(solution)/shard_map/pallas_call | solution.py:63
  60.7 3.3 %collective-permute-start.5 = (bf16[256,1024]{1,0:T(8,128)(2,1)}, bf16[256,1024]{1,0:T(8,128)(2,1)}, u32[]{:S(2)}, u32[]{:S(2)}) collective-permute-start(bf16[256,1024]{1,0:T(8,128)(2,1)} %get-tuple-element.81.part_own), channel_id=1, source_target_pairs={{0,1},{1,0},{2,3},{3,2},{4,5},{5,4},{6,7},{7,6},{8,9},{9,8},{10,11... | collective-permute-start | bytes 1572872 | tf_op jit(solution)/shard_map/ppermute | solution.py:578
  63.9 12.6 %collective-permute-done.5.part_oth = bf16[256,1024]{1,0:T(8,128)(2,1)} collective-permute-done((bf16[256,1024]{1,0:T(8,128)(2,1)}, bf16[256,1024]{1,0:T(8,128)(2,1)}, u32[]{:S(2)}, u32[]{:S(2)}) %collective-permute-start.5) | collective-permute-done | bytes 524320 | tf_op jit(solution)/shard_map/ppermute | solution.py:578
  76.5 4.9 %shard_map.224 = (f32[256,128]{1,0:T(8,128)}, f32[256,1024]{1,0:T(8,128)}, bf16[256,1024]{1,0:T(8,128)(2,1)}, bf16[16,656,128]{2,1,0:T(8,128)(2,1)}) custom-call(s32[7]{0:T(128)} %stack.43.pos, bf16[256,1024]{1,0:T(8,128)(2,1)} %get-tuple-element.80.rows.rows_at, bf16[256,1024]{1,0:T(8,128)(2,1)} %get-tuple-element.81.part_own, ...), custom_call_target="tpu_custom_call" | custom-call | flops 3450000896 | bytes 7274524 | tf_op jit(solution)/shard_map/pallas_call | solution.py:63
  81.4 2.8 %all-to-all-done.2.c = bf16[16,832,128]{2,1,0:T(8,128)(2,1)} async-done(((bf16[16,832,128]{2,1,0:T(8,128)(2,1)}), bf16[16,832,128]{2,1,0:T(8,128)(2,1)}, u32[]{:S(2)}, u32[]{:S(2)}) %all-to-all-start.2) | async-done | bytes 3407904 | tf_op jit(solution)/shard_map/all_to_all | solution.py:586
  84.3 12.0 %all-to-all-start.1 = ((bf16[16,656,128]{2,1,0:T(8,128)(2,1)}), bf16[16,656,128]{2,1,0:T(8,128)(2,1)}, u32[]{:S(2)}, u32[]{:S(2)}) async-start(bf16[16,656,128]{2,1,0:T(8,128)(2,1)} %get-tuple-element.83), calls=%async_computation.1 | async-start | bytes 5373952 | tf_op jit(solution)/shard_map/all_to_all | solution.py:586
  97.4 3.1 %collective-permute-start.8 = (bf16[16,96,128]{2,1,0:T(8,128)(2,1)S(1)}, bf16[16,96,128]{2,1,0:T(8,128)(2,1)S(1)}, u32[]{:S(2)}, u32[]{:S(2)}) collective-permute-start(bf16[16,96,128]{2,1,0:T(8,128)(2,1)S(1)} %get-tuple-element.138), channel_id=1, source_target_pairs={{0,65},{65,0},{1,64},{64,1},{2,67},{67,2},{3,66},{66,3},{4,69},{69... | collective-permute-start | bytes 1179656 | tf_op jit(solution)/shard_map/ppermute | solution.py:577
  101.6 15.3 %collective-permute-done.8.a3 = bf16[16,96,128]{2,1,0:T(8,128)(2,1)S(1)} collective-permute-done((bf16[16,96,128]{2,1,0:T(8,128)(2,1)S(1)}, bf16[16,96,128]{2,1,0:T(8,128)(2,1)S(1)}, u32[]{:S(2)}, u32[]{:S(2)}) %collective-permute-start.8) | collective-permute-done | bytes 393248 | tf_op jit(solution)/shard_map/ppermute | solution.py:577
  121.0 11.5 %all-to-all-done.1.x = bf16[16,656,128]{2,1,0:T(8,128)(2,1)} async-done(((bf16[16,656,128]{2,1,0:T(8,128)(2,1)}), bf16[16,656,128]{2,1,0:T(8,128)(2,1)}, u32[]{:S(2)}, u32[]{:S(2)}) %all-to-all-start.1) | async-done | bytes 2687008 | tf_op jit(solution)/shard_map/all_to_all | solution.py:586
  132.5 11.5 %shard_map.226 = (bf16[16,656,128]{2,1,0:T(8,128)(2,1)}, bf16[1280,512]{1,0:T(8,128)(2,1)}, bf16[1280,512]{1,0:T(8,128)(2,1)}, bf16[1280,512]{1,0:T(8,128)(2,1)}) custom-call(s32[7]{0:T(128)S(1)} %copy-done.1, bf16[16,656,128]{2,1,0:T(8,128)(2,1)} %all-to-all-done.1.x, bf16[16,832,128]{2,1,0:T(8,128)(2,1)} %all-to-all-done.2.c, ...), custom_call_target="tpu_custom_call" | custom-call | flops 13800000512 | bytes 15859740 | tf_op jit(solution)/shard_map/pallas_call | solution.py:73
  144.0 4.5 %all-to-all-start.3 = ((bf16[16,656,128]{2,1,0:T(8,128)(2,1)}), bf16[16,656,128]{2,1,0:T(8,128)(2,1)}, u32[]{:S(2)}, u32[]{:S(2)}) async-start(bf16[16,656,128]{2,1,0:T(8,128)(2,1)} %get-tuple-element.88), calls=%async_computation.3 | async-start | bytes 5373952 | tf_op jit(solution)/shard_map/all_to_all | solution.py:586
  148.4 9.8 %shard_map.227 = (bf16[2,2,16,96,128]{4,3,2,1,0:T(8,128)(2,1)}, bf16[2,2,16,96,128]{4,3,2,1,0:T(8,128)(2,1)}) custom-call(s32[7]{0:T(128)} %stack.43.pos, bf16[16,656,128]{2,1,0:T(8,128)(2,1)} %all-to-all-done.1.x, bf16[16,832,128]{2,1,0:T(8,128)(2,1)} %all-to-all-done.2.c, bf16[1280,512]{1,0:T(8,128)(2,1)} %get-tuple-element.89.gate_g, ...), custom_call_target="tpu_custom_call" | custom-call | flops 1000 | bytes 1000 | tf_op jit(solution)/shard_map/pallas_call | solution.py:83
  158.3 3.6 %collective-permute-done.13.got = bf16[2,2,16,96,128]{4,3,2,1,0:T(8,128)(2,1)S(1)} collective-permute-done((bf16[2,2,16,96,128]{4,3,2,1,0:T(8,128)(2,1)}, bf16[2,2,16,96,128]{4,3,2,1,0:T(8,128)(2,1)S(1)}, u32[]{:S(2)}, u32[]{:S(2)}) %collective-permute-start.13) | collective-permute-done | bytes 1572896 | tf_op jit(solution)/shard_map/ppermute | solution.py:578
  161.9 3.0 %fusion.2 = (bf16[16,96,128]{2,1,0:T(8,128)(2,1)}, bf16[16,96,128]{2,1,0:T(8,128)(2,1)}, bf16[16,96,128]{2,1,0:T(8,128)(2,1)}) fusion(bf16[2,2,16,96,128]{4,3,2,1,0:T(8,128)(2,1)S(1)} %collective-permute-done.13.got, bf16[2,2,16,96,128]{4,3,2,1,0:T(8,128)(2,1)} %get-tuple-element.97.mine), kind=kLoop, calls=%fused_computation.6 | loop fusion | flops 2359296 | bytes 3538944 | tf_op jit(solution)/shard_map/convert_element_type | solution.py:593
  164.9 1.6 collective-permute-start.14
  166.5 2.2 collective-permute-start.16
  169.4 5.2 %shard_map.228 = bf16[16,640,128]{2,1,0:T(8,128)(2,1)} custom-call(s32[7]{0:T(128)} %stack.43.pos, bf16[1280,512]{1,0:T(8,128)(2,1)} %get-tuple-element.94.scaled, bf16[1024,512]{1,0:T(8,128)(2,1)} %copy-done), custom_call_target="tpu_custom_call" | custom-call | flops 1000 | bytes 1000 | tf_op jit(solution)/shard_map/pallas_call | solution.py:73
  174.6 2.6 collective-permute-done.14.got_yl
  177.2 4.5 %all-to-all-done.3.got = bf16[16,656,128]{2,1,0:T(8,128)(2,1)} async-done(((bf16[16,656,128]{2,1,0:T(8,128)(2,1)}), bf16[16,656,128]{2,1,0:T(8,128)(2,1)}, u32[]{:S(2)}, u32[]{:S(2)}) %all-to-all-start.3) | async-done | bytes 2687008 | tf_op jit(solution)/shard_map/all_to_all | solution.py:586
  181.7 4.1 %shard_map.229.comb_own = bf16[256,1152]{1,0:T(8,128)(2,1)} custom-call(s32[7]{0:T(128)} %stack.43.pos, bf16[256,1280]{1,0:T(8,128)(2,1)} %get-tuple-element.79.tab_t, bf16[16,656,128]{2,1,0:T(8,128)(2,1)} %all-to-all-done.3.got), custom_call_target="tpu_custom_call" | custom-call | flops 1000 | bytes 1000 | tf_op jit(solution)/shard_map/pallas_call | solution.py:63
  187.3 1.8 collective-permute-start.17
  189.1 7.1 %all-to-all-start.4 = ((bf16[16,640,128]{2,1,0:T(8,128)(2,1)}), bf16[16,640,128]{2,1,0:T(8,128)(2,1)}, u32[]{:S(2)}, u32[]{:S(2)}) async-start(bf16[16,640,128]{2,1,0:T(8,128)(2,1)} %shard_map.228), calls=%async_computation.4 | async-start | bytes 5242880 | tf_op jit(solution)/shard_map/all_to_all | solution.py:586
  196.2 2.6 shard_map.230
  198.8 4.8 %collective-permute-done.17.comb_oth = bf16[256,1152]{1,0:T(8,128)(2,1)} collective-permute-done((bf16[256,1152]{1,0:T(8,128)(2,1)}, bf16[256,1152]{1,0:T(8,128)(2,1)}, u32[]{:S(2)}, u32[]{:S(2)}) %collective-permute-start.17) | collective-permute-done | bytes 589856 | tf_op jit(solution)/shard_map/ppermute | solution.py:578
  203.6 12.1 %shard_map.231 = (bf16[128,1024]{1,0:T(8,128)(2,1)}, f32[8,128]{1,0:T(8,128)}, f32[128,1024]{1,0:T(8,128)}, f32[128,1024]{1,0:T(8,128)}, bf16[2,16,16,1664]{3,2,...) custom-call(s32[7]{0:T(128)} %stack.43.pos, bf16[256,1152]{1,0:T(8,128)(2,1)} %shard_map.229.comb_own, ...), custom_call_target="tpu_custom_call" | custom-call | flops 1000 | bytes 1000 | tf_op jit(solution)/shard_map/pallas_call | solution.py:63
  216.7 2.9 %collective-permute-start.18 = (f32[8,128]{1,0:T(8,128)}, f32[8,128]{1,0:T(8,128)}, u32[]{:S(2)}, u32[]{:S(2)}) collective-permute-start(f32[8,128]{1,0:T(8,128)} %get-tuple-element.111.g_own), channel_id=1, source_target_pairs={{0,1},{1,0},{2,3},{3,2},{4,5},{5,4},{6,7},{7,6},{8,9},{9,8},{10,11... | collective-permute-start | bytes 12296 | tf_op jit(solution)/shard_map/ppermute | solution.py:578
  222.1 3.4 %shard_map.232 = (bf16[16,16,1792]{2,1,0:T(8,128)(2,1)}, f32[16,128]{1,0:T(8,128)}) custom-call(s32[7]{0:T(128)} %stack.43.pos, f32[8,128]{1,0:T(8,128)} %get-tuple-element.111.g_own, f32[8,128]{1,0:T(8,128)} %collective-permute-done.18.g_yh, f32[8,128]{1,0:T(8,128)} %collective-permute-done.19.g_core, f32[8,128]{1,0:T(8,128)} %collective-permute-done.20.g_twist, ...), custom_call_target="tpu_custom_call" | custom-call | flops 1000 | bytes 1000 | tf_op jit(solution)/shard_map/pallas_call | solution.py:63
  225.5 2.2 collective-permute-start.22
  227.6 2.4 all-to-all-done.4.got
  230.0 4.8 %all-to-all-start.5 = ((bf16[16,192,128]{2,1,0:T(8,128)(2,1)}), bf16[16,192,128]{2,1,0:T(8,128)(2,1)}, u32[]{:S(2)}, u32[]{:S(2)}) async-start(bf16[16,192,128]{2,1,0:T(8,128)(2,1)} %shard_map.230), calls=%async_computation.5 | async-start | bytes 1572864 | tf_op jit(solution)/shard_map/all_to_all | solution.py:586
  234.8 4.3 %shard_map.233 = (f32[128,1024]{1,0:T(8,128)}, bf16[2,128,1024]{2,1,0:T(8,128)(2,1)}) custom-call(s32[7]{0:T(128)} %stack.43.pos, bf16[256,1280]{1,0:T(8,128)(2,1)} %get-tuple-element.79.tab_t, f32[256,1024]{1,0:T(8,128)} %get-tuple-element.99.middle, bf16[16,640,128]{2,1,0:T(8,128)(2,1)} %all-to-all-done.4.got, bf16[128,1024]{1,0:T(8,128)(2,1)} %get-tuple-element.116.part_sent), custom_call_target="tpu_custom_call" | custom-call | flops 1000 | bytes 1000 | tf_op jit(solution)/shard_map/pallas_call | solution.py:63
  239.1 9.0 %collective-permute-done.22.got_yl_at = bf16[16,16,1792]{2,1,0:T(8,128)(2,1)} collective-permute-done((bf16[16,16,1792]{2,1,0:T(8,128)(2,1)}, bf16[16,16,1792]{2,1,0:T(8,128)(2,1)}, u32[]{:S(2)}, u32[]{:S(2)}) %collective-permute-start.22) | collective-permute-done | bytes 917536 | tf_op jit(solution)/shard_map/ppermute | solution.py:578
  248.1 3.6 %shard_map.234 = bf16[16,16,1792]{2,1,0:T(8,128)(2,1)} custom-call(s32[7]{0:T(128)} %stack.43.pos, f32[16,128]{1,0:T(8,128)} %get-tuple-element.119.gain, bf16[2,16,16,1664]{3,2,1,0:T(8,128)(2,1)} %get-tuple-element.112.mine_at, bf16[2,16,16,1664]{3,2,1,0:T(8,128)(2,1)} %collective-permute-done.21.got_at, bf16[16,16,1792]{2,1,0:T(8,128)(2,1)} %collective-permute-done.22.got_yl_at), custom_call_target="tpu_custom_call" | custom-call | flops 1000 | bytes 1000 | tf_op jit(solution)/shard_map/pallas_call | solution.py:63
  251.7 7.2 %all-to-all-start.6 = ((bf16[16,16,1792]{2,1,0:T(8,128)(2,1)}), bf16[16,16,1792]{2,1,0:T(8,128)(2,1)}, u32[]{:S(2)}, u32[]{:S(2)}) async-start(bf16[16,16,1792]{2,1,0:T(8,128)(2,1)} %shard_map.234), calls=%async_computation.6 | async-start | bytes 1835008 | tf_op jit(solution)/shard_map/all_to_all | solution.py:586
  258.9 2.6 collective-permute-start.23
  261.5 2.5 shard_map.235
  264.0 9.4 %collective-permute-done.23.got = bf16[2,128,1024]{2,1,0:T(8,128)(2,1)} collective-permute-done((bf16[2,128,1024]{2,1,0:T(8,128)(2,1)}, bf16[2,128,1024]{2,1,0:T(8,128)(2,1)}, u32[]{:S(2)}, u32[]{:S(2)}) %collective-permute-start.23) | collective-permute-done | bytes 524320 | tf_op jit(solution)/shard_map/ppermute | solution.py:578
  273.3 2.8 %shard_map.236 = (bf16[128,1024]{1,0:T(8,128)(2,1)}, bf16[128,1024]{1,0:T(8,128)(2,1)}) custom-call(s32[7]{0:T(128)} %stack.43.pos, bf16[128,1024]{1,0:T(8,128)(2,1)} %tok.1, f32[128,1024]{1,0:T(8,128)} %get-tuple-element.78.aux, f32[128,1024]{1,0:T(8,128)} %get-tuple-element.109.mg, f32[128,1024]{1,0:T(8,128)} %get-tuple-element.110.part_own, ...), custom_call_target="tpu_custom_call" | custom-call | flops 1000 | bytes 1000 | tf_op jit(solution)/shard_map/pallas_call | solution.py:63
  276.1 1.9 shard_map.237
  (62 shorter events, 21.5 us)
Async XLA Ops:
  3.2 11.4 %copy-start.6 = (s32[256,8]{0,1:T(8,128)S(1)}, s32[256,8]{0,1:T(8,128)}, u32[]{:S(2)}) copy-start(s32[256,8]{0,1:T(8,128)} %param.14) | copy-start | bytes 24580
  3.2 23.5 %all-to-all-start = ((bf16[16,16,1664]{2,1,0:T(8,128)(2,1)}), bf16[16,16,1664]{2,1,0:T(8,128)(2,1)}, u32[]{:S(2)}, u32[]{:S(2)}) async-start(bf16[16,16,1664]{2,1,0:T(8,128)(2,1)} %shard_map.220), calls=%async_computation | async-start | bytes 1703936 | tf_op jit(solution)/shard_map/all_to_all | solution.py:586
  11.3 11.3 %collective-permute-start.1 = (bf16[128,1024]{1,0:T(8,128)(2,1)}, bf16[128,1024]{1,0:T(8,128)(2,1)}, u32[]{:S(2)}, u32[]{:S(2)}) collective-permute-start(bf16[128,1024]{1,0:T(8,128)(2,1)} %cot_own.1), channel_id=1, source_target_pairs={{0,1},{1,0},{2,3},{3,2},{4,5},{5,4},{6,7},{7,6},{8,9},{9,8},{10,11... | collective-permute-start | bytes 786440 | tf_op jit(solution)/shard_map/ppermute | solution.py:578
  15.4 11.3 %collective-permute-start = (bf16[128,1024]{1,0:T(8,128)(2,1)}, bf16[128,1024]{1,0:T(8,128)(2,1)}, u32[]{:S(2)}, u32[]{:S(2)}) collective-permute-start(bf16[128,1024]{1,0:T(8,128)(2,1)} %tok.1), channel_id=1, source_target_pairs={{0,1},{1,0},{2,3},{3,2},{4,5},{5,4},{6,7},{7,6},{8,9},{9,8},{10,11... | collective-permute-start | bytes 786440 | tf_op jit(solution)/shard_map/ppermute | solution.py:578
  18.5 2.7 copy-start.5
  26.7 2.8 %collective-permute-start.3 = (bf16[16,16,1664]{2,1,0:T(8,128)(2,1)}, bf16[16,16,1664]{2,1,0:T(8,128)(2,1)}, u32[]{:S(2)}, u32[]{:S(2)}) collective-permute-start(bf16[16,16,1664]{2,1,0:T(8,128)(2,1)} %all-to-all-done.w_a), channel_id=1, source_target_pairs={{0,2},{2,0},{1,3},{3,1},{4,6},{6,4},{5,7},{7,5},{8,10},{10,8},{9,1... | collective-permute-start | bytes 2555912 | tf_op jit(solution)/shard_map/ppermute | solution.py:578
  26.8 21.6 %collective-permute-start.2 = (bf16[16,16,1664]{2,1,0:T(8,128)(2,1)}, bf16[16,16,1664]{2,1,0:T(8,128)(2,1)S(1)}, u32[]{:S(2)}, u32[]{:S(2)}) collective-permute-start(bf16[16,16,1664]{2,1,0:T(8,128)(2,1)} %all-to-all-done.w_a), channel_id=1, source_target_pairs={{0,64},{64,0},{1,65},{65,1},{2,66},{66,2},{3,67},{67,3},{4,68},{68... | collective-permute-start | bytes 2555912 | tf_op jit(solution)/shard_map/ppermute | solution.py:578
  29.5 54.7 %all-to-all-start.2 = ((bf16[16,832,128]{2,1,0:T(8,128)(2,1)}), bf16[16,832,128]{2,1,0:T(8,128)(2,1)}, u32[]{:S(2)}, u32[]{:S(2)}) async-start(bf16[16,832,128]{2,1,0:T(8,128)(2,1)} %get-tuple-element.84), calls=%async_computation.2 | async-start | bytes 6815744 | tf_op jit(solution)/shard_map/all_to_all | solution.py:586
  48.4 0.9 copy-start.3
  49.3 2.4 collective-permute-start.4
  51.7 1.0 copy-start.4
  60.7 15.9 %collective-permute-start.5 = (bf16[256,1024]{1,0:T(8,128)(2,1)}, bf16[256,1024]{1,0:T(8,128)(2,1)}, u32[]{:S(2)}, u32[]{:S(2)}) collective-permute-start(bf16[256,1024]{1,0:T(8,128)(2,1)} %get-tuple-element.81.part_own), channel_id=1, source_target_pairs={{0,1},{1,0},{2,3},{3,2},{4,5},{5,4},{6,7},{7,6},{8,9},{9,8},{10,11... | collective-permute-start | bytes 1572872 | tf_op jit(solution)/shard_map/ppermute | solution.py:578
  84.3 35.5 %copy-start.1 = (s32[7]{0:T(128)S(1)}, s32[7]{0:T(128)}, u32[]{:S(2)}) copy-start(s32[7]{0:T(128)} %stack.43.pos) | copy-start | bytes 88
  84.3 48.2 %all-to-all-start.1 = ((bf16[16,656,128]{2,1,0:T(8,128)(2,1)}), bf16[16,656,128]{2,1,0:T(8,128)(2,1)}, u32[]{:S(2)}, u32[]{:S(2)}) async-start(bf16[16,656,128]{2,1,0:T(8,128)(2,1)} %get-tuple-element.83), calls=%async_computation.1 | async-start | bytes 5373952 | tf_op jit(solution)/shard_map/all_to_all | solution.py:586
  97.4 19.5 %collective-permute-start.8 = (bf16[16,96,128]{2,1,0:T(8,128)(2,1)S(1)}, bf16[16,96,128]{2,1,0:T(8,128)(2,1)S(1)}, u32[]{:S(2)}, u32[]{:S(2)}) collective-permute-start(bf16[16,96,128]{2,1,0:T(8,128)(2,1)S(1)} %get-tuple-element.138), channel_id=1, source_target_pairs={{0,65},{65,0},{1,64},{64,1},{2,67},{67,2},{3,66},{66,3},{4,69},{69... | collective-permute-start | bytes 1179656 | tf_op jit(solution)/shard_map/ppermute | solution.py:577
  100.5 16.4 %collective-permute-start.7 = (bf16[16,96,128]{2,1,0:T(8,128)(2,1)S(1)}, bf16[16,96,128]{2,1,0:T(8,128)(2,1)S(1)}, u32[]{:S(2)}, u32[]{:S(2)}) collective-permute-start(bf16[16,96,128]{2,1,0:T(8,128)(2,1)S(1)} %get-tuple-element.138), channel_id=1, source_target_pairs={{0,1},{1,0},{2,3},{3,2},{4,5},{5,4},{6,7},{7,6},{8,9},{9,8},{10,11... | collective-permute-start | bytes 1179656 | tf_op jit(solution)/shard_map/ppermute | solution.py:578
  101.1 16.5 %collective-permute-start.6 = (bf16[16,96,128]{2,1,0:T(8,128)(2,1)S(1)}, bf16[16,96,128]{2,1,0:T(8,128)(2,1)S(1)}, u32[]{:S(2)}, u32[]{:S(2)}) collective-permute-start(bf16[16,96,128]{2,1,0:T(8,128)(2,1)S(1)} %get-tuple-element.139.a0), channel_id=1, source_target_pairs={{0,64},{64,0},{1,65},{65,1},{2,66},{66,2},{3,67},{67,3},{4,68},{68... | collective-permute-start | bytes 1179656 | tf_op jit(solution)/shard_map/ppermute | solution.py:578
  101.6 16.0 %collective-permute-start.9 = (bf16[16,96,128]{2,1,0:T(8,128)(2,1)S(1)}, bf16[16,96,128]{2,1,0:T(8,128)(2,1)S(1)}, u32[]{:S(2)}, u32[]{:S(2)}) collective-permute-start(bf16[16,96,128]{2,1,0:T(8,128)(2,1)S(1)} %get-tuple-element.139.a0), channel_id=1, source_target_pairs={{0,2},{2,0},{1,3},{3,1},{4,6},{6,4},{5,7},{7,5},{8,10},{10,8},{9,1... | collective-permute-start | bytes 1179656 | tf_op jit(solution)/shard_map/ppermute | solution.py:578
  116.9 1.7 collective-permute-start.12
  116.9 2.3 collective-permute-start.11
  117.6 2.1 collective-permute-start.10
  121.0 23.0 %copy-start = (bf16[1024,512]{1,0:T(8,128)(2,1)}, bf16[1024,512]{1,0:T(8,128)(2,1)S(1)}, u32[]{:S(2)}) copy-start(bf16[1024,512]{1,0:T(8,128)(2,1)S(1)} %get-tuple-element.87.w_down) | copy-start | bytes 3145732
  144.0 37.7 %all-to-all-start.3 = ((bf16[16,656,128]{2,1,0:T(8,128)(2,1)}), bf16[16,656,128]{2,1,0:T(8,128)(2,1)}, u32[]{:S(2)}, u32[]{:S(2)}) async-start(bf16[16,656,128]{2,1,0:T(8,128)(2,1)} %get-tuple-element.88), calls=%async_computation.3 | async-start | bytes 5373952 | tf_op jit(solution)/shard_map/all_to_all | solution.py:586
  158.3 3.6 %collective-permute-start.13 = (bf16[2,2,16,96,128]{4,3,2,1,0:T(8,128)(2,1)}, bf16[2,2,16,96,128]{4,3,2,1,0:T(8,128)(2,1)S(1)}, u32[]{:S(2)}, u32[]{:S(2)}) collective-permute-start(bf16[2,2,16,96,128]{4,3,2,1,0:T(8,128)(2,1)} %get-tuple-element.93), channel_id=1, source_target_pairs={{0,2},{2,0},{1,3},{3,1},{4,6},{6,4},{5,7},{7,5},{8,10},{10,8},{9,1... | collective-permute-start | bytes 4718600 | tf_op jit(solution)/shard_map/ppermute | solution.py:578
  161.9 3.0 %copy-start.2 = (bf16[2,2,16,96,128]{4,3,2,1,0:T(8,128)(2,1)}, bf16[2,2,16,96,128]{4,3,2,1,0:T(8,128)(2,1)S(1)}, u32[]{:S(2)}) copy-start(bf16[2,2,16,96,128]{4,3,2,1,0:T(8,128)(2,1)S(1)} %collective-permute-done.13.got) | copy-start | bytes 4718596
  164.9 12.3 %collective-permute-start.14 = (bf16[16,96,128]{2,1,0:T(8,128)(2,1)}, bf16[16,96,128]{2,1,0:T(8,128)(2,1)}, u32[]{:S(2)}, u32[]{:S(2)}) collective-permute-start(bf16[16,96,128]{2,1,0:T(8,128)(2,1)} %get-tuple-element.142), channel_id=1, source_target_pairs={{0,64},{64,0},{1,65},{65,1},{2,66},{66,2},{3,67},{67,3},{4,68},{68... | collective-permute-start | bytes 1179656 | tf_op jit(solution)/shard_map/ppermute | solution.py:578
  166.5 19.3 %collective-permute-start.16 = (bf16[16,96,128]{2,1,0:T(8,128)(2,1)}, bf16[16,96,128]{2,1,0:T(8,128)(2,1)}, u32[]{:S(2)}, u32[]{:S(2)}) collective-permute-start(bf16[16,96,128]{2,1,0:T(8,128)(2,1)} %get-tuple-element.140), channel_id=1, source_target_pairs={{0,65},{65,0},{1,64},{64,1},{2,67},{67,2},{3,66},{66,3},{4,69},{69... | collective-permute-start | bytes 1179656 | tf_op jit(solution)/shard_map/ppermute | solution.py:577
  168.6 18.7 %collective-permute-start.15 = (bf16[16,96,128]{2,1,0:T(8,128)(2,1)}, bf16[16,96,128]{2,1,0:T(8,128)(2,1)}, u32[]{:S(2)}, u32[]{:S(2)}) collective-permute-start(bf16[16,96,128]{2,1,0:T(8,128)(2,1)} %get-tuple-element.141), channel_id=1, source_target_pairs={{0,1},{1,0},{2,3},{3,2},{4,5},{5,4},{6,7},{7,6},{8,9},{9,8},{10,11... | collective-permute-start | bytes 1179656 | tf_op jit(solution)/shard_map/ppermute | solution.py:578
  187.3 16.3 %collective-permute-start.17 = (bf16[256,1152]{1,0:T(8,128)(2,1)}, bf16[256,1152]{1,0:T(8,128)(2,1)}, u32[]{:S(2)}, u32[]{:S(2)}) collective-permute-start(bf16[256,1152]{1,0:T(8,128)(2,1)} %shard_map.229.comb_own), channel_id=1, source_target_pairs={{0,1},{1,0},{2,3},{3,2},{4,5},{5,4},{6,7},{7,6},{8,9},{9,8},{10,11... | collective-permute-start | bytes 1769480 | tf_op jit(solution)/shard_map/ppermute | solution.py:578
  189.1 40.9 %all-to-all-start.4 = ((bf16[16,640,128]{2,1,0:T(8,128)(2,1)}), bf16[16,640,128]{2,1,0:T(8,128)(2,1)}, u32[]{:S(2)}, u32[]{:S(2)}) async-start(bf16[16,640,128]{2,1,0:T(8,128)(2,1)} %shard_map.228), calls=%async_computation.4 | async-start | bytes 5242880 | tf_op jit(solution)/shard_map/all_to_all | solution.py:586
  215.7 6.4 %collective-permute-start.21 = (bf16[2,16,16,1664]{3,2,1,0:T(8,128)(2,1)}, bf16[2,16,16,1664]{3,2,1,0:T(8,128)(2,1)}, u32[]{:S(2)}, u32[]{:S(2)}) collective-permute-start(bf16[2,16,16,1664]{3,2,1,0:T(8,128)(2,1)} %get-tuple-element.113), channel_id=1, source_target_pairs={{0,2},{2,0},{1,3},{3,1},{4,6},{6,4},{5,7},{7,5},{8,10},{10,8},{9,1... | collective-permute-start | bytes 5111816 | tf_op jit(solution)/shard_map/ppermute | solution.py:578
  215.8 4.9 %collective-permute-start.20 = (f32[8,128]{1,0:T(8,128)}, f32[8,128]{1,0:T(8,128)}, u32[]{:S(2)}, u32[]{:S(2)}) collective-permute-start(f32[8,128]{1,0:T(8,128)} %get-tuple-element.111.g_own), channel_id=1, source_target_pairs={{0,3},{3,0},{1,2},{2,1},{4,7},{7,4},{5,6},{6,5},{8,11},{11,8},{9,1... | collective-permute-start | bytes 12296 | tf_op jit(solution)/shard_map/ppermute | solution.py:575
  216.6 4.2 %collective-permute-start.19 = (f32[8,128]{1,0:T(8,128)}, f32[8,128]{1,0:T(8,128)}, u32[]{:S(2)}, u32[]{:S(2)}) collective-permute-start(f32[8,128]{1,0:T(8,128)} %get-tuple-element.111.g_own), channel_id=1, source_target_pairs={{0,2},{2,0},{1,3},{3,1},{4,6},{6,4},{5,7},{7,5},{8,10},{10,8},{9,1... | collective-permute-start | bytes 12296 | tf_op jit(solution)/shard_map/ppermute | solution.py:578
  216.7 5.4 %collective-permute-start.18 = (f32[8,128]{1,0:T(8,128)}, f32[8,128]{1,0:T(8,128)}, u32[]{:S(2)}, u32[]{:S(2)}) collective-permute-start(f32[8,128]{1,0:T(8,128)} %get-tuple-element.111.g_own), channel_id=1, source_target_pairs={{0,1},{1,0},{2,3},{3,2},{4,5},{5,4},{6,7},{7,6},{8,9},{9,8},{10,11... | collective-permute-start | bytes 12296 | tf_op jit(solution)/shard_map/ppermute | solution.py:578
  225.5 22.6 %collective-permute-start.22 = (bf16[16,16,1792]{2,1,0:T(8,128)(2,1)}, bf16[16,16,1792]{2,1,0:T(8,128)(2,1)}, u32[]{:S(2)}, u32[]{:S(2)}) collective-permute-start(bf16[16,16,1792]{2,1,0:T(8,128)(2,1)} %get-tuple-element.114), channel_id=1, source_target_pairs={{0,64},{64,0},{1,65},{65,1},{2,66},{66,2},{3,67},{67,3},{4,68},{68... | collective-permute-start | bytes 2752520 | tf_op jit(solution)/shard_map/ppermute | solution.py:578
  230.0 21.7 %all-to-all-start.5 = ((bf16[16,192,128]{2,1,0:T(8,128)(2,1)}), bf16[16,192,128]{2,1,0:T(8,128)(2,1)}, u32[]{:S(2)}, u32[]{:S(2)}) async-start(bf16[16,192,128]{2,1,0:T(8,128)(2,1)} %shard_map.230), calls=%async_computation.5 | async-start | bytes 1572864 | tf_op jit(solution)/shard_map/all_to_all | solution.py:586
  251.7 24.4 %all-to-all-start.6 = ((bf16[16,16,1792]{2,1,0:T(8,128)(2,1)}), bf16[16,16,1792]{2,1,0:T(8,128)(2,1)}, u32[]{:S(2)}, u32[]{:S(2)}) async-start(bf16[16,16,1792]{2,1,0:T(8,128)(2,1)} %shard_map.234), calls=%async_computation.6 | async-start | bytes 1835008 | tf_op jit(solution)/shard_map/all_to_all | solution.py:586
  258.9 14.4 %collective-permute-start.23 = (bf16[2,128,1024]{2,1,0:T(8,128)(2,1)}, bf16[2,128,1024]{2,1,0:T(8,128)(2,1)}, u32[]{:S(2)}, u32[]{:S(2)}) collective-permute-start(bf16[2,128,1024]{2,1,0:T(8,128)(2,1)} %get-tuple-element.121), channel_id=1, source_target_pairs={{0,1},{1,0},{2,3},{3,2},{4,5},{5,4},{6,7},{7,6},{8,9},{9,8},{10,11... | collective-permute-start | bytes 1572872 | tf_op jit(solution)/shard_map/ppermute | solution.py:578

commit v5 on v4

--- a/solution.py
+++ b/solution.py
@@ -819,17 +819,17 @@
     )
 
     rows_oth = swap(after(out_sent, a_sum), "yh")
-    rows_oth = after(rows_oth, grad_gate)
+    w_query, w_key, w_value, w_out, w_router, gain_two, gain_one = call(
+        final_kernel,
+        [((16, n), f32) for n in (512, 256, 256, 512, 32)] + [((1, 16), f32)] * 2,
+        [pos, total],
+        us=0,
+    )
+    rows_oth = after(rows_oth, grad_gate, w_query)
     input_grad, output = call(
         rows_kernel,
         [((HALF, D), bf16), ((HALF, D), bf16)],
         [pos, tokens, aux, mg_own, part_own, out_own, rows_oth],
-        us=0,
-    )
-    w_query, w_key, w_value, w_out, w_router, gain_two, gain_one = call(
-        final_kernel,
-        [((16, n), f32) for n in (512, 256, 256, 512, 32)] + [((1, 16), f32)] * 2,
-        [pos, total],
         us=0,
     )
 

time: 280 us -> 280 us (level)
    all_to_all x7, waiting for transfers between devices: 21.2 us -> 31.1 us  [plane(): return lax.all_to_all(value, PLANE, 0, 0, tiled=True)]
    ppermute x21, waiting for transfers between devices: 60.4 us -> 51.1 us  [swap(): return lax.ppermute(value, axis, [(0, 1), (1, 0)])]
  transfers between devices with their start and end apart: 31 -> 31, of which waited for: 21 -> 21; matrix products, arithmetic and copies ran while one was open for 4% -> 4% of each run, Pallas kernels for 26% -> 25%
where the time goes in v5:
time: 280 us; the launch traced here: 279 us
  waiting for transfers between devices  98.7 us (35%)
  Pallas kernels  86.6 us (31%)
  starting transfers between devices  78.9 us (28%)
  local copies, waits for them, and re-layouts  7.6 us (3%)
  other arithmetic  5.8 us (2%)
    pallas_call x14, Pallas kernels, call(): pl.pallas_call(kernel, out_shape=out_shape, in_specs=in_specs, out_specs=...  57.5 us
    ppermute x21, waiting for transfers between devices, swap(): return lax.ppermute(value, axis, [(0, 1), (1, 0)])  51.1 us
    all_to_all x7, starting transfers between devices, plane(): return lax.all_to_all(value, PLANE, 0, 0, tiled=True)  50.8 us
    all_to_all x7, waiting for transfers between devices, plane(): return lax.all_to_all(value, PLANE, 0, 0, tiled=True)  31.1 us
    ppermute x21, starting transfers between devices, swap(): return lax.ppermute(value, axis, [(0, 1), (1, 0)])  22.1 us
    pallas_call x3, Pallas kernels, call(): pl.pallas_call(kernel, grid=grid, out_shape=out_shape, in_specs=[smem] +...  19.3 us
    ppermute x2, waiting for transfers between devices, swap(): return lax.ppermute(value, ('yl', 'yh'), [(0, 3), (3, 0), (1, 2), (2, 1)])  15.3 us
    pallas_call x1, Pallas kernels, call(): pl.pallas_call(kernel, grid_spec=pltpu.PrefetchScalarGridSpec(num_scalar_...  9.83 us
  transfers between devices with their start and end apart: 31, of which 21 were waited for; matrix products, arithmetic and copies ran while one was open for 4% of the time, Pallas kernels for 25%

profile of v5, /device:TPU:0, one launch (start us, length us, event | category | flops | bytes accessed | tf_op | source)
XLA Modules:
  0.0 278.6 jit_solution(15213401998859705762)
XLA Ops:
  1.3 1.9 shard_map.220
  3.2 8.1 %all-to-all-start = ((bf16[16,16,1664]{2,1,0:T(8,128)(2,1)}), bf16[16,16,1664]{2,1,0:T(8,128)(2,1)}, u32[]{:S(2)}, u32[]{:S(2)}) async-start(bf16[16,16,1664]{2,1,0:T(8,128)(2,1)} %shard_map.220), calls=%async_computation | async-start | bytes 1703936 | tf_op jit(solution)/shard_map/all_to_all | solution.py:586
  11.3 3.3 %collective-permute-start.1 = (bf16[128,1024]{1,0:T(8,128)(2,1)}, bf16[128,1024]{1,0:T(8,128)(2,1)}, u32[]{:S(2)}, u32[]{:S(2)}) collective-permute-start(bf16[128,1024]{1,0:T(8,128)(2,1)} %cot_own.1), channel_id=1, source_target_pairs={{0,1},{1,0},{2,3},{3,2},{4,5},{5,4},{6,7},{7,6},{8,9},{9,8},{10,11... | collective-permute-start | bytes 786440 | tf_op jit(solution)/shard_map/ppermute | solution.py:578
  15.7 2.8 shard_map.221
  22.6 4.1 %shard_map.222 = (bf16[256,1024]{1,0:T(8,128)(2,1)}, bf16[16,832,128]{2,1,0:T(8,128)(2,1)}) custom-call(s32[7]{0:T(128)} %stack.43.pos, bf16[1280,256]{1,0:T(8,128)(2,1)} %get-tuple-element.75.tab, bf16[128,1024]{1,0:T(8,128)(2,1)} %cot_own.1, bf16[128,1024]{1,0:T(8,128)(2,1)} %collective-permute-done.1.cot_oth, bf16[16,192,128]{2,1,0:T(8,128)(2,1)} %bitcast.20), custom_call_target="tpu_custom_call" | custom-call | flops 3450000896 | bytes 5898268 | tf_op jit(solution)/shard_map/pallas_call | solution.py:63
  26.8 1.7 collective-permute-start.2
  29.5 7.1 %all-to-all-start.2 = ((bf16[16,832,128]{2,1,0:T(8,128)(2,1)}), bf16[16,832,128]{2,1,0:T(8,128)(2,1)}, u32[]{:S(2)}, u32[]{:S(2)}) async-start(bf16[16,832,128]{2,1,0:T(8,128)(2,1)} %get-tuple-element.84), calls=%async_computation.2 | async-start | bytes 6815744 | tf_op jit(solution)/shard_map/all_to_all | solution.py:586
  36.7 11.7 %collective-permute-done.2.w_b = bf16[16,16,1664]{2,1,0:T(8,128)(2,1)S(1)} collective-permute-done((bf16[16,16,1664]{2,1,0:T(8,128)(2,1)}, bf16[16,16,1664]{2,1,0:T(8,128)(2,1)S(1)}, u32[]{:S(2)}, u32[]{:S(2)}) %collective-permute-start.2) | collective-permute-done | bytes 852000 | tf_op jit(solution)/shard_map/ppermute | solution.py:578
  49.4 1.8 negate_select_fusion
  52.7 8.0 %shard_map.223 = (bf16[256,1024]{1,0:T(8,128)(2,1)}, bf16[256,1024]{1,0:T(8,128)(2,1)}, f32[128,1024]{1,0:T(8,128)}, bf16[256,1024]{1,0:T(8,128)(2,1)}, bf16[256...) custom-call(s32[7]{0:T(128)} %stack.43.pos, ...), custom_call_target="tpu_custom_call" | custom-call | flops 8050000896 | bytes 8650780 | tf_op jit(solution)/shard_map/pallas_call | solution.py:63
  60.7 3.3 %collective-permute-start.5 = (bf16[256,1024]{1,0:T(8,128)(2,1)}, bf16[256,1024]{1,0:T(8,128)(2,1)}, u32[]{:S(2)}, u32[]{:S(2)}) collective-permute-start(bf16[256,1024]{1,0:T(8,128)(2,1)} %get-tuple-element.81.part_own), channel_id=1, source_target_pairs={{0,1},{1,0},{2,3},{3,2},{4,5},{5,4},{6,7},{7,6},{8,9},{9,8},{10,11... | collective-permute-start | bytes 1572872 | tf_op jit(solution)/shard_map/ppermute | solution.py:578
  63.9 12.6 %collective-permute-done.5.part_oth = bf16[256,1024]{1,0:T(8,128)(2,1)} collective-permute-done((bf16[256,1024]{1,0:T(8,128)(2,1)}, bf16[256,1024]{1,0:T(8,128)(2,1)}, u32[]{:S(2)}, u32[]{:S(2)}) %collective-permute-start.5) | collective-permute-done | bytes 524320 | tf_op jit(solution)/shard_map/ppermute | solution.py:578
  76.5 4.9 %shard_map.224 = (f32[256,128]{1,0:T(8,128)}, f32[256,1024]{1,0:T(8,128)}, bf16[256,1024]{1,0:T(8,128)(2,1)}, bf16[16,656,128]{2,1,0:T(8,128)(2,1)}) custom-call(s32[7]{0:T(128)} %stack.43.pos, bf16[256,1024]{1,0:T(8,128)(2,1)} %get-tuple-element.80.rows.rows_at, bf16[256,1024]{1,0:T(8,128)(2,1)} %get-tuple-element.81.part_own, ...), custom_call_target="tpu_custom_call" | custom-call | flops 3450000896 | bytes 7274524 | tf_op jit(solution)/shard_map/pallas_call | solution.py:63
  81.4 2.8 %all-to-all-done.2.c = bf16[16,832,128]{2,1,0:T(8,128)(2,1)} async-done(((bf16[16,832,128]{2,1,0:T(8,128)(2,1)}), bf16[16,832,128]{2,1,0:T(8,128)(2,1)}, u32[]{:S(2)}, u32[]{:S(2)}) %all-to-all-start.2) | async-done | bytes 3407904 | tf_op jit(solution)/shard_map/all_to_all | solution.py:586
  84.3 12.0 %all-to-all-start.1 = ((bf16[16,656,128]{2,1,0:T(8,128)(2,1)}), bf16[16,656,128]{2,1,0:T(8,128)(2,1)}, u32[]{:S(2)}, u32[]{:S(2)}) async-start(bf16[16,656,128]{2,1,0:T(8,128)(2,1)} %get-tuple-element.83), calls=%async_computation.1 | async-start | bytes 5373952 | tf_op jit(solution)/shard_map/all_to_all | solution.py:586
  97.4 3.1 %collective-permute-start.8 = (bf16[16,96,128]{2,1,0:T(8,128)(2,1)S(1)}, bf16[16,96,128]{2,1,0:T(8,128)(2,1)S(1)}, u32[]{:S(2)}, u32[]{:S(2)}) collective-permute-start(bf16[16,96,128]{2,1,0:T(8,128)(2,1)S(1)} %get-tuple-element.138), channel_id=1, source_target_pairs={{0,65},{65,0},{1,64},{64,1},{2,67},{67,2},{3,66},{66,3},{4,69},{69... | collective-permute-start | bytes 1179656 | tf_op jit(solution)/shard_map/ppermute | solution.py:577
  101.6 15.3 %collective-permute-done.8.a3 = bf16[16,96,128]{2,1,0:T(8,128)(2,1)S(1)} collective-permute-done((bf16[16,96,128]{2,1,0:T(8,128)(2,1)S(1)}, bf16[16,96,128]{2,1,0:T(8,128)(2,1)S(1)}, u32[]{:S(2)}, u32[]{:S(2)}) %collective-permute-start.8) | collective-permute-done | bytes 393248 | tf_op jit(solution)/shard_map/ppermute | solution.py:577
  121.0 11.5 %all-to-all-done.1.x = bf16[16,656,128]{2,1,0:T(8,128)(2,1)} async-done(((bf16[16,656,128]{2,1,0:T(8,128)(2,1)}), bf16[16,656,128]{2,1,0:T(8,128)(2,1)}, u32[]{:S(2)}, u32[]{:S(2)}) %all-to-all-start.1) | async-done | bytes 2687008 | tf_op jit(solution)/shard_map/all_to_all | solution.py:586
  132.5 11.5 %shard_map.226 = (bf16[16,656,128]{2,1,0:T(8,128)(2,1)}, bf16[1280,512]{1,0:T(8,128)(2,1)}, bf16[1280,512]{1,0:T(8,128)(2,1)}, bf16[1280,512]{1,0:T(8,128)(2,1)}) custom-call(s32[7]{0:T(128)S(1)} %copy-done.1, bf16[16,656,128]{2,1,0:T(8,128)(2,1)} %all-to-all-done.1.x, bf16[16,832,128]{2,1,0:T(8,128)(2,1)} %all-to-all-done.2.c, ...), custom_call_target="tpu_custom_call" | custom-call | flops 13800000512 | bytes 15859740 | tf_op jit(solution)/shard_map/pallas_call | solution.py:73
  144.0 4.5 %all-to-all-start.3 = ((bf16[16,656,128]{2,1,0:T(8,128)(2,1)}), bf16[16,656,128]{2,1,0:T(8,128)(2,1)}, u32[]{:S(2)}, u32[]{:S(2)}) async-start(bf16[16,656,128]{2,1,0:T(8,128)(2,1)} %get-tuple-element.88), calls=%async_computation.3 | async-start | bytes 5373952 | tf_op jit(solution)/shard_map/all_to_all | solution.py:586
  148.4 9.8 %shard_map.227 = (bf16[2,2,16,96,128]{4,3,2,1,0:T(8,128)(2,1)}, bf16[2,2,16,96,128]{4,3,2,1,0:T(8,128)(2,1)}) custom-call(s32[7]{0:T(128)} %stack.43.pos, bf16[16,656,128]{2,1,0:T(8,128)(2,1)} %all-to-all-done.1.x, bf16[16,832,128]{2,1,0:T(8,128)(2,1)} %all-to-all-done.2.c, bf16[1280,512]{1,0:T(8,128)(2,1)} %get-tuple-element.89.gate_g, ...), custom_call_target="tpu_custom_call" | custom-call | flops 1000 | bytes 1000 | tf_op jit(solution)/shard_map/pallas_call | solution.py:83
  158.3 3.6 %collective-permute-done.13.got = bf16[2,2,16,96,128]{4,3,2,1,0:T(8,128)(2,1)S(1)} collective-permute-done((bf16[2,2,16,96,128]{4,3,2,1,0:T(8,128)(2,1)}, bf16[2,2,16,96,128]{4,3,2,1,0:T(8,128)(2,1)S(1)}, u32[]{:S(2)}, u32[]{:S(2)}) %collective-permute-start.13) | collective-permute-done | bytes 1572896 | tf_op jit(solution)/shard_map/ppermute | solution.py:578
  161.9 3.0 %fusion.2 = (bf16[16,96,128]{2,1,0:T(8,128)(2,1)}, bf16[16,96,128]{2,1,0:T(8,128)(2,1)}, bf16[16,96,128]{2,1,0:T(8,128)(2,1)}) fusion(bf16[2,2,16,96,128]{4,3,2,1,0:T(8,128)(2,1)S(1)} %collective-permute-done.13.got, bf16[2,2,16,96,128]{4,3,2,1,0:T(8,128)(2,1)} %get-tuple-element.97.mine), kind=kLoop, calls=%fused_computation.6 | loop fusion | flops 2359296 | bytes 3538944 | tf_op jit(solution)/shard_map/convert_element_type | solution.py:593
  164.9 1.6 collective-permute-start.14
  166.5 2.2 collective-permute-start.16
  169.4 5.2 %shard_map.228 = bf16[16,640,128]{2,1,0:T(8,128)(2,1)} custom-call(s32[7]{0:T(128)} %stack.43.pos, bf16[1280,512]{1,0:T(8,128)(2,1)} %get-tuple-element.94.scaled, bf16[1024,512]{1,0:T(8,128)(2,1)} %copy-done), custom_call_target="tpu_custom_call" | custom-call | flops 1000 | bytes 1000 | tf_op jit(solution)/shard_map/pallas_call | solution.py:73
  174.6 2.6 collective-permute-done.14.got_yl
  177.2 4.5 %all-to-all-done.3.got = bf16[16,656,128]{2,1,0:T(8,128)(2,1)} async-done(((bf16[16,656,128]{2,1,0:T(8,128)(2,1)}), bf16[16,656,128]{2,1,0:T(8,128)(2,1)}, u32[]{:S(2)}, u32[]{:S(2)}) %all-to-all-start.3) | async-done | bytes 2687008 | tf_op jit(solution)/shard_map/all_to_all | solution.py:586
  181.7 4.1 %shard_map.229.comb_own = bf16[256,1152]{1,0:T(8,128)(2,1)} custom-call(s32[7]{0:T(128)} %stack.43.pos, bf16[256,1280]{1,0:T(8,128)(2,1)} %get-tuple-element.79.tab_t, bf16[16,656,128]{2,1,0:T(8,128)(2,1)} %all-to-all-done.3.got), custom_call_target="tpu_custom_call" | custom-call | flops 1000 | bytes 1000 | tf_op jit(solution)/shard_map/pallas_call | solution.py:63
  187.3 1.8 collective-permute-start.17
  189.1 7.1 %all-to-all-start.4 = ((bf16[16,640,128]{2,1,0:T(8,128)(2,1)}), bf16[16,640,128]{2,1,0:T(8,128)(2,1)}, u32[]{:S(2)}, u32[]{:S(2)}) async-start(bf16[16,640,128]{2,1,0:T(8,128)(2,1)} %shard_map.228), calls=%async_computation.4 | async-start | bytes 5242880 | tf_op jit(solution)/shard_map/all_to_all | solution.py:586
  196.2 2.6 shard_map.230
  198.8 4.8 %collective-permute-done.17.comb_oth = bf16[256,1152]{1,0:T(8,128)(2,1)} collective-permute-done((bf16[256,1152]{1,0:T(8,128)(2,1)}, bf16[256,1152]{1,0:T(8,128)(2,1)}, u32[]{:S(2)}, u32[]{:S(2)}) %collective-permute-start.17) | collective-permute-done | bytes 589856 | tf_op jit(solution)/shard_map/ppermute | solution.py:578
  203.6 12.1 %shard_map.231 = (bf16[128,1024]{1,0:T(8,128)(2,1)}, f32[8,128]{1,0:T(8,128)}, f32[128,1024]{1,0:T(8,128)}, f32[128,1024]{1,0:T(8,128)}, bf16[2,16,16,1664]{3,2,...) custom-call(s32[7]{0:T(128)} %stack.43.pos, bf16[256,1152]{1,0:T(8,128)(2,1)} %shard_map.229.comb_own, ...), custom_call_target="tpu_custom_call" | custom-call | flops 1000 | bytes 1000 | tf_op jit(solution)/shard_map/pallas_call | solution.py:63
  216.7 2.9 %collective-permute-start.18 = (f32[8,128]{1,0:T(8,128)}, f32[8,128]{1,0:T(8,128)}, u32[]{:S(2)}, u32[]{:S(2)}) collective-permute-start(f32[8,128]{1,0:T(8,128)} %get-tuple-element.111.g_own), channel_id=1, source_target_pairs={{0,1},{1,0},{2,3},{3,2},{4,5},{5,4},{6,7},{7,6},{8,9},{9,8},{10,11... | collective-permute-start | bytes 12296 | tf_op jit(solution)/shard_map/ppermute | solution.py:578
  222.1 3.4 %shard_map.232 = (bf16[16,16,1792]{2,1,0:T(8,128)(2,1)}, f32[16,128]{1,0:T(8,128)}) custom-call(s32[7]{0:T(128)} %stack.43.pos, f32[8,128]{1,0:T(8,128)} %get-tuple-element.111.g_own, f32[8,128]{1,0:T(8,128)} %collective-permute-done.18.g_yh, f32[8,128]{1,0:T(8,128)} %collective-permute-done.19.g_core, f32[8,128]{1,0:T(8,128)} %collective-permute-done.20.g_twist, ...), custom_call_target="tpu_custom_call" | custom-call | flops 1000 | bytes 1000 | tf_op jit(solution)/shard_map/pallas_call | solution.py:63
  225.5 2.2 collective-permute-start.22
  227.6 2.4 all-to-all-done.4.got
  230.0 4.8 %all-to-all-start.5 = ((bf16[16,192,128]{2,1,0:T(8,128)(2,1)}), bf16[16,192,128]{2,1,0:T(8,128)(2,1)}, u32[]{:S(2)}, u32[]{:S(2)}) async-start(bf16[16,192,128]{2,1,0:T(8,128)(2,1)} %shard_map.230), calls=%async_computation.5 | async-start | bytes 1572864 | tf_op jit(solution)/shard_map/all_to_all | solution.py:586
  234.8 4.3 %shard_map.233 = (f32[128,1024]{1,0:T(8,128)}, bf16[2,128,1024]{2,1,0:T(8,128)(2,1)}) custom-call(s32[7]{0:T(128)} %stack.43.pos, bf16[256,1280]{1,0:T(8,128)(2,1)} %get-tuple-element.79.tab_t, f32[256,1024]{1,0:T(8,128)} %get-tuple-element.99.middle, bf16[16,640,128]{2,1,0:T(8,128)(2,1)} %all-to-all-done.4.got, bf16[128,1024]{1,0:T(8,128)(2,1)} %get-tuple-element.116.part_sent), custom_call_target="tpu_custom_call" | custom-call | flops 1000 | bytes 1000 | tf_op jit(solution)/shard_map/pallas_call | solution.py:63
  239.1 9.0 %collective-permute-done.22.got_yl_at = bf16[16,16,1792]{2,1,0:T(8,128)(2,1)} collective-permute-done((bf16[16,16,1792]{2,1,0:T(8,128)(2,1)}, bf16[16,16,1792]{2,1,0:T(8,128)(2,1)}, u32[]{:S(2)}, u32[]{:S(2)}) %collective-permute-start.22) | collective-permute-done | bytes 917536 | tf_op jit(solution)/shard_map/ppermute | solution.py:578
  248.1 3.6 %shard_map.234 = bf16[16,16,1792]{2,1,0:T(8,128)(2,1)} custom-call(s32[7]{0:T(128)} %stack.43.pos, f32[16,128]{1,0:T(8,128)} %get-tuple-element.119.gain, bf16[2,16,16,1664]{3,2,1,0:T(8,128)(2,1)} %get-tuple-element.112.mine_at, bf16[2,16,16,1664]{3,2,1,0:T(8,128)(2,1)} %collective-permute-done.21.got_at, bf16[16,16,1792]{2,1,0:T(8,128)(2,1)} %collective-permute-done.22.got_yl_at), custom_call_target="tpu_custom_call" | custom-call | flops 1000 | bytes 1000 | tf_op jit(solution)/shard_map/pallas_call | solution.py:63
  251.7 7.2 %all-to-all-start.6 = ((bf16[16,16,1792]{2,1,0:T(8,128)(2,1)}), bf16[16,16,1792]{2,1,0:T(8,128)(2,1)}, u32[]{:S(2)}, u32[]{:S(2)}) async-start(bf16[16,16,1792]{2,1,0:T(8,128)(2,1)} %shard_map.234), calls=%async_computation.6 | async-start | bytes 1835008 | tf_op jit(solution)/shard_map/all_to_all | solution.py:586
  258.9 2.6 collective-permute-start.23
  261.5 2.5 shard_map.235
  264.0 9.8 %all-to-all-done.6.got = bf16[16,16,1792]{2,1,0:T(8,128)(2,1)} async-done(((bf16[16,16,1792]{2,1,0:T(8,128)(2,1)}), bf16[16,16,1792]{2,1,0:T(8,128)(2,1)}, u32[]{:S(2)}, u32[]{:S(2)}) %all-to-all-start.6) | async-done | bytes 917536 | tf_op jit(solution)/shard_map/all_to_all | solution.py:586
  273.8 1.9 shard_map.236
  275.7 2.8 %shard_map.237 = (bf16[128,1024]{1,0:T(8,128)(2,1)}, bf16[128,1024]{1,0:T(8,128)(2,1)}) custom-call(s32[7]{0:T(128)} %stack.43.pos, bf16[128,1024]{1,0:T(8,128)(2,1)} %tok.1, f32[128,1024]{1,0:T(8,128)} %get-tuple-element.78.aux, f32[128,1024]{1,0:T(8,128)} %get-tuple-element.109.mg, f32[128,1024]{1,0:T(8,128)} %get-tuple-element.110.part_own, ...), custom_call_target="tpu_custom_call" | custom-call | flops 1000 | bytes 1000 | tf_op jit(solution)/shard_map/pallas_call | solution.py:63
  (62 shorter events, 21.5 us)
Async XLA Ops:
  3.2 11.4 %copy-start.6 = (s32[256,8]{0,1:T(8,128)S(1)}, s32[256,8]{0,1:T(8,128)}, u32[]{:S(2)}) copy-start(s32[256,8]{0,1:T(8,128)} %param.14) | copy-start | bytes 24580
  3.2 23.5 %all-to-all-start = ((bf16[16,16,1664]{2,1,0:T(8,128)(2,1)}), bf16[16,16,1664]{2,1,0:T(8,128)(2,1)}, u32[]{:S(2)}, u32[]{:S(2)}) async-start(bf16[16,16,1664]{2,1,0:T(8,128)(2,1)} %shard_map.220), calls=%async_computation | async-start | bytes 1703936 | tf_op jit(solution)/shard_map/all_to_all | solution.py:586
  11.3 11.3 %collective-permute-start.1 = (bf16[128,1024]{1,0:T(8,128)(2,1)}, bf16[128,1024]{1,0:T(8,128)(2,1)}, u32[]{:S(2)}, u32[]{:S(2)}) collective-permute-start(bf16[128,1024]{1,0:T(8,128)(2,1)} %cot_own.1), channel_id=1, source_target_pairs={{0,1},{1,0},{2,3},{3,2},{4,5},{5,4},{6,7},{7,6},{8,9},{9,8},{10,11... | collective-permute-start | bytes 786440 | tf_op jit(solution)/shard_map/ppermute | solution.py:578
  15.4 11.3 %collective-permute-start = (bf16[128,1024]{1,0:T(8,128)(2,1)}, bf16[128,1024]{1,0:T(8,128)(2,1)}, u32[]{:S(2)}, u32[]{:S(2)}) collective-permute-start(bf16[128,1024]{1,0:T(8,128)(2,1)} %tok.1), channel_id=1, source_target_pairs={{0,1},{1,0},{2,3},{3,2},{4,5},{5,4},{6,7},{7,6},{8,9},{9,8},{10,11... | collective-permute-start | bytes 786440 | tf_op jit(solution)/shard_map/ppermute | solution.py:578
  18.5 2.7 copy-start.5
  26.7 2.8 %collective-permute-start.3 = (bf16[16,16,1664]{2,1,0:T(8,128)(2,1)}, bf16[16,16,1664]{2,1,0:T(8,128)(2,1)}, u32[]{:S(2)}, u32[]{:S(2)}) collective-permute-start(bf16[16,16,1664]{2,1,0:T(8,128)(2,1)} %all-to-all-done.w_a), channel_id=1, source_target_pairs={{0,2},{2,0},{1,3},{3,1},{4,6},{6,4},{5,7},{7,5},{8,10},{10,8},{9,1... | collective-permute-start | bytes 2555912 | tf_op jit(solution)/shard_map/ppermute | solution.py:578
  26.8 21.6 %collective-permute-start.2 = (bf16[16,16,1664]{2,1,0:T(8,128)(2,1)}, bf16[16,16,1664]{2,1,0:T(8,128)(2,1)S(1)}, u32[]{:S(2)}, u32[]{:S(2)}) collective-permute-start(bf16[16,16,1664]{2,1,0:T(8,128)(2,1)} %all-to-all-done.w_a), channel_id=1, source_target_pairs={{0,64},{64,0},{1,65},{65,1},{2,66},{66,2},{3,67},{67,3},{4,68},{68... | collective-permute-start | bytes 2555912 | tf_op jit(solution)/shard_map/ppermute | solution.py:578
  29.5 54.7 %all-to-all-start.2 = ((bf16[16,832,128]{2,1,0:T(8,128)(2,1)}), bf16[16,832,128]{2,1,0:T(8,128)(2,1)}, u32[]{:S(2)}, u32[]{:S(2)}) async-start(bf16[16,832,128]{2,1,0:T(8,128)(2,1)} %get-tuple-element.84), calls=%async_computation.2 | async-start | bytes 6815744 | tf_op jit(solution)/shard_map/all_to_all | solution.py:586
  48.4 0.9 copy-start.3
  49.3 2.4 collective-permute-start.4
  51.7 1.0 copy-start.4
  60.7 15.9 %collective-permute-start.5 = (bf16[256,1024]{1,0:T(8,128)(2,1)}, bf16[256,1024]{1,0:T(8,128)(2,1)}, u32[]{:S(2)}, u32[]{:S(2)}) collective-permute-start(bf16[256,1024]{1,0:T(8,128)(2,1)} %get-tuple-element.81.part_own), channel_id=1, source_target_pairs={{0,1},{1,0},{2,3},{3,2},{4,5},{5,4},{6,7},{7,6},{8,9},{9,8},{10,11... | collective-permute-start | bytes 1572872 | tf_op jit(solution)/shard_map/ppermute | solution.py:578
  84.3 35.5 %copy-start.1 = (s32[7]{0:T(128)S(1)}, s32[7]{0:T(128)}, u32[]{:S(2)}) copy-start(s32[7]{0:T(128)} %stack.43.pos) | copy-start | bytes 88
  84.3 48.2 %all-to-all-start.1 = ((bf16[16,656,128]{2,1,0:T(8,128)(2,1)}), bf16[16,656,128]{2,1,0:T(8,128)(2,1)}, u32[]{:S(2)}, u32[]{:S(2)}) async-start(bf16[16,656,128]{2,1,0:T(8,128)(2,1)} %get-tuple-element.83), calls=%async_computation.1 | async-start | bytes 5373952 | tf_op jit(solution)/shard_map/all_to_all | solution.py:586
  97.4 19.5 %collective-permute-start.8 = (bf16[16,96,128]{2,1,0:T(8,128)(2,1)S(1)}, bf16[16,96,128]{2,1,0:T(8,128)(2,1)S(1)}, u32[]{:S(2)}, u32[]{:S(2)}) collective-permute-start(bf16[16,96,128]{2,1,0:T(8,128)(2,1)S(1)} %get-tuple-element.138), channel_id=1, source_target_pairs={{0,65},{65,0},{1,64},{64,1},{2,67},{67,2},{3,66},{66,3},{4,69},{69... | collective-permute-start | bytes 1179656 | tf_op jit(solution)/shard_map/ppermute | solution.py:577
  100.5 16.4 %collective-permute-start.7 = (bf16[16,96,128]{2,1,0:T(8,128)(2,1)S(1)}, bf16[16,96,128]{2,1,0:T(8,128)(2,1)S(1)}, u32[]{:S(2)}, u32[]{:S(2)}) collective-permute-start(bf16[16,96,128]{2,1,0:T(8,128)(2,1)S(1)} %get-tuple-element.138), channel_id=1, source_target_pairs={{0,1},{1,0},{2,3},{3,2},{4,5},{5,4},{6,7},{7,6},{8,9},{9,8},{10,11... | collective-permute-start | bytes 1179656 | tf_op jit(solution)/shard_map/ppermute | solution.py:578
  101.1 16.5 %collective-permute-start.6 = (bf16[16,96,128]{2,1,0:T(8,128)(2,1)S(1)}, bf16[16,96,128]{2,1,0:T(8,128)(2,1)S(1)}, u32[]{:S(2)}, u32[]{:S(2)}) collective-permute-start(bf16[16,96,128]{2,1,0:T(8,128)(2,1)S(1)} %get-tuple-element.139.a0), channel_id=1, source_target_pairs={{0,64},{64,0},{1,65},{65,1},{2,66},{66,2},{3,67},{67,3},{4,68},{68... | collective-permute-start | bytes 1179656 | tf_op jit(solution)/shard_map/ppermute | solution.py:578
  101.6 16.0 %collective-permute-start.9 = (bf16[16,96,128]{2,1,0:T(8,128)(2,1)S(1)}, bf16[16,96,128]{2,1,0:T(8,128)(2,1)S(1)}, u32[]{:S(2)}, u32[]{:S(2)}) collective-permute-start(bf16[16,96,128]{2,1,0:T(8,128)(2,1)S(1)} %get-tuple-element.139.a0), channel_id=1, source_target_pairs={{0,2},{2,0},{1,3},{3,1},{4,6},{6,4},{5,7},{7,5},{8,10},{10,8},{9,1... | collective-permute-start | bytes 1179656 | tf_op jit(solution)/shard_map/ppermute | solution.py:578
  116.9 1.7 collective-permute-start.12
  116.9 2.3 collective-permute-start.11
  117.6 2.1 collective-permute-start.10
  121.0 23.0 %copy-start = (bf16[1024,512]{1,0:T(8,128)(2,1)}, bf16[1024,512]{1,0:T(8,128)(2,1)S(1)}, u32[]{:S(2)}) copy-start(bf16[1024,512]{1,0:T(8,128)(2,1)S(1)} %get-tuple-element.87.w_down) | copy-start | bytes 3145732
  144.0 37.7 %all-to-all-start.3 = ((bf16[16,656,128]{2,1,0:T(8,128)(2,1)}), bf16[16,656,128]{2,1,0:T(8,128)(2,1)}, u32[]{:S(2)}, u32[]{:S(2)}) async-start(bf16[16,656,128]{2,1,0:T(8,128)(2,1)} %get-tuple-element.88), calls=%async_computation.3 | async-start | bytes 5373952 | tf_op jit(solution)/shard_map/all_to_all | solution.py:586
  158.3 3.6 %collective-permute-start.13 = (bf16[2,2,16,96,128]{4,3,2,1,0:T(8,128)(2,1)}, bf16[2,2,16,96,128]{4,3,2,1,0:T(8,128)(2,1)S(1)}, u32[]{:S(2)}, u32[]{:S(2)}) collective-permute-start(bf16[2,2,16,96,128]{4,3,2,1,0:T(8,128)(2,1)} %get-tuple-element.93), channel_id=1, source_target_pairs={{0,2},{2,0},{1,3},{3,1},{4,6},{6,4},{5,7},{7,5},{8,10},{10,8},{9,1... | collective-permute-start | bytes 4718600 | tf_op jit(solution)/shard_map/ppermute | solution.py:578
  161.9 3.0 %copy-start.2 = (bf16[2,2,16,96,128]{4,3,2,1,0:T(8,128)(2,1)}, bf16[2,2,16,96,128]{4,3,2,1,0:T(8,128)(2,1)S(1)}, u32[]{:S(2)}) copy-start(bf16[2,2,16,96,128]{4,3,2,1,0:T(8,128)(2,1)S(1)} %collective-permute-done.13.got) | copy-start | bytes 4718596
  164.9 12.3 %collective-permute-start.14 = (bf16[16,96,128]{2,1,0:T(8,128)(2,1)}, bf16[16,96,128]{2,1,0:T(8,128)(2,1)}, u32[]{:S(2)}, u32[]{:S(2)}) collective-permute-start(bf16[16,96,128]{2,1,0:T(8,128)(2,1)} %get-tuple-element.142), channel_id=1, source_target_pairs={{0,64},{64,0},{1,65},{65,1},{2,66},{66,2},{3,67},{67,3},{4,68},{68... | collective-permute-start | bytes 1179656 | tf_op jit(solution)/shard_map/ppermute | solution.py:578
  166.5 19.3 %collective-permute-start.16 = (bf16[16,96,128]{2,1,0:T(8,128)(2,1)}, bf16[16,96,128]{2,1,0:T(8,128)(2,1)}, u32[]{:S(2)}, u32[]{:S(2)}) collective-permute-start(bf16[16,96,128]{2,1,0:T(8,128)(2,1)} %get-tuple-element.140), channel_id=1, source_target_pairs={{0,65},{65,0},{1,64},{64,1},{2,67},{67,2},{3,66},{66,3},{4,69},{69... | collective-permute-start | bytes 1179656 | tf_op jit(solution)/shard_map/ppermute | solution.py:577
  168.6 18.7 %collective-permute-start.15 = (bf16[16,96,128]{2,1,0:T(8,128)(2,1)}, bf16[16,96,128]{2,1,0:T(8,128)(2,1)}, u32[]{:S(2)}, u32[]{:S(2)}) collective-permute-start(bf16[16,96,128]{2,1,0:T(8,128)(2,1)} %get-tuple-element.141), channel_id=1, source_target_pairs={{0,1},{1,0},{2,3},{3,2},{4,5},{5,4},{6,7},{7,6},{8,9},{9,8},{10,11... | collective-permute-start | bytes 1179656 | tf_op jit(solution)/shard_map/ppermute | solution.py:578
  187.3 16.3 %collective-permute-start.17 = (bf16[256,1152]{1,0:T(8,128)(2,1)}, bf16[256,1152]{1,0:T(8,128)(2,1)}, u32[]{:S(2)}, u32[]{:S(2)}) collective-permute-start(bf16[256,1152]{1,0:T(8,128)(2,1)} %shard_map.229.comb_own), channel_id=1, source_target_pairs={{0,1},{1,0},{2,3},{3,2},{4,5},{5,4},{6,7},{7,6},{8,9},{9,8},{10,11... | collective-permute-start | bytes 1769480 | tf_op jit(solution)/shard_map/ppermute | solution.py:578
  189.1 40.9 %all-to-all-start.4 = ((bf16[16,640,128]{2,1,0:T(8,128)(2,1)}), bf16[16,640,128]{2,1,0:T(8,128)(2,1)}, u32[]{:S(2)}, u32[]{:S(2)}) async-start(bf16[16,640,128]{2,1,0:T(8,128)(2,1)} %shard_map.228), calls=%async_computation.4 | async-start | bytes 5242880 | tf_op jit(solution)/shard_map/all_to_all | solution.py:586
  215.7 6.4 %collective-permute-start.21 = (bf16[2,16,16,1664]{3,2,1,0:T(8,128)(2,1)}, bf16[2,16,16,1664]{3,2,1,0:T(8,128)(2,1)}, u32[]{:S(2)}, u32[]{:S(2)}) collective-permute-start(bf16[2,16,16,1664]{3,2,1,0:T(8,128)(2,1)} %get-tuple-element.113), channel_id=1, source_target_pairs={{0,2},{2,0},{1,3},{3,1},{4,6},{6,4},{5,7},{7,5},{8,10},{10,8},{9,1... | collective-permute-start | bytes 5111816 | tf_op jit(solution)/shard_map/ppermute | solution.py:578
  215.8 4.9 %collective-permute-start.20 = (f32[8,128]{1,0:T(8,128)}, f32[8,128]{1,0:T(8,128)}, u32[]{:S(2)}, u32[]{:S(2)}) collective-permute-start(f32[8,128]{1,0:T(8,128)} %get-tuple-element.111.g_own), channel_id=1, source_target_pairs={{0,3},{3,0},{1,2},{2,1},{4,7},{7,4},{5,6},{6,5},{8,11},{11,8},{9,1... | collective-permute-start | bytes 12296 | tf_op jit(solution)/shard_map/ppermute | solution.py:575
  216.6 4.2 %collective-permute-start.19 = (f32[8,128]{1,0:T(8,128)}, f32[8,128]{1,0:T(8,128)}, u32[]{:S(2)}, u32[]{:S(2)}) collective-permute-start(f32[8,128]{1,0:T(8,128)} %get-tuple-element.111.g_own), channel_id=1, source_target_pairs={{0,2},{2,0},{1,3},{3,1},{4,6},{6,4},{5,7},{7,5},{8,10},{10,8},{9,1... | collective-permute-start | bytes 12296 | tf_op jit(solution)/shard_map/ppermute | solution.py:578
  216.7 5.4 %collective-permute-start.18 = (f32[8,128]{1,0:T(8,128)}, f32[8,128]{1,0:T(8,128)}, u32[]{:S(2)}, u32[]{:S(2)}) collective-permute-start(f32[8,128]{1,0:T(8,128)} %get-tuple-element.111.g_own), channel_id=1, source_target_pairs={{0,1},{1,0},{2,3},{3,2},{4,5},{5,4},{6,7},{7,6},{8,9},{9,8},{10,11... | collective-permute-start | bytes 12296 | tf_op jit(solution)/shard_map/ppermute | solution.py:578
  225.5 22.6 %collective-permute-start.22 = (bf16[16,16,1792]{2,1,0:T(8,128)(2,1)}, bf16[16,16,1792]{2,1,0:T(8,128)(2,1)}, u32[]{:S(2)}, u32[]{:S(2)}) collective-permute-start(bf16[16,16,1792]{2,1,0:T(8,128)(2,1)} %get-tuple-element.114), channel_id=1, source_target_pairs={{0,64},{64,0},{1,65},{65,1},{2,66},{66,2},{3,67},{67,3},{4,68},{68... | collective-permute-start | bytes 2752520 | tf_op jit(solution)/shard_map/ppermute | solution.py:578
  230.0 21.7 %all-to-all-start.5 = ((bf16[16,192,128]{2,1,0:T(8,128)(2,1)}), bf16[16,192,128]{2,1,0:T(8,128)(2,1)}, u32[]{:S(2)}, u32[]{:S(2)}) async-start(bf16[16,192,128]{2,1,0:T(8,128)(2,1)} %shard_map.230), calls=%async_computation.5 | async-start | bytes 1572864 | tf_op jit(solution)/shard_map/all_to_all | solution.py:586
  251.7 22.1 %all-to-all-start.6 = ((bf16[16,16,1792]{2,1,0:T(8,128)(2,1)}), bf16[16,16,1792]{2,1,0:T(8,128)(2,1)}, u32[]{:S(2)}, u32[]{:S(2)}) async-start(bf16[16,16,1792]{2,1,0:T(8,128)(2,1)} %shard_map.234), calls=%async_computation.6 | async-start | bytes 1835008 | tf_op jit(solution)/shard_map/all_to_all | solution.py:586
  258.9 16.9 %collective-permute-start.23 = (bf16[2,128,1024]{2,1,0:T(8,128)(2,1)}, bf16[2,128,1024]{2,1,0:T(8,128)(2,1)}, u32[]{:S(2)}, u32[]{:S(2)}) collective-permute-start(bf16[2,128,1024]{2,1,0:T(8,128)(2,1)} %get-tuple-element.121), channel_id=1, source_target_pairs={{0,1},{1,0},{2,3},{3,2},{4,5},{5,4},{6,7},{7,6},{8,9},{9,8},{10,11... | collective-permute-start | bytes 1572872 | tf_op jit(solution)/shard_map/ppermute | solution.py:578
